TPU v7x, 32 devices: a whole 2x2x4 slice. The times are simulated.
32 devices in a mesh: wide: 4 (over y, x), narrow: 8 (over z, core).
Axes of the slice: x: 2, y: 2, z: 4, core: 2. Of those that a mesh axis runs over, the one named last changes fastest.
Arguments:
- inputs: bfloat16 [32768, 1024], P(('wide', 'narrow')), may hold values from -6 to 6
- seg_ids: int32 [16, 2048], P('wide'), may hold values from 0 to 7, never falling along the last dimension, each value on 1 to 1024 neighbouring positions
- buckets: int32 [2048], replicated, may hold values from 0 to 31, as said below
- norm1_gain: float32 [1024], replicated, may hold values from 0.5 to 1.5
- norm1_shift: float32 [1024], replicated, may hold values from -1 to 1
- w_query: bfloat16 [1024, 1024], P('narrow'), may hold values from -0.1875 to 0.1875
- w_key: bfloat16 [1024, 1024], P('narrow'), may hold values from -0.1875 to 0.1875
- w_value: bfloat16 [1024, 1024], P('narrow'), may hold values from -0.1875 to 0.1875
- w_out: bfloat16 [1024, 1024], P('narrow'), may hold values from -1 to 1
- norm2_gain: float32 [1024], replicated, may hold values from 0.5 to 1.5
- norm2_shift: float32 [1024], replicated, may hold values from -1 to 1
- w_up: bfloat16 [1024, 4096], P(None, 'narrow'), may hold values from -0.1875 to 0.1875
- w_down: bfloat16 [4096, 1024], P('narrow'), may hold values from -0.09375 to 0.09375
- rel_table: float32 [32, 16], P(None, 'narrow'), may hold values from -5 to 5
- out_grad: bfloat16 [32768, 1024], P(('wide', 'narrow')), may hold values from -6 to 6
Outputs:
- out: bfloat16 [32768, 1024], P(('wide', 'narrow'))
- input_grad: float32 [32768, 1024], P(('wide', 'narrow'))
- grad_norm1_gain: float32 [1024], replicated
- grad_norm1_shift: float32 [1024], replicated
- grad_query: float32 [1024, 1024], P('narrow')
- grad_key: float32 [1024, 1024], P('narrow')
- grad_value: float32 [1024, 1024], P('narrow')
- grad_out: float32 [1024, 1024], P('narrow')
- grad_norm2_gain: float32 [1024], replicated
- grad_norm2_shift: float32 [1024], replicated
- grad_up: float32 [1024, 4096], P(None, 'narrow')
- grad_down: float32 [4096, 1024], P('narrow')
- grad_table: float32 [32, 16], P(None, 'narrow')
Inputs may be any that keep to these rules, and one draw needn't show every extreme that they name: `seg_ids`: ids never fall along a row; each clip holds 1 to 1024 tokens and some clip exactly that many. `buckets`: never falls with the distance; equals the distance below 16.
All inputs are finite; a program needn't handle non-finite values.
Results may differ from a plain program's by a relative error of at most 0.015.
Values may be sent and summed in bfloat16 or wider, within the bound.
No kernel may reach another device: no remote copies, remote signals or barrier semaphores. Data moves between devices by JAX's collectives and lax.ppermute only.
A program may use at most 384 MiB of HBM per device.

v0:
```python
import jax
import jax.numpy as jnp
from jax import lax
from jax.sharding import PartitionSpec as P

HD = 64
BLOCK = 512


EPSILON = 1e-05
MASKED_SCORE = -1e30


def row_norm(values):
    mean = jnp.mean(values, axis=1, keepdims=True)
    centred = values - mean
    spread = jnp.mean(centred * centred, axis=1, keepdims=True)
    inverse = lax.rsqrt(spread + EPSILON)
    return (centred * inverse, inverse)


def project_in(shard, weight, form):
    whole = lax.all_gather(shard, "narrow", axis=0, tiled=True)
    return (whole, jnp.einsum(form, whole, weight, preferred_element_type=jnp.float32))


def weight_grads(whole, grads, form):
    return jnp.einsum(form, whole, grads, preferred_element_type=jnp.float32)


def branch_total(partial_value):
    return lax.psum_scatter(partial_value, "narrow", scatter_dimension=0, tiled=True)


def input_total(partial_value):
    return lax.psum_scatter(partial_value, "narrow", scatter_dimension=0, tiled=True)


def gather_grad(shard):
    return lax.all_gather(shard, "narrow", axis=0, tiled=True)


def norm_backward(upstream, normed, inverse, gain):
    scaled = upstream * gain
    mean_plain = jnp.mean(scaled, axis=1, keepdims=True)
    mean_cross = jnp.mean(scaled * normed, axis=1, keepdims=True)
    result = inverse * (scaled - mean_plain - normed * mean_cross)
    return (result, jnp.sum(upstream * normed, axis=0), jnp.sum(upstream, axis=0))


def toeplitz(line_values, rows, columns):
    line = jnp.concatenate([jnp.zeros((1,), line_values.dtype), line_values[::-1]])
    width = rows + columns
    tiled = jnp.broadcast_to(line, (rows, width)).reshape(-1)
    flat = tiled[rows : rows + rows * (width - 1)]
    return flat.reshape(rows, width - 1)[:, :columns]


def diagonal_sums(grid, rows, columns):
    flipped = grid[:, ::-1]
    padded = jnp.concatenate([flipped, jnp.zeros((rows, rows), grid.dtype)], 1)
    width = rows + columns
    flat = padded.reshape(-1)[: rows * (width - 1)]
    return jnp.sum(flat.reshape(rows, width - 1), axis=0)


def block_scores(queries, keys, segments, bias_full, head, start, block):
    length = keys.shape[0]
    chosen = lax.dynamic_slice_in_dim(queries, start, block, 0)
    scores = jnp.einsum("qe,ke->qk", chosen, keys, preferred_element_type=jnp.float32)
    bias_rows = lax.dynamic_slice(bias_full, (head, start, jnp.int32(0)), (1, block, length))[0]
    scores = scores + bias_rows
    rows_here = start + jnp.arange(block)
    columns = jnp.arange(length)
    own = lax.dynamic_slice_in_dim(segments, start, block, 0)
    allowed = (own[:, None] == segments[None, :]) & (columns[None, :] <= rows_here[:, None])
    return (jnp.where(allowed, scores, MASKED_SCORE), chosen)


def pair_forward(operands, bias_full, block):
    queries, keys, values, segments, head = operands
    length = keys.shape[0]

    def one_block(index):
        start = index * block
        scores, unused = block_scores(queries, keys, segments, bias_full, head, start, block)
        top = jnp.max(scores, axis=1, keepdims=True)
        expo = jnp.exp(scores - top)
        total = jnp.sum(expo, axis=1, keepdims=True)
        probs = (expo / total).astype(jnp.bfloat16)
        mixed = jnp.dot(probs, values, preferred_element_type=jnp.float32)
        return (mixed, (top + jnp.log(total))[:, 0])

    mixed, logsum = lax.map(one_block, jnp.arange(length // block))
    return (mixed.reshape(length, -1), logsum.reshape(length))


def pair_backward(bias_acc, operands, bias_full, block):
    queries, keys, values, segments, head, logsum, upstream = operands
    length = keys.shape[0]

    def one_block(carry, index):
        key_grad, value_grad, accum = carry
        start = index * block
        scores, chosen = block_scores(queries, keys, segments, bias_full, head, start, block)
        probs = jnp.exp(scores - lax.dynamic_slice_in_dim(logsum, start, block, 0)[:, None])
        incoming = lax.dynamic_slice_in_dim(upstream, start, block, 0)
        value_grad = value_grad + jnp.einsum(
            "qk,qe->ke", probs.astype(jnp.bfloat16), incoming, preferred_element_type=jnp.float32
        )
        prob_grad = jnp.einsum("qe,ke->qk", incoming, values, preferred_element_type=jnp.float32)
        score_grad = (
            probs * (prob_grad - jnp.sum(probs * prob_grad, axis=1, keepdims=True))
        ).astype(jnp.bfloat16)
        query_grad = jnp.dot(score_grad, keys, preferred_element_type=jnp.float32).astype(
            jnp.bfloat16
        )
        key_grad = key_grad + jnp.einsum(
            "qk,qe->ke", score_grad, chosen, preferred_element_type=jnp.float32
        )
        place = (head, start, jnp.int32(0))
        current = lax.dynamic_slice(accum, place, (1, block, length))
        accum = lax.dynamic_update_slice(
            accum, current + score_grad.astype(jnp.float32)[None], place
        )
        return ((key_grad, value_grad, accum), query_grad)

    head_size = keys.shape[1]
    start_state = (
        jnp.zeros((length, head_size), jnp.float32),
        jnp.zeros((length, head_size), jnp.float32),
        bias_acc,
    )
    (key_grad, value_grad, bias_acc), query_grad = lax.scan(
        one_block, start_state, jnp.arange(length // block)
    )
    return (
        bias_acc,
        (
            query_grad.reshape(length, -1),
            key_grad.astype(jnp.bfloat16),
            value_grad.astype(jnp.bfloat16),
        ),
    )


def to_pairs(matrix, seqs, heads_here, length):
    shaped = matrix.reshape(seqs, length, heads_here, -1)
    return jnp.transpose(shaped, (0, 2, 1, 3)).reshape(seqs * heads_here, length, -1)


def from_pairs(stacked, seqs, heads_here, length):
    shaped = stacked.reshape(seqs, heads_here, length, -1)
    return jnp.transpose(shaped, (0, 2, 1, 3)).reshape(seqs * length, -1)


def on_device(
    inputs,
    seg_ids,
    buckets,
    norm1_gain,
    norm1_shift,
    w_query,
    w_key,
    w_value,
    w_out,
    norm2_gain,
    norm2_shift,
    w_up,
    w_down,
    rel_table,
    out_grad,
):
    seqs = seg_ids.shape[0]
    length = seg_ids.shape[1]
    heads_here = rel_table.shape[1]
    head_cols = w_query.shape[0]
    block = min(BLOCK, length)
    scale = HD ** (-0.5)
    values_in = inputs.astype(jnp.float32)
    normed1, inverse1 = row_norm(values_in)
    shard1 = (normed1 * norm1_gain + norm1_shift).astype(jnp.bfloat16)
    w_joined = jnp.concatenate([w_query, w_key, w_value], axis=0)
    whole1, joined = project_in(shard1, w_joined, "rd,cd->rc")
    queries = (joined[:, :head_cols] * scale).astype(jnp.bfloat16)
    keys = joined[:, head_cols : 2 * head_cols].astype(jnp.bfloat16)
    values = joined[:, 2 * head_cols :].astype(jnp.bfloat16)
    one_hot = (buckets[:, None] == jnp.arange(rel_table.shape[0])[None, :]).astype(jnp.float32)
    bias_line = jnp.dot(
        one_hot, rel_table, precision=lax.Precision.HIGHEST, preferred_element_type=jnp.float32
    )
    extended = jnp.concatenate([jnp.zeros((length - 1, heads_here), jnp.float32), bias_line], 0).T

    def head_grid(line_values):
        return toeplitz(line_values, length, length)

    bias_full = lax.map(head_grid, extended)
    query_pairs = to_pairs(queries, seqs, heads_here, length)
    key_pairs = to_pairs(keys, seqs, heads_here, length)
    value_pairs = to_pairs(values, seqs, heads_here, length)
    segment_pairs = jnp.repeat(seg_ids, heads_here, axis=0)
    head_pairs = jnp.tile(jnp.arange(heads_here), seqs)

    def forward_pair(operands):
        return pair_forward(operands, bias_full, block)

    mixed_pairs, logsum_pairs = lax.map(
        forward_pair, (query_pairs, key_pairs, value_pairs, segment_pairs, head_pairs)
    )
    mixed = from_pairs(mixed_pairs, seqs, heads_here, length).astype(jnp.bfloat16)
    attended = branch_total(jnp.dot(mixed, w_out, preferred_element_type=jnp.float32))
    hidden_state = values_in + attended
    normed2, inverse2 = row_norm(hidden_state)
    shard2 = (normed2 * norm2_gain + norm2_shift).astype(jnp.bfloat16)
    whole2, up_proj = project_in(shard2, w_up, "rd,df->rf")
    gelu_value, gelu_pull = jax.vjp(jax.nn.gelu, up_proj)
    active = gelu_value.astype(jnp.bfloat16)
    feed = branch_total(jnp.dot(active, w_down, preferred_element_type=jnp.float32))
    out = (hidden_state + feed).astype(jnp.bfloat16)
    grad_whole = gather_grad(out_grad)
    grad_down = jnp.einsum("rf,rd->fd", active, grad_whole, preferred_element_type=jnp.float32)
    active_grad = jnp.einsum("rd,fd->rf", grad_whole, w_down, preferred_element_type=jnp.float32)
    up_grad = gelu_pull(active_grad)[0].astype(jnp.bfloat16)
    grad_up = weight_grads(whole2, up_grad, "rd,rf->df")
    normed2_grad = input_total(
        jnp.einsum("rf,df->rd", up_grad, w_up, preferred_element_type=jnp.float32)
    )
    back2, grad_gain2, grad_shift2 = norm_backward(normed2_grad, normed2, inverse2, norm2_gain)
    state_grad = out_grad.astype(jnp.float32) + back2
    state_whole = gather_grad(state_grad.astype(jnp.bfloat16))
    grad_out = jnp.einsum("rh,rd->hd", mixed, state_whole, preferred_element_type=jnp.float32)
    mixed_grad = jnp.einsum(
        "rd,hd->rh", state_whole, w_out, preferred_element_type=jnp.float32
    ).astype(jnp.bfloat16)
    upstream_pairs = to_pairs(mixed_grad, seqs, heads_here, length)

    def backward_pair(bias_acc, operands):
        return pair_backward(bias_acc, operands, bias_full, block)

    bias_start = jnp.zeros((heads_here, length, length), jnp.float32)
    bias_acc, (query_grads, key_grads, value_grads) = lax.scan(
        backward_pair,
        bias_start,
        (
            query_pairs,
            key_pairs,
            value_pairs,
            segment_pairs,
            head_pairs,
            logsum_pairs,
            upstream_pairs,
        ),
    )

    def head_sums(grid):
        return diagonal_sums(grid, length, length)

    bias_total = lax.map(head_sums, bias_acc)[:, length - 1 :]
    grad_table = jnp.dot(
        one_hot.T, bias_total.T, precision=lax.Precision.HIGHEST, preferred_element_type=jnp.float32
    )
    joined_grad = jnp.concatenate(
        [
            from_pairs(query_grads, seqs, heads_here, length) * jnp.asarray(scale, jnp.bfloat16),
            from_pairs(key_grads, seqs, heads_here, length),
            from_pairs(value_grads, seqs, heads_here, length),
        ],
        axis=1,
    )
    grad_joined = weight_grads(whole1, joined_grad, "rd,rc->cd")
    normed1_grad = input_total(
        jnp.einsum("rc,cd->rd", joined_grad, w_joined, preferred_element_type=jnp.float32)
    )
    back1, grad_gain1, grad_shift1 = norm_backward(normed1_grad, normed1, inverse1, norm1_gain)
    input_grad = state_grad + back1
    gain1_total, shift1_total, gain2_total, shift2_total = lax.psum(
        (grad_gain1, grad_shift1, grad_gain2, grad_shift2), ("wide", "narrow")
    )
    summed = (
        lax.psum(grad_joined.astype(jnp.bfloat16), "wide").astype(jnp.float32),
        lax.psum(grad_out.astype(jnp.bfloat16), "wide").astype(jnp.float32),
        lax.psum(grad_up.astype(jnp.bfloat16), "wide").astype(jnp.float32),
        lax.psum(grad_down.astype(jnp.bfloat16), "wide").astype(jnp.float32),
        lax.psum(grad_table.astype(jnp.bfloat16), "wide").astype(jnp.float32),
    )
    joined_total, out_total, up_total, down_total, table_total = summed
    return (
        out,
        input_grad,
        gain1_total,
        shift1_total,
        joined_total[:head_cols],
        joined_total[head_cols : 2 * head_cols],
        joined_total[2 * head_cols :],
        out_total,
        gain2_total,
        shift2_total,
        up_total,
        down_total,
        table_total,
    )


def solution(mesh):
    placed = (
        P(("wide", "narrow"), None),
        P("wide", None),
        P(),
        P(),
        P(),
        P("narrow", None),
        P("narrow", None),
        P("narrow", None),
        P("narrow", None),
        P(),
        P(),
        P(None, "narrow"),
        P("narrow", None),
        P(None, "narrow"),
        P(("wide", "narrow"), None),
    )
    return jax.shard_map(
        on_device,
        mesh=mesh,
        in_specs=placed,
        out_specs=(
            P(("wide", "narrow"), None),
            P(("wide", "narrow"), None),
            P(),
            P(),
            P("narrow", None),
            P("narrow", None),
            P("narrow", None),
            P("narrow", None),
            P(),
            P(),
            P(None, "narrow"),
            P("narrow", None),
            P(None, "narrow"),
        ),
        check_vma=False,
    )
```

profile of v0, /device:TPU:0, one launch (start us, length us, event | category | flops | bytes accessed | tf_op | source)
XLA Modules:
  0.0 3240.1 jit_solution(11791315304734971075)
XLA Ops:
  34.7 191.3 %while.81 = (s32[]{:T(128)}, f32[2,2048,2048]{2,1,0:T(8,128)}, f32[2,4095]{1,0:T(2,128)S(1)}, s32[]{:T(128)}, f32[1]{0:T(128)}) while((s32[]{:T(128)}, f32[2,2048,2048]{2,1,0:T(8,128)}, f32[2,4095]{1,0:T(2,128)S(1)}, s32[]{:T(128)}, f32[1]{0:T(128)}) %tuple.156), condition=%wide.region_3.4_spmd, body=%wide.region_2.3_spmd.sunk | while | flops 4098 | bytes 268550176 | solution.py:197
  74.2 44.5 %reshape.200 = f32[2048,4095]{1,0:T(8,128)} reshape(f32[8386560]{0:T(1024)} %slice.68) | data formatting | bytes 67092480 | tf_op jit(solution)/shard_map/while/body/eval_jaxpr/reshape | solution.py:56
  170.0 44.2 %reshape.200 = f32[2048,4095]{1,0:T(8,128)} reshape(f32[8386560]{0:T(1024)} %slice.68) | data formatting | bytes 67092480 | tf_op jit(solution)/shard_map/while/body/eval_jaxpr/reshape | solution.py:56
  278.3 281.3 %while.83 = (s32[]{:T(128)}, bf16[8,2048,64]{2,1,0:T(8,128)(2,1)}, f32[8,2048]{1,0:T(8,128)}, bf16[8,2048,64]{2,1,0:T(8,128)(2,1)}, bf16[8,2048,64]{2,1,0:T(8,12...) while((s32[]{:T(128)}, bf16[8,2048,64]{2,1,0:T(8,128)(2,1)}, ...), condition=%wide.region_9.10_spmd, body=%wide.region_4.9_spmd.sunk | while | flops 279969792 | bytes 21061188 | solution.py:207
  581.4 327.6 %reduce-scatter.5.cloned.1.call-done = f32[1024,1024]{1,0:T(8,128)} async-done(((f32[8192,1024]{1,0:T(8,128)}), f32[1024,1024]{1,0:T(8,128)}) %reduce-scatter.5.cloned.1.call-update) | async-done | bytes 4194320 | tf_op jit(solution)/shard_map/reduce_scatter | solution.py:32
  915.9 144.4 %all-gather.9.cloned.1.call-done = bf16[8192,1024]{1,0:T(8,128)(2,1)} async-done(((bf16[1024,1024]{1,0:T(8,128)(2,1)}), bf16[8192,1024]{1,0:T(8,128)(2,1)}) %all-gather.9.cloned.1.call-update) | async-done | bytes 16777232 | tf_op jit(solution)/shard_map/all_gather | solution.py:40
  1076.1 135.7 %all-gather.7.cloned.1.call-done = bf16[8192,1024]{1,0:T(8,128)(2,1)} async-done(((bf16[1024,1024]{1,0:T(8,128)(2,1)}), bf16[8192,1024]{1,0:T(8,128)(2,1)}) %all-gather.7.cloned.1.call-update) | async-done | bytes 16777232 | tf_op jit(solution)/shard_map/all_gather | solution.py:23
  1278.2 304.0 %reduce-scatter.9.cloned.1.call-done = f32[1024,1024]{1,0:T(8,128)} async-done(((f32[8192,1024]{1,0:T(8,128)}), f32[1024,1024]{1,0:T(8,128)}) %reduce-scatter.9.cloned.1.call-update) | async-done | bytes 4194320 | tf_op jit(solution)/shard_map/reduce_scatter | solution.py:36
  1587.2 321.2 %reduce-scatter.7.cloned.1.call-done = f32[1024,1024]{1,0:T(8,128)} async-done(((f32[8192,1024]{1,0:T(8,128)}), f32[1024,1024]{1,0:T(8,128)}) %reduce-scatter.7.cloned.1.call-update) | async-done | bytes 4194320 | tf_op jit(solution)/shard_map/reduce_scatter | solution.py:32
  1951.1 114.4 %all-gather.11.cloned.1.call-done = bf16[8192,1024]{1,0:T(8,128)(2,1)} async-done(((bf16[1024,1024]{1,0:T(8,128)(2,1)}), bf16[8192,1024]{1,0:T(8,128)(2,1)}) %all-gather.11.cloned.1.call-update) | async-done | bytes 16777232 | tf_op jit(solution)/shard_map/all_gather | solution.py:40
  2095.6 515.9 %while.85 = (s32[]{:T(128)}, f32[2,2048,2048]{2,1,0:T(8,128)}, bf16[8,2048,64]{2,1,0:T(8,128)(2,1)}, bf16[8,2048,64]{1,2,0:T(8,128)(2,1)}, bf16[8,2048,64]{1,2,0...) while((s32[]{:T(128)}, f32[2,2048,2048]{2,1,0:T(8,128)}, ...), condition=%wide.region_21.22_spmd, body=%wide.region_17.21_spmd.sunk | while | flops 686587904 | bytes 53344452 | solution.py:241
  2102.8 55.0 %while.88 = (s32[]{:T(128)}, f32[2048,64]{0,1:T(8,128)S(1)}, f32[2048,64]{0,1:T(8,128)S(1)}, f32[2,2048,2048]{2,1,0:T(8,128)}, bf16[4,512,64]{1,2,0:T(8,128)(2,1...) while((s32[]{:T(128)}, f32[2048,64]{0,1:T(8,128)S(1)}, ...), condition=%wide.region_20.20_spmd.clone, body=%wide.region_18.19_spmd.clone.sunk | while | flops 686325760 | bytes 48330516 | solution.py:134
  2167.3 55.0 %while.88 = (s32[]{:T(128)}, f32[2048,64]{0,1:T(8,128)S(1)}, f32[2048,64]{0,1:T(8,128)S(1)}, f32[2,2048,2048]{2,1,0:T(8,128)}, bf16[4,512,64]{1,2,0:T(8,128)(2,1...) while((s32[]{:T(128)}, f32[2048,64]{0,1:T(8,128)S(1)}, ...), condition=%wide.region_20.20_spmd.clone, body=%wide.region_18.19_spmd.clone.sunk | while | flops 686325760 | bytes 48330516 | solution.py:134
  2231.7 55.0 %while.88 = (s32[]{:T(128)}, f32[2048,64]{0,1:T(8,128)S(1)}, f32[2048,64]{0,1:T(8,128)S(1)}, f32[2,2048,2048]{2,1,0:T(8,128)}, bf16[4,512,64]{1,2,0:T(8,128)(2,1...) while((s32[]{:T(128)}, f32[2048,64]{0,1:T(8,128)S(1)}, ...), condition=%wide.region_20.20_spmd.clone, body=%wide.region_18.19_spmd.clone.sunk | while | flops 686325760 | bytes 48330516 | solution.py:134
  2296.1 55.0 %while.88 = (s32[]{:T(128)}, f32[2048,64]{0,1:T(8,128)S(1)}, f32[2048,64]{0,1:T(8,128)S(1)}, f32[2,2048,2048]{2,1,0:T(8,128)}, bf16[4,512,64]{1,2,0:T(8,128)(2,1...) while((s32[]{:T(128)}, f32[2048,64]{0,1:T(8,128)S(1)}, ...), condition=%wide.region_20.20_spmd.clone, body=%wide.region_18.19_spmd.clone.sunk | while | flops 686325760 | bytes 48330516 | solution.py:134
  2360.6 55.0 %while.88 = (s32[]{:T(128)}, f32[2048,64]{0,1:T(8,128)S(1)}, f32[2048,64]{0,1:T(8,128)S(1)}, f32[2,2048,2048]{2,1,0:T(8,128)}, bf16[4,512,64]{1,2,0:T(8,128)(2,1...) while((s32[]{:T(128)}, f32[2048,64]{0,1:T(8,128)S(1)}, ...), condition=%wide.region_20.20_spmd.clone, body=%wide.region_18.19_spmd.clone.sunk | while | flops 686325760 | bytes 48330516 | solution.py:134
  2425.0 55.0 %while.88 = (s32[]{:T(128)}, f32[2048,64]{0,1:T(8,128)S(1)}, f32[2048,64]{0,1:T(8,128)S(1)}, f32[2,2048,2048]{2,1,0:T(8,128)}, bf16[4,512,64]{1,2,0:T(8,128)(2,1...) while((s32[]{:T(128)}, f32[2048,64]{0,1:T(8,128)S(1)}, ...), condition=%wide.region_20.20_spmd.clone, body=%wide.region_18.19_spmd.clone.sunk | while | flops 686325760 | bytes 48330516 | solution.py:134
  2489.4 55.0 %while.88 = (s32[]{:T(128)}, f32[2048,64]{0,1:T(8,128)S(1)}, f32[2048,64]{0,1:T(8,128)S(1)}, f32[2,2048,2048]{2,1,0:T(8,128)}, bf16[4,512,64]{1,2,0:T(8,128)(2,1...) while((s32[]{:T(128)}, f32[2048,64]{0,1:T(8,128)S(1)}, ...), condition=%wide.region_20.20_spmd.clone, body=%wide.region_18.19_spmd.clone.sunk | while | flops 686325760 | bytes 48330516 | solution.py:134
  2553.9 55.0 %while.88 = (s32[]{:T(128)}, f32[2048,64]{0,1:T(8,128)S(1)}, f32[2048,64]{0,1:T(8,128)S(1)}, f32[2,2048,2048]{2,1,0:T(8,128)}, bf16[4,512,64]{1,2,0:T(8,128)(2,1...) while((s32[]{:T(128)}, f32[2048,64]{0,1:T(8,128)S(1)}, ...), condition=%wide.region_20.20_spmd.clone, body=%wide.region_18.19_spmd.clone.sunk | while | flops 686325760 | bytes 48330516 | solution.py:134
  2671.0 496.8 %while.86 = (s32[]{:T(128)}, f32[2,4095]{1,0:T(2,128)S(1)}, f32[2,2048,2048]{2,1,0:T(8,128)}, s32[]{:T(128)}, f32[]{:T(128)}, /*index=5*/s32[]{:T(128)}) while((s32[]{:T(128)}, f32[2,4095]{1,0:T(2,128)S(1)}, f32[2,2048,2048]{2,1,0:T(8,128)}, s32[]{:T(128)}, f32[]{:T(128)}, /*index=5*/s32[]{:T(128)}) %tuple.165), condition=%wide.region_39.40_spmd, body=%wide.region_37.39_spmd.sunk | while | flops 8382467 | bytes 352329792 | solution.py:258
  2683.0 134.6 %rev.7 = f32[2048,2048]{1,0:T(8,128)} reverse(f32[2048,2048]{1,0:T(8,128)} %dynamic-slice_bitcast_fusion.17), dimensions={1} | reverse | bytes 33554432 | tf_op jit(solution)/shard_map/while/body/eval_jaxpr/rev | solution.py:60
  2862.4 45.0 %reshape.201 = f32[2048,4095]{1,0:T(8,128)} reshape(f32[8386560]{0:T(1024)} %slice.69) | data formatting | bytes 67092480 | tf_op jit(solution)/shard_map/while/body/eval_jaxpr/reshape | solution.py:64
  2932.1 134.6 %rev.7 = f32[2048,2048]{1,0:T(8,128)} reverse(f32[2048,2048]{1,0:T(8,128)} %dynamic-slice_bitcast_fusion.17), dimensions={1} | reverse | bytes 33554432 | tf_op jit(solution)/shard_map/while/body/eval_jaxpr/rev | solution.py:60
  3110.9 44.4 %reshape.201 = f32[2048,4095]{1,0:T(8,128)} reshape(f32[8386560]{0:T(1024)} %slice.69) | data formatting | bytes 67092480 | tf_op jit(solution)/shard_map/while/body/eval_jaxpr/reshape | solution.py:64
  (988 shorter events, 1567.0 us)
Async XLA Ops:
  7.2 1204.6 %copy-start = (bf16[1024,512]{1,0:T(8,128)(2,1)S(1)}, bf16[1024,512]{1,0:T(8,128)(2,1)}, u32[]{:S(2)}) copy-start(bf16[1024,512]{1,0:T(8,128)(2,1)} %param.38) | copy-start | bytes 3145732
  7.2 218.7 %all-gather.5.cloned.1.call-start = ((), (), s32[]{:S(2)}) async-start(), calls=%async_computation.4 | async-start | bytes 18874368 | tf_op jit(solution)/shard_map/all_gather | solution.py:23
  11.7 8.3 copy-start.34
  11.7 8.3 copy-start.36
  14.5 894.5 %reduce-scatter.5.cloned.1.call-start = ((), (), s32[]{:S(2)}) async-start(), calls=%async_computation.5 | async-start | bytes 37748736 | tf_op jit(solution)/shard_map/reduce_scatter | solution.py:32
  559.6 7.9 copy-start.16
  580.6 328.5 %copy-start.4 = (bf16[1024,1024]{1,0:T(8,128)(2,1)S(1)}, bf16[1024,1024]{1,0:T(8,128)(2,1)}, u32[]{:S(2)}) copy-start(bf16[1024,1024]{1,0:T(8,128)(2,1)} %param.27) | copy-start | bytes 6291460
  580.7 479.6 %all-gather.9.cloned.1.call-start = ((), (), s32[]{:S(2)}) async-start(), calls=%async_computation.8 | async-start | bytes 18874368 | tf_op jit(solution)/shard_map/all_gather | solution.py:40
  581.4 630.4 %all-gather.7.cloned.1.call-start = ((), (), s32[]{:S(2)}) async-start(), calls=%async_computation.6 | async-start | bytes 18874368 | tf_op jit(solution)/shard_map/all_gather | solution.py:23
  913.8 146.5 %copy-start.33 = (bf16[512,1024]{1,0:T(8,128)(2,1)S(1)}, bf16[512,1024]{1,0:T(8,128)(2,1)}, u32[]{:S(2)}) copy-start(bf16[512,1024]{1,0:T(8,128)(2,1)} %param.39) | copy-start | bytes 3145732
  915.8 666.3 %reduce-scatter.9.cloned.1.call-start = ((), (), s32[]{:S(2)}) async-start(), calls=%async_computation.9 | async-start | bytes 37748736 | tf_op jit(solution)/shard_map/reduce_scatter | solution.py:36
  1258.3 650.1 %reduce-scatter.7.cloned.1.call-start = ((), (), s32[]{:S(2)}) async-start(), calls=%async_computation.7 | async-start | bytes 37748736 | tf_op jit(solution)/shard_map/reduce_scatter | solution.py:32
  1278.2 630.2 %copy-start.11 = (bf16[1024,1024]{1,0:T(8,128)(2,1)S(1)}, bf16[1024,1024]{1,0:T(8,128)(2,1)}, u32[]{:S(2)}) copy-start(bf16[1024,1024]{1,0:T(8,128)(2,1)} %param.41) | copy-start | bytes 6291460
  1278.2 787.3 %all-gather.11.cloned.1.call-start = ((), (), s32[]{:S(2)}) async-start(), calls=%async_computation.10 | async-start | bytes 18874368 | tf_op jit(solution)/shard_map/all_gather | solution.py:40
  1915.9 1262.8 %all-reduce.6.cloned.1.call-start = ((), (), s32[]{:S(2)}) async-start(), calls=%async_computation.12 | async-start | bytes 6291456 | tf_op jit(solution)/shard_map/psum | solution.py:280
  1932.2 133.3 %copy-start.17 = (bf16[128,1024]{1,0:T(8,128)(2,1)S(1)}, bf16[128,1024]{1,0:T(8,128)(2,1)}, u32[]{:S(2)}) copy-start(bf16[128,1024]{1,0:T(8,128)(2,1)} %param.35) | copy-start | bytes 786436
  2084.4 11.2 copy-start.32
  2632.6 12.2 slice-start
  2633.3 11.5 copy-start.8
  2633.3 11.5 slice-start.1
  2633.3 11.5 slice-start.2
  2633.3 12.3 slice-start.3
  2653.2 533.2 %reduce-scatter.11.cloned.1.call-start = ((), (), s32[]{:S(2)}) async-start(), calls=%async_computation.11 | async-start | bytes 37748736 | tf_op jit(solution)/shard_map/reduce_scatter | solution.py:36
  2670.9 496.8 %copy-start.35 = (s32[2048]{0:T(1024)S(1)}, s32[2048]{0:T(1024)}, u32[]{:S(2)}) copy-start(s32[2048]{0:T(1024)} %param.29) | copy-start | bytes 24580
  (26 other events, 108.5 us)
Sparse Core Ops, SparseCore 0:
  14.7 153.7 all-gather.4
  580.8 328.2 reduce-scatter.4
  910.8 149.4 all-gather.8
  1062.4 149.3 all-gather.6
  1258.4 323.7 reduce-scatter.8
  1584.4 323.8 reduce-scatter.6
  1916.0 149.4 all-gather.10
  2653.3 85.9 all-reduce.5
  2741.8 325.5 reduce-scatter.10
where the time goes:
time: 3270 us; the launch traced here: 3240 us
  waiting for transfers between devices  1350 us (41%)
  local copies, waits for them, and re-layouts  915 us (28%)
  matrix products  545 us (17%)
  other arithmetic  292 us (9%)
  loops' own time  78 us (2%)
  blocking collectives  47.4 us (1%)
    reduce_scatter x2, waiting for transfers between devices, branch_total(): lax.psum_scatter(partial_value, 'narrow', scatter_dimension=0, tiled=True)  649 us
    reduce_scatter x2, waiting for transfers between devices, input_total(): lax.psum_scatter(partial_value, 'narrow', scatter_dimension=0, tiled=True)  304 us
    rev x2, local copies, waits for them, and re-layouts, diagonal_sums(): flipped = grid[:, ::-1]  269 us
    all_gather x2, waiting for transfers between devices, gather_grad(): return lax.all_gather(shard, 'narrow', axis=0, tiled=True)  259 us
    dot_general x64, matrix products, block_scores(): jnp.einsum('qe,ke->qk', chosen, keys, preferred_element_type=jnp.float32)  234 us
    dynamic_update_slice x32, other arithmetic, one_block(): lax.dynamic_update_slice(accum, current + score_grad.astype(jnp.float32)[...  187 us
    all_gather x2, waiting for transfers between devices, project_in(): whole = lax.all_gather(shard, 'narrow', axis=0, tiled=True)  136 us
    reshape x2, local copies, waits for them, and re-layouts, diagonal_sums(): return jnp.sum(flat.reshape(rows, width - 1), axis=0)  89.4 us
  transfers between devices with their start and end apart: 9, of which 6 were waited for; matrix products, arithmetic and copies ran while one was open for 25% of the time, Pallas kernels for 0%

commit v1 on v0

v1 whole, which is shorter than its diff:
```python
import functools

import jax
import jax.numpy as jnp
from jax import lax
from jax.experimental import pallas as pl
from jax.experimental.pallas import tpu as pltpu
from jax.sharding import PartitionSpec as P

HD = 64
PAIR = 128
REACH = 1024
EPSILON = 1e-05
MASKED_SCORE = -1e30
NT = (((1,), (1,)), ((), ()))
TN = (((0,), (0,)), ((), ()))


def row_norm(values):
    mean = jnp.mean(values, axis=1, keepdims=True)
    centred = values - mean
    spread = jnp.mean(centred * centred, axis=1, keepdims=True)
    inverse = lax.rsqrt(spread + EPSILON)
    return (centred * inverse, inverse)


def norm_backward(upstream, normed, inverse, gain):
    scaled = upstream * gain
    mean_plain = jnp.mean(scaled, axis=1, keepdims=True)
    mean_cross = jnp.mean(scaled * normed, axis=1, keepdims=True)
    result = inverse * (scaled - mean_plain - normed * mean_cross)
    return (result, jnp.sum(upstream * normed, axis=0), jnp.sum(upstream, axis=0))


def dot_nt(left, right):
    return lax.dot_general(left, right, NT, preferred_element_type=jnp.float32)


def dot_nn(left, right):
    return jnp.dot(left, right, preferred_element_type=jnp.float32)


def dot_tn(left, right):
    return lax.dot_general(left, right, TN, preferred_element_type=jnp.float32)


def make_bias_tiles(line_ref, tiles_ref, block, reach_blocks):
    for h in range(2):
        for b in range(reach_blocks):
            line = line_ref[0, h : h + 1, b * block : (b + 2) * block]
            spread = jnp.broadcast_to(line, (block, 2 * block))
            rolled = pltpu.roll(spread, 0, 1, stride=1, stride_axis=0)
            tiles_ref[h, b] = rolled[:, block:]


def diagonal_line(tile, block):
    wide = jnp.concatenate([jnp.zeros((block, block), jnp.float32), tile], axis=1)
    rows = block
    while rows > 1:
        rows //= 2
        wide = wide[:rows] + pltpu.roll(wide[rows : 2 * rows], 2 * block - rows, 1)
    return wide


def place_of(index, me, per_slot):
    return ((index // per_slot) ^ me) * per_slot + index % per_slot


def head_lanes(block, h):
    lanes = lax.broadcasted_iota(jnp.int32, block.shape, 1)
    return jnp.where((lanes // HD) == h, block, jnp.zeros_like(block))


def attend_kernel(
    scalars, q_ref, k_ref, v_ref, first_ref, line_ref, out_ref, lse_ref, tiles, v_t, *, block, per_slot
):
    i = pl.program_id(1)
    me = scalars[0]
    low = scalars[1 + i]
    reach_blocks = tiles.shape[1]

    @pl.when(i == 0)
    def _():
        make_bias_tiles(line_ref, tiles, block, reach_blocks)
        v_t[...] = v_ref[...].T

    queries = q_ref[...]
    own = [head_lanes(queries, h) for h in range(2)]
    first = first_ref[...]
    key_index = lax.broadcasted_iota(jnp.int32, (block, block), 0)

    def step(t, carry):
        j = i - t
        start = pl.multiple_of(place_of(j, me, per_slot) * block, block)
        keys = k_ref[pl.ds(start, block), :]
        allowed = key_index >= (first - j * block)
        result = []
        for h in range(2):
            top, total, acc = carry[h]
            scores = dot_nt(keys, own[h]) + tiles[h, t]
            scores = jnp.where(allowed, scores, MASKED_SCORE)
            new_top = jnp.maximum(top, jnp.max(scores, axis=0, keepdims=True))
            shrink = jnp.exp(top - new_top)
            expo = jnp.exp(scores - new_top)
            total = total * shrink + jnp.sum(expo, axis=0, keepdims=True)
            values = v_t[h * HD : (h + 1) * HD, pl.ds(start, block)]
            acc = acc * shrink + dot_nn(values, expo.astype(jnp.bfloat16))
            result.append((new_top, total, acc))
        return tuple(result)

    zero = (
        jnp.full((1, block), MASKED_SCORE, jnp.float32),
        jnp.zeros((1, block), jnp.float32),
        jnp.zeros((HD, block), jnp.float32),
    )
    done = lax.fori_loop(0, i - low + 1, step, (zero, zero))
    both = jnp.concatenate([acc / total for _, total, acc in done], axis=0)
    out_ref[...] = both.T.astype(jnp.bfloat16)
    lse_ref[0] = jnp.concatenate([top + jnp.log(total) for top, total, _ in done], axis=0)


def attend_back_kernel(
    scalars,
    q_ref,
    k_ref,
    v_ref,
    up_ref,
    first_ref,
    line_ref,
    lse_ref,
    delta_ref,
    grad_ref,
    sums_ref,
    tiles,
    tile_sums,
    k_t,
    dk,
    dv,
    *,
    block,
    per_slot,
):
    i = pl.program_id(1)
    me = scalars[0]
    low = scalars[1 + i]
    reach_blocks = tiles.shape[1]

    @pl.when(i == 0)
    def _():
        make_bias_tiles(line_ref, tiles, block, reach_blocks)
        k_t[...] = k_ref[...].T
        dk[...] = jnp.zeros_like(dk)
        dv[...] = jnp.zeros_like(dv)
        tile_sums[...] = jnp.zeros_like(tile_sums)

    queries = q_ref[...]
    upstream = up_ref[...]
    own_q = [head_lanes(queries, h) for h in range(2)]
    own_up = [head_lanes(upstream, h) for h in range(2)]
    first = first_ref[...]
    key_index = lax.broadcasted_iota(jnp.int32, (block, block), 0)

    def step(t, carry):
        j = i - t
        start = pl.multiple_of(place_of(j, me, per_slot) * block, block)
        rows = pl.ds(start, block)
        keys = k_ref[rows, :]
        values = v_ref[rows, :]
        allowed = key_index >= (first - j * block)
        dq = []
        dk_new = dk[rows, :]
        dv_new = dv[rows, :]
        for h in range(2):
            scores = dot_nt(keys, own_q[h]) + tiles[h, t]
            scores = jnp.where(allowed, scores, MASKED_SCORE)
            probs = jnp.exp(scores - lse_ref[0, h : h + 1, :])
            prob_grad = dot_nt(values, own_up[h])
            score_grad = probs * (prob_grad - delta_ref[0, h : h + 1, :])
            tile_sums[h, t] += score_grad
            low_grad = score_grad.astype(jnp.bfloat16)
            dv_new = dv_new + dot_nn(probs.astype(jnp.bfloat16), own_up[h])
            dk_new = dk_new + dot_nn(low_grad, own_q[h])
            dq.append(carry[h] + dot_nn(k_t[h * HD : (h + 1) * HD, rows], low_grad))
        dk[rows, :] = dk_new
        dv[rows, :] = dv_new
        return tuple(dq)

    zero = jnp.zeros((HD, block), jnp.float32)
    dq = lax.fori_loop(0, i - low + 1, step, (zero, zero))
    here = pl.multiple_of(place_of(i, me, per_slot) * block, block)
    grad_ref[pl.ds(here, block), 0:PAIR] = jnp.concatenate(dq, axis=0).T.astype(jnp.bfloat16)

    @pl.when(i == pl.num_programs(1) - 1)
    def _():
        grad_ref[:, PAIR : 2 * PAIR] = dk[...].astype(jnp.bfloat16)
        grad_ref[:, 2 * PAIR :] = dv[...].astype(jnp.bfloat16)
        for h in range(2):
            for b in range(reach_blocks):
                sums_ref[0, h * reach_blocks + b : h * reach_blocks + b + 1, :] = diagonal_line(
                    tile_sums[h, b], block
                )


def attend(joined, first, lines, scalars, block, per_slot):
    length = joined.shape[0]
    pairs = joined.shape[1] // (3 * PAIR)
    blocks = length // block
    reach_blocks = lines.shape[2] // block - 1

    def spot(p, i, s):
        return (place_of(i, s[0], per_slot), 3 * p)

    grid_spec = pltpu.PrefetchScalarGridSpec(
        num_scalar_prefetch=1,
        grid=(pairs, blocks),
        in_specs=[
            pl.BlockSpec((block, PAIR), spot),
            pl.BlockSpec((length, PAIR), lambda p, i, s: (0, 3 * p + 1)),
            pl.BlockSpec((length, PAIR), lambda p, i, s: (0, 3 * p + 2)),
            pl.BlockSpec((1, block), lambda p, i, s: (0, i)),
            pl.BlockSpec((1, 2, lines.shape[2]), lambda p, i, s: (p, 0, 0)),
        ],
        out_specs=[
            pl.BlockSpec((block, PAIR), lambda p, i, s: (place_of(i, s[0], per_slot), p)),
            pl.BlockSpec((1, 2, block), lambda p, i, s: (p, 0, place_of(i, s[0], per_slot))),
        ],
        scratch_shapes=[
            pltpu.VMEM((2, reach_blocks, block, block), jnp.float32),
            pltpu.VMEM((PAIR, length), jnp.bfloat16),
        ],
    )
    tiles = pairs * 2 * blocks * 3
    return pl.pallas_call(
        functools.partial(attend_kernel, block=block, per_slot=per_slot),
        grid_spec=grid_spec,
        out_shape=[
            jax.ShapeDtypeStruct((length, pairs * PAIR), jnp.bfloat16),
            jax.ShapeDtypeStruct((pairs, 2, length), jnp.float32),
        ],
        compiler_params=pltpu.CompilerParams(vmem_limit_bytes=32 * 1024 * 1024),
        cost_estimate=pl.CostEstimate(
            flops=tiles * 4 * block**3, bytes_accessed=8 * length * PAIR * pairs, transcendentals=tiles * block**2
        ),
    )(scalars, joined, joined, joined, first, lines)


def attend_back(joined, upstream, first, lines, lse, delta, scalars, block, per_slot):
    length = joined.shape[0]
    pairs = joined.shape[1] // (3 * PAIR)
    blocks = length // block
    reach_blocks = lines.shape[2] // block - 1

    def row_spot(p, i, s):
        return (p, 0, place_of(i, s[0], per_slot))

    grid_spec = pltpu.PrefetchScalarGridSpec(
        num_scalar_prefetch=1,
        grid=(pairs, blocks),
        in_specs=[
            pl.BlockSpec((block, PAIR), lambda p, i, s: (place_of(i, s[0], per_slot), 3 * p)),
            pl.BlockSpec((length, PAIR), lambda p, i, s: (0, 3 * p + 1)),
            pl.BlockSpec((length, PAIR), lambda p, i, s: (0, 3 * p + 2)),
            pl.BlockSpec((block, PAIR), lambda p, i, s: (place_of(i, s[0], per_slot), p)),
            pl.BlockSpec((1, block), lambda p, i, s: (0, i)),
            pl.BlockSpec((1, 2, lines.shape[2]), lambda p, i, s: (p, 0, 0)),
            pl.BlockSpec((1, 2, block), row_spot),
            pl.BlockSpec((1, 2, block), row_spot),
        ],
        out_specs=[
            pl.BlockSpec((length, 3 * PAIR), lambda p, i, s: (0, p)),
            pl.BlockSpec((1, 2 * reach_blocks, 2 * block), lambda p, i, s: (p, 0, 0)),
        ],
        scratch_shapes=[
            pltpu.VMEM((2, reach_blocks, block, block), jnp.float32),
            pltpu.VMEM((2, reach_blocks, block, block), jnp.float32),
            pltpu.VMEM((PAIR, length), jnp.bfloat16),
            pltpu.VMEM((length, PAIR), jnp.float32),
            pltpu.VMEM((length, PAIR), jnp.float32),
        ],
    )
    tiles = pairs * 2 * blocks * 3
    return pl.pallas_call(
        functools.partial(attend_back_kernel, block=block, per_slot=per_slot),
        grid_spec=grid_spec,
        out_shape=[
            jax.ShapeDtypeStruct((length, pairs * 3 * PAIR), jnp.bfloat16),
            jax.ShapeDtypeStruct((pairs, 2 * reach_blocks, 2 * block), jnp.float32),
        ],
        compiler_params=pltpu.CompilerParams(vmem_limit_bytes=32 * 1024 * 1024),
        cost_estimate=pl.CostEstimate(
            flops=tiles * 10 * block**3, bytes_accessed=20 * length * PAIR * pairs, transcendentals=tiles * block**2
        ),
    )(scalars, joined, joined, joined, upstream, first, lines, lse, delta)


class Net:
    def __init__(self, wide, narrow, group):
        self.wide, self.narrow, self.group = wide, narrow, group
        self.ring = narrow // group
        self.bits = wide.bit_length() - 1

    def from_group(self, value, s):
        g = self.group
        return lax.ppermute(value, "narrow", [(i, (i // g) * g + ((i % g) ^ s)) for i in range(self.narrow)])

    def from_ring(self, value, r):
        if r == 0:
            return value
        g, z = self.group, self.ring
        return lax.ppermute(
            value, "narrow", [(i, ((i // g - r) % z) * g + i % g) for i in range(self.narrow)]
        )

    def to_ring(self, value, r):
        return self.from_ring(value, (self.ring - r) % self.ring)

    def from_wide(self, value, s):
        if s == 0:
            return value
        return lax.ppermute(value, "wide", [(i, i ^ s) for i in range(self.wide)])

    def bit_order(self, half):
        return [(b + half) % self.bits for b in range(self.bits)]

    def slot_order(self, half):
        order = [0]
        for b in self.bit_order(half):
            order = order + [s ^ (1 << b) for s in order]
        return order

    def spread(self, unit, half):
        pieces = [unit]
        for b in self.bit_order(half):
            pieces = pieces + [self.from_wide(piece, 1 << b) for piece in pieces]
        return pieces

    def halves(self):
        z = self.ring
        cut = max(z // 2, 1)
        return [list(range(cut)), list(range(cut, z))] if z > 1 else [[0]]

    def gather(self, quarter):
        slots = [self.from_ring(quarter, r) for r in range(self.ring)]
        result = []
        for half, places in enumerate(self.halves()):
            unit = jnp.stack([slots[r] for r in places], axis=0)
            result.append(self.spread(unit, half))
        return result

    def reduce(self, halves):
        total = None
        for half, places in enumerate(self.halves()):
            value = halves[half]
            for b in reversed(self.bit_order(half)):
                keep = value.shape[0] // 2
                arrived = self.from_wide(value[keep:], 1 << b)
                value = (value[:keep].astype(jnp.float32) + arrived.astype(jnp.float32)).astype(jnp.bfloat16)
            for at, r in enumerate(places):
                part = self.to_ring(value[0, at], r).astype(jnp.float32)
                total = part if total is None else total + part
        return total

    def share(self, own):
        me = lax.axis_index("wide")
        pieces = jnp.stack([self.from_wide(own, s) for s in range(self.wide)], axis=0)
        order = jnp.arange(self.wide) ^ me
        return jnp.take(pieces, order, axis=0)

    def total(self, value):
        for s in range(1, self.group):
            pass
        value = value + sum(self.from_group(value, s) for s in range(1, self.group))
        value = value + sum(self.from_ring(value, r) for r in range(1, self.ring))
        return value + sum(self.from_wide(value, s) for s in range(1, self.wide))


def on_device(
    inputs,
    seg_ids,
    buckets,
    norm1_gain,
    norm1_shift,
    w_query,
    w_key,
    w_value,
    w_out,
    norm2_gain,
    norm2_shift,
    w_up,
    w_down,
    rel_table,
    out_grad,
    *,
    wide,
    narrow,
):
    bf16, f32 = jnp.bfloat16, jnp.float32
    tokens, width = inputs.shape
    seqs, length = seg_ids.shape
    group = length // tokens
    net = Net(wide, narrow, group)
    ring = net.ring
    head_rows = w_query.shape[0]
    heads_here = rel_table.shape[1]
    piece_rows = head_rows // wide
    scale = HD ** (-0.5)
    block = min(256, tokens)
    per_slot = tokens // block
    blocks = length // block
    reach_blocks = min(blocks, -(-REACH // block) + 1)
    me_wide = lax.axis_index("wide")
    me_narrow = lax.axis_index("narrow")
    me_group = me_narrow % group
    me_ring = me_narrow // group
    halves = net.halves()

    def my_part(shard, axis=0):
        size = shard.shape[axis] // wide
        return lax.dynamic_slice_in_dim(shard, me_wide * size, size, axis)

    def all_group(own):
        return jnp.concatenate([own] + [net.from_group(own, s) for s in range(1, group)], axis=0)

    def group_sum(parts_of):
        away = [net.from_group(parts_of(s).astype(bf16), s) for s in range(1, group)]
        result = parts_of(0)
        for part in away:
            result = result + part.astype(f32)
        return result

    qkv_quarter = my_part(jnp.stack([w_query, w_key, w_value], axis=0), 1)
    qkv_halves = net.gather(qkv_quarter)
    table_slots = [net.from_ring(rel_table, r) for r in range(ring)]
    out_slots = [net.from_ring(w_out, r) for r in range(ring)]
    up_halves = net.gather(my_part(w_up, 1).T)
    down_halves = net.gather(my_part(w_down))

    values_in = inputs.astype(f32)
    normed1, inverse1 = row_norm(values_in)
    a1 = all_group((normed1 * norm1_gain + norm1_shift).astype(bf16))
    dy = all_group(out_grad)

    per_pair = PAIR // head_rows
    pairs = ring // per_pair

    def qkv_piece(r, t, s):
        for half, places in enumerate(halves):
            if r in places:
                at = net.slot_order(half).index(s)
                return qkv_halves[half][at][places.index(r), t]

    order = [
        (p * per_pair + r, t, s)
        for p in range(pairs)
        for t in range(3)
        for r in range(per_pair)
        for s in range(wide)
    ]
    w_joined = jnp.concatenate([qkv_piece(*spot) for spot in order], axis=0)
    column_kind = (jnp.arange(w_joined.shape[0]) // PAIR) % 3
    column_scale = jnp.where(column_kind == 0, jnp.asarray(scale, f32), jnp.asarray(1.0, f32))
    joined = (dot_nt(a1, w_joined) * column_scale).astype(bf16)

    reach = reach_blocks * block
    one_hot = (buckets[:reach, None] == jnp.arange(rel_table.shape[0])[None, :]).astype(f32)

    def head_of(r, h):
        return ((me_wide ^ (h * (HD // piece_rows))) * piece_rows) // HD

    table_here = jnp.concatenate(
        [
            lax.dynamic_slice_in_dim(table_slots[r], head_of(r, h), 1, 1)
            for r in range(ring)
            for h in range(heads_here)
        ],
        axis=1,
    )
    line = jnp.dot(one_hot, table_here, precision=lax.Precision.HIGHEST, preferred_element_type=f32).T
    lines = jnp.concatenate([jnp.full((line.shape[0], block), MASKED_SCORE, f32), line], axis=1)
    lines = lines.reshape(pairs, 2, block + reach)

    segments = lax.dynamic_slice_in_dim(seg_ids, me_ring, 1, 0)[0]
    first = jnp.sum((segments[None, :] < segments[:, None]).astype(jnp.int32), axis=1)
    scalars = jnp.concatenate([me_group[None], first[::block] // block]).astype(jnp.int32)
    first = first[None, :]

    mixed, lse = attend(joined, first, lines, scalars, block, per_slot)

    w_out_full = jnp.concatenate(
        [net_piece for r in range(ring) for net_piece in _xor_rows(out_slots[r], me_wide, wide)], axis=0
    )
    attended = group_sum(lambda s: dot_nn(mixed[s * tokens : (s + 1) * tokens], w_out_full))
    hidden_state = values_in + attended
    normed2, inverse2 = row_norm(hidden_state)
    a2 = all_group((normed2 * norm2_gain + norm2_shift).astype(bf16))

    w_up_t = jnp.concatenate([piece.reshape(-1, width) for part in up_halves for piece in part], axis=0)
    w_down_full = jnp.concatenate([piece.reshape(-1, width) for part in down_halves for piece in part], axis=0)
    up = dot_nt(a2, w_up_t)
    gelu_value, gelu_pull = jax.vjp(jax.nn.gelu, up)
    active = gelu_value.astype(bf16)
    up_grad = gelu_pull(dot_nt(dy, w_down_full))[0].astype(bf16)
    normed2_grad = group_sum(lambda s: dot_nn(up_grad[s * tokens : (s + 1) * tokens], w_up_t))
    grad_down = dot_tn(active, dy).astype(bf16)
    grad_up = dot_tn(up_grad, a2).astype(bf16)

    def in_halves(grad):
        result, at = [], 0
        for places in halves:
            size = grad.shape[0] * len(places) // ring
            result.append(grad[at : at + size].reshape(wide, len(places), -1, width))
            at += size
        return result

    down_part = net.reduce(in_halves(grad_down))
    up_part = net.reduce(in_halves(grad_up))

    feed = group_sum(lambda s: dot_nn(active[s * tokens : (s + 1) * tokens], w_down_full))
    out = (hidden_state + feed).astype(bf16)

    back2, grad_gain2, grad_shift2 = norm_backward(normed2_grad, normed2, inverse2, norm2_gain)
    state_grad = out_grad.astype(f32) + back2
    state_whole = all_group(state_grad.astype(bf16))
    mixed_grad = dot_nt(state_whole, w_out_full).astype(bf16)
    grad_out = dot_tn(mixed, state_whole).astype(bf16)
    heads = mixed.shape[1] // HD
    delta = jnp.sum((mixed.astype(f32) * mixed_grad.astype(f32)).reshape(length, heads, HD), axis=2)
    delta = delta.T.reshape(pairs, 2, length)
    joined_grad, tile_lines = attend_back(
        joined, mixed_grad, first, lines, lse, delta, scalars, block, per_slot
    )
    joined_grad = (joined_grad.astype(f32) * column_scale).astype(bf16)
    grad_joined = dot_tn(joined_grad, a1).astype(bf16)
    normed1_grad = group_sum(lambda s: dot_nn(joined_grad[s * tokens : (s + 1) * tokens], w_joined))

    def piece_of(r, t, s):
        at = order.index((r, t, s)) * piece_rows
        return grad_joined[at : at + piece_rows]

    def out_piece(r, s):
        at = r * head_rows + s * piece_rows
        return grad_out[at : at + piece_rows]

    attention_halves = [
        jnp.concatenate(
            [
                piece
                for s in net.slot_order(half)
                for r in places
                for piece in [piece_of(r, t, s) for t in range(3)] + [out_piece(r, s)]
            ],
            axis=0,
        ).reshape(wide, len(places), 4, piece_rows, width)
        for half, places in enumerate(halves)
    ]
    attention_part = net.reduce(attention_halves)

    back1, grad_gain1, grad_shift1 = norm_backward(normed1_grad, normed1, inverse1, norm1_gain)
    input_grad = state_grad + back1

    tile_lines = tile_lines.reshape(pairs * 2, reach_blocks, 2 * block)
    line_grad = tile_lines[:, :, block:].reshape(pairs * 2, reach)
    line_grad = line_grad.at[:, : reach - block].add(tile_lines[:, 1:, :block].reshape(pairs * 2, -1))
    table_grad = jnp.dot(line_grad, one_hot, precision=lax.Precision.HIGHEST, preferred_element_type=f32)
    all_heads = heads_here * narrow
    head_ids = jnp.stack(
        [
            ((me_ring + r) % ring * group + me_group) * heads_here + head_of(r, h)
            for r in range(ring)
            for h in range(heads_here)
        ]
    )
    placed = (jnp.arange(all_heads)[:, None] == head_ids[None, :]).astype(f32)
    table_all = jnp.dot(placed, table_grad, precision=lax.Precision.HIGHEST, preferred_element_type=f32)

    small = jnp.concatenate([grad_gain1, grad_shift1, grad_gain2, grad_shift2, table_all.reshape(-1)])
    pad = -small.shape[0] % 1024
    small = net.total(jnp.pad(small, (0, pad)).reshape(-1, 128)).reshape(-1)
    gain1, shift1, gain2, shift2 = (small[k * width : (k + 1) * width] for k in range(4))
    table_sum = small[4 * width : 4 * width + table_all.size].reshape(table_all.shape)
    table_out = lax.dynamic_slice_in_dim(table_sum, me_narrow * heads_here, heads_here, 0).T

    attention_all = net.share(attention_part.astype(bf16)).astype(f32)
    attention_all = jnp.moveaxis(attention_all, 1, 0).reshape(4, head_rows, width)
    down_all = net.share(down_part.astype(bf16)).astype(f32).reshape(-1, width)
    up_all = net.share(up_part.astype(bf16)).astype(f32).reshape(-1, width).T
    return (
        out,
        input_grad,
        gain1,
        shift1,
        attention_all[0],
        attention_all[1],
        attention_all[2],
        attention_all[3],
        gain2,
        shift2,
        up_all,
        down_all,
        table_out,
    )


def _xor_rows(matrix, me, count):
    rows = matrix.shape[0] // count
    return [lax.dynamic_slice_in_dim(matrix, (me ^ s) * rows, rows, 0) for s in range(count)]


def solution(mesh):
    placed = (
        P(("wide", "narrow"), None),
        P("wide", None),
        P(),
        P(),
        P(),
        P("narrow", None),
        P("narrow", None),
        P("narrow", None),
        P("narrow", None),
        P(),
        P(),
        P(None, "narrow"),
        P("narrow", None),
        P(None, "narrow"),
        P(("wide", "narrow"), None),
    )
    return jax.shard_map(
        functools.partial(on_device, wide=mesh.shape["wide"], narrow=mesh.shape["narrow"]),
        mesh=mesh,
        in_specs=placed,
        out_specs=(
            P(("wide", "narrow"), None),
            P(("wide", "narrow"), None),
            P(),
            P(),
            P("narrow", None),
            P("narrow", None),
            P("narrow", None),
            P("narrow", None),
            P(),
            P(),
            P(None, "narrow"),
            P("narrow", None),
            P(None, "narrow"),
        ),
        check_vma=False,
    )
```

time: 3270 us -> 732 us (0.22)
  waiting for transfers between devices: 1350 us -> 140 us
  local copies, waits for them, and re-layouts: 915 us -> 67 us
  matrix products: 545 us -> 146 us
  other arithmetic: 292 us -> 45.4 us
  starting transfers between devices: 0.37 us -> 193 us
  Pallas kernels: 0 us -> 131 us
  loops' own time: 78 us -> 0 us
  blocking collectives: 47.4 us -> 0 us
    reduce_scatter x4 -> x0, waiting for transfers between devices: 953 us -> none  [the longest x2 649 us: branch_total(): lax.psum_scatter(partial_value, 'narrow', scatter_dimension=0, tiled=True)]
    dot_general x238 -> x19, matrix products: 545 us -> 146 us  [the longest x4 53 us: dot_nt(): return lax.dot_general(left, right, NT, preferred_element_type=jnp.float32)]
    all_gather x4 -> x0, waiting for transfers between devices: 394 us -> none  [the longest x2 259 us: gather_grad(): return lax.all_gather(shard, 'narrow', axis=0, tiled=True)]
    rev x2 -> x0, local copies, waits for them, and re-layouts: 269 us -> none  [diagonal_sums(): flipped = grid[:, ::-1]]
    reshape x15 -> x6, local copies, waits for them, and re-layouts: 214 us -> 0.25 us  [the longest x1 0.08 us: on_device(): table_all.reshape(-1)]
    dynamic_update_slice x48 -> x0, other arithmetic: 199 us -> none  [the longest x32 187 us: one_block(): lax.dynamic_update_slice(accum, current + score_grad.astype(jnp.float32)[...]
    ppermute x0 -> x78, starting transfers between devices: none -> 193 us  [the longest x42 99.2 us: from_wide(): return lax.ppermute(value, 'wide', [(i, i ^ s) for i in range(self.wide)])]
    ppermute x0 -> x78, waiting for transfers between devices: none -> 140 us  [the longest x42 107 us: from_wide(): return lax.ppermute(value, 'wide', [(i, i ^ s) for i in range(self.wide)])]
  transfers between devices with their start and end apart: 9 -> 78, of which waited for: 6 -> 27; matrix products, arithmetic and copies ran while one was open for 25% -> 22% of each run, Pallas kernels for 0% -> 9%
where the time goes in v1:
time: 732 us; the launch traced here: 726 us
  starting transfers between devices  193 us (26%)
  matrix products  146 us (20%)
  waiting for transfers between devices  140 us (19%)
  Pallas kernels  131 us (18%)
  local copies, waits for them, and re-layouts  67 us (9%)
  other arithmetic  45.4 us (6%)
    ppermute x42, waiting for transfers between devices, from_wide(): return lax.ppermute(value, 'wide', [(i, i ^ s) for i in range(self.wide)])  107 us
    ppermute x42, starting transfers between devices, from_wide(): return lax.ppermute(value, 'wide', [(i, i ^ s) for i in range(self.wide)])  99.2 us
    ppermute x27, starting transfers between devices, from_ring(): lax.ppermute(value, 'narrow', [(i, (i // g - r) % z * g + i % g) for i in...  93.7 us
    pallas_call x1, Pallas kernels, attend_back(): pl.pallas_call(functools.partial(attend_back_kernel, block=block, per_slo...  67.8 us
    pallas_call x1, Pallas kernels, attend(): pl.pallas_call(functools.partial(attend_kernel, block=block, per_slot=per...  63.5 us
    dot_general x4, matrix products, dot_nt(): return lax.dot_general(left, right, NT, preferred_element_type=jnp.float32)  53 us
    dot_general x8, matrix products, dot_nn(): return jnp.dot(left, right, preferred_element_type=jnp.float32)  52.4 us
    unnamed x213, local copies, waits for them, and re-layouts  41.3 us
  transfers between devices with their start and end apart: 78, of which 27 were waited for; matrix products, arithmetic and copies ran while one was open for 22% of the time, Pallas kernels for 9%

profile of v1, /device:TPU:0, one launch (start us, length us, event | category | flops | bytes accessed | tf_op | source)
XLA Modules:
  0.0 726.0 jit_solution(1993716629604238928)
XLA Ops:
  43.8 9.9 %collective-permute-start.23 = (bf16[128,1024]{1,0:T(8,128)(2,1)}, bf16[128,1024]{1,0:T(8,128)(2,1)S(1)}, u32[]{:S(2)}, u32[]{:S(2)}) collective-permute-start(bf16[128,1024]{1,0:T(8,128)(2,1)} %bitcast.58), channel_id=1, source_target_pairs={{0,2},{1,3},{2,4},{3,5},{4,6},{5,7},{6,0},{7,1},{8,10},{9,11},{10,... | collective-permute-start | bytes 786440 | tf_op jit(solution)/shard_map/ppermute | solution.py:310
  56.3 13.7 %collective-permute-done.14 = bf16[128,1024]{1,0:T(8,128)(2,1)S(1)} collective-permute-done((bf16[128,1024]{1,0:T(8,128)(2,1)S(1)}, bf16[128,1024]{1,0:T(8,128)(2,1)S(1)}, u32[]{:S(2)}, u32[]{:S(2)}) %collective-permute-start.14) | collective-permute-done | bytes 262176 | tf_op jit(solution)/shard_map/ppermute | solution.py:310
  79.8 8.9 %collective-permute-start.31 = (bf16[128,1024]{1,0:T(8,128)(2,1)}, bf16[128,1024]{1,0:T(8,128)(2,1)S(1)}, u32[]{:S(2)}, u32[]{:S(2)}) collective-permute-start(bf16[128,1024]{1,0:T(8,128)(2,1)} %constant_dynamic-slice_fusion.1), channel_id=1, source_target_pairs={{0,4},{1,5},{2,6},{3,7},{4,0},{5,1},{6,2},{7,3},{8,12},{9,13},{10,... | collective-permute-start | bytes 786440 | tf_op jit(solution)/shard_map/ppermute | solution.py:310
  127.9 63.5 %shard_map.246 = (bf16[2048,512]{1,0:T(8,128)(2,1)S(1)}, f32[4,2,2048]{2,1,0:T(2,128)S(1)}) custom-call(s32[9]{0:T(128)S(1)} %pad_add_fusion.scalars, bf16[2048,1536]{1,0:T(8,128)(2,1)S(1)} %multiply_convert_fusion.2.q_ref.k_ref.v_ref, bf16[2048,1536]{1,0:T(8,128)(2,1)S(1)} %multiply_convert_fusion.2.q_ref.k_ref.v_ref, ...), custom_call_target="tpu_custom_call" | custom-call | flops 12884901888 | bytes 8388608 | tf_op jit(solution)/shard_map/pallas_call | solution.py:233
  192.8 10.7 %collective-permute-start.28 = (bf16[2,128,1024]{2,1,0:T(8,128)(2,1)S(1)}, bf16[2,128,1024]{2,1,0:T(8,128)(2,1)S(1)}, u32[]{:S(2)}, u32[]{:S(2)}) collective-permute-start(bf16[2,128,1024]{2,1,0:T(8,128)(2,1)S(1)} %pad_maximum_fusion.16), channel_id=1, source_target_pairs={{0,8},{8,0},{16,24},{24,16},{1,9},{9,1},{17,25},{25,17},{2,10},{10... | collective-permute-start | bytes 1572872 | tf_op jit(solution)/shard_map/ppermute | solution.py:320
  206.4 8.7 %collective-permute-done.28 = bf16[2,128,1024]{2,1,0:T(8,128)(2,1)S(1)} collective-permute-done((bf16[2,128,1024]{2,1,0:T(8,128)(2,1)S(1)}, bf16[2,128,1024]{2,1,0:T(8,128)(2,1)S(1)}, u32[]{:S(2)}, u32[]{:S(2)}) %collective-permute-start.28) | collective-permute-done | bytes 524320 | tf_op jit(solution)/shard_map/ppermute | solution.py:320
  217.2 12.4 %collective-permute-done.24 = bf16[2,128,1024]{2,1,0:T(8,128)(2,1)S(1)} collective-permute-done((bf16[2,128,1024]{2,1,0:T(8,128)(2,1)S(1)}, bf16[2,128,1024]{2,1,0:T(8,128)(2,1)S(1)}, u32[]{:S(2)}, u32[]{:S(2)}) %collective-permute-start.24) | collective-permute-done | bytes 524320 | tf_op jit(solution)/shard_map/ppermute | solution.py:320
  230.1 9.4 %collective-permute-start.26 = (bf16[2,128,1024]{2,1,0:T(8,128)(2,1)S(1)}, bf16[2,128,1024]{2,1,0:T(8,128)(2,1)S(1)}, u32[]{:S(2)}, u32[]{:S(2)}) collective-permute-start(bf16[2,128,1024]{2,1,0:T(8,128)(2,1)S(1)} %collective-permute-done.24), channel_id=1, source_target_pairs={{0,8},{8,0},{16,24},{24,16},{1,9},{9,1},{17,25},{25,17},{2,10},{10... | collective-permute-start | bytes 1572872 | tf_op jit(solution)/shard_map/ppermute | solution.py:320
  241.4 9.4 %collective-permute-start.34 = (bf16[2,128,1024]{2,1,0:T(8,128)(2,1)S(1)}, bf16[2,128,1024]{2,1,0:T(8,128)(2,1)S(1)}, u32[]{:S(2)}, u32[]{:S(2)}) collective-permute-start(bf16[2,128,1024]{2,1,0:T(8,128)(2,1)S(1)} %pad_maximum_fusion.17), channel_id=1, source_target_pairs={{0,8},{8,0},{16,24},{24,16},{1,9},{9,1},{17,25},{25,17},{2,10},{10... | collective-permute-start | bytes 1572872 | tf_op jit(solution)/shard_map/ppermute | solution.py:320
  263.1 9.9 %collective-permute-done.35 = bf16[2,128,1024]{2,1,0:T(8,128)(2,1)S(1)} collective-permute-done((bf16[2,128,1024]{2,1,0:T(8,128)(2,1)S(1)}, bf16[2,128,1024]{2,1,0:T(8,128)(2,1)S(1)}, u32[]{:S(2)}, u32[]{:S(2)}) %collective-permute-start.35) | collective-permute-done | bytes 524320 | tf_op jit(solution)/shard_map/ppermute | solution.py:320
  282.3 11.9 %fusion.100 = f32[2048,2048]{1,0:T(8,128)} fusion(bf16[2048,1024]{1,0:T(8,128)(2,1)S(1)} %constant_dynamic-update-slice_fusion.80, bf16[2048,1024]{1,0:T(8,128)(2,1)S(1)} %copy-done.33), kind=kOutput, calls=%fused_computation.412 | convolution fusion | flops 8589934592 | bytes 25165824 | tf_op jit(solution)/shard_map/dot_general | solution.py:36
  294.2 26.6 %fusion.6 = (bf16[2048,2048]{1,0:T(8,128)(2,1)}, bf16[2048,2048]{1,0:T(8,128)(2,1)}) fusion(f32[2048,2048]{1,0:T(8,128)} %fusion.100, bf16[2048,1024]{1,0:T(8,128)(2,1)} %copy-done.30, bf16[1024,1024]{1,0:T(8,128)(2,1)} %collective-permute-done.17, bf16[1024,1024]{1,0:T(8,128)(2,1)} %copy-done.20), kind=kOutput, calls=%fused_computation.11 | convolution fusion | flops 8690597888 | bytes 41943040 | tf_op jit(solution)/shard_map/dot_general | solution.py:36
  320.8 13.1 %convolution_convert_fusion.2 = bf16[2048,1024]{1,0:T(8,128)(2,1)S(1)} fusion(bf16[2048,2048]{1,0:T(8,128)(2,1)} %get-tuple-element.44, bf16[1024,1024]{1,0:T(8,128)(2,1)} %collective-permute-done.17, bf16[1024,1024]{1,0:T(8,128)(2,1)} %copy-done.20), kind=kOutput, calls=%fused_computation.57 | convolution fusion | flops 8600420352 | bytes 16777216 | tf_op jit(solution)/shard_map/dot_general | solution.py:44
  337.7 11.5 %convolution_convert_fusion.1 = bf16[2048,1024]{1,0:T(8,128)(2,1)S(1)} fusion(bf16[2048,2048]{1,0:T(8,128)(2,1)} %get-tuple-element.45, bf16[2048,1024]{1,0:T(8,128)(2,1)S(1)} %copy-done.27), kind=kOutput, calls=%fused_computation.56 | convolution fusion | flops 8592031744 | bytes 16777216 | tf_op jit(solution)/shard_map/dot_general | solution.py:44
  364.8 18.1 %collective-permute-done.68 = bf16[2,2,128,1024]{3,2,1,0:T(8,128)(2,1)S(1)} collective-permute-done((bf16[2,2,128,1024]{3,2,1,0:T(8,128)(2,1)S(1)}, bf16[2,2,128,1024]{3,2,1,0:T(8,128)(2,1)S(1)}, u32[]{:S(2)}, u32[]{:S(2)}) %collective-permute-start.68) | collective-permute-done | bytes 1048608 | tf_op jit(solution)/shard_map/ppermute | solution.py:320
  418.3 15.8 %collective-permute-start.74 = (bf16[128,1024]{1,0:T(8,128)(2,1)S(1)}, bf16[128,1024]{1,0:T(8,128)(2,1)S(1)}, u32[]{:S(2)}, u32[]{:S(2)}) collective-permute-start(bf16[128,1024]{1,0:T(8,128)(2,1)S(1)} %get-tuple-element.123), channel_id=1, source_target_pairs={{0,6},{1,7},{2,0},{3,1},{4,2},{5,3},{6,4},{7,5},{8,14},{9,15},{10,... | collective-permute-start | bytes 786440 | tf_op jit(solution)/shard_map/ppermute | solution.py:310
  485.9 11.1 %add_convert_fusion = bf16[1024,1024]{1,0:T(8,128)(2,1)} fusion(f32[1024,1024]{1,0:T(8,128)} %copy-done.11, bf16[1024,1024]{1,0:T(8,128)(2,1)} %collective-permute-done.36, bf16[2048,1024]{1,0:T(8,128)(2,1)} %copy-done.32, bf16[2048,2048]{1,0:T(8,128)(2,1)} %get-tuple-element.45), kind=kOutput, calls=%fused_computation.51 | convolution fusion | flops 4299161600 | bytes 16777216 | tf_op jit(solution)/shard_map/dot_general | solution.py:40
  516.9 67.8 %shard_map.247 = (bf16[2048,1536]{1,0:T(8,128)(2,1)S(1)}, f32[4,10,512]{2,1,0:T(8,128)S(1)}) custom-call(s32[9]{0:T(128)S(1)} %copy-done.7, bf16[2048,1536]{1,0:T(8,128)(2,1)S(1)} %copy-done.10, bf16[2048,1536]{1,0:T(8,128)(2,1)S(1)} %copy-done.10, bf16[2048,1536]{1,0:T(8,128)(2,1)S(1)} %copy-done.10, bf16[2048,512]{1,0:T(8,128)(2,1)S(1)} %copy-done.8, ...), custom_call_target="tpu_custom_call" | custom-call | flops 32212254720 | bytes 20971520 | tf_op jit(solution)/shard_map/pallas_call | solution.py:282
  585.9 10.5 %convolution_convert_fusion = bf16[1536,1024]{1,0:T(8,128)(2,1)S(1)} fusion(bf16[2048,1536]{1,0:T(8,128)(2,1)S(1)} %multiply_convert_fusion.1, bf16[1024,1024]{1,0:T(8,128)(2,1)} %copy-done.51, bf16[1024,1024]{1,0:T(8,128)(2,1)} %fusion.14), kind=kOutput, calls=%fused_computation.55 | convolution fusion | flops 6452412416 | bytes 13631488 | tf_op jit(solution)/shard_map/dot_general | solution.py:44
  612.5 9.5 %collective-permute-start.51 = (bf16[2,2,4,32,1024]{4,3,2,1,0:T(8,128)(2,1)}, bf16[2,2,4,32,1024]{4,3,2,1,0:T(8,128)(2,1)S(1)}, u32[]{:S(2)}, u32[]{:S(2)}) collective-permute-start(bf16[2,2,4,32,1024]{4,3,2,1,0:T(8,128)(2,1)} %bitcast.101), channel_id=1, source_target_pairs={{0,8},{8,0},{16,24},{24,16},{1,9},{9,1},{17,25},{25,17},{2,10},{10... | collective-permute-start | bytes 3145736 | tf_op jit(solution)/shard_map/ppermute | solution.py:320
  629.7 8.6 %collective-permute-done.48 = bf16[2,2,4,32,1024]{4,3,2,1,0:T(8,128)(2,1)S(1)} collective-permute-done((bf16[2,2,4,32,1024]{4,3,2,1,0:T(8,128)(2,1)}, bf16[2,2,4,32,1024]{4,3,2,1,0:T(8,128)(2,1)S(1)}, u32[]{:S(2)}, u32[]{:S(2)}) %collective-permute-start.48) | collective-permute-done | bytes 1048608 | tf_op jit(solution)/shard_map/ppermute | solution.py:320
  664.6 8.7 %collective-permute-start.53 = (bf16[4,32,1024]{2,1,0:T(8,128)(2,1)}, bf16[4,32,1024]{2,1,0:T(8,128)(2,1)S(1)}, u32[]{:S(2)}, u32[]{:S(2)}) collective-permute-start(bf16[4,32,1024]{2,1,0:T(8,128)(2,1)} %get-tuple-element.126), channel_id=1, source_target_pairs={{0,4},{1,5},{2,6},{3,7},{4,0},{5,1},{6,2},{7,3},{8,12},{9,13},{10,... | collective-permute-start | bytes 786440 | tf_op jit(solution)/shard_map/ppermute | solution.py:310
  674.1 10.4 %collective-permute-done.53 = bf16[4,32,1024]{2,1,0:T(8,128)(2,1)S(1)} collective-permute-done((bf16[4,32,1024]{2,1,0:T(8,128)(2,1)}, bf16[4,32,1024]{2,1,0:T(8,128)(2,1)S(1)}, u32[]{:S(2)}, u32[]{:S(2)}) %collective-permute-start.53) | collective-permute-done | bytes 262176 | tf_op jit(solution)/shard_map/ppermute | solution.py:310
  702.6 8.9 %collective-permute-start.42 = (f32[40,128]{1,0:T(8,128)S(1)}, f32[40,128]{1,0:T(8,128)S(1)}, u32[]{:S(2)}, u32[]{:S(2)}) collective-permute-start(f32[40,128]{1,0:T(8,128)S(1)} %fusion.94), channel_id=1, source_target_pairs={{0,6},{1,7},{2,0},{3,1},{4,2},{5,3},{6,4},{7,5},{8,14},{9,15},{10,... | collective-permute-start | bytes 61448 | tf_op jit(solution)/shard_map/ppermute | solution.py:310
  (475 shorter events, 334.4 us)
Async XLA Ops:
  2.4 35.5 %collective-permute-start.1 = (bf16[3,32,1024]{2,1,0:T(8,128)(2,1)}, bf16[3,32,1024]{2,1,0:T(8,128)(2,1)}, u32[]{:S(2)}, u32[]{:S(2)}) collective-permute-start(bf16[3,32,1024]{2,1,0:T(8,128)(2,1)} %fusion.73), channel_id=1, source_target_pairs={{0,6},{1,7},{2,0},{3,1},{4,2},{5,3},{6,4},{7,5},{8,14},{9,15},{10,... | collective-permute-start | bytes 589832 | tf_op jit(solution)/shard_map/ppermute | solution.py:310
  7.5 33.2 %collective-permute-start.5 = (bf16[3,32,1024]{2,1,0:T(8,128)(2,1)}, bf16[3,32,1024]{2,1,0:T(8,128)(2,1)}, u32[]{:S(2)}, u32[]{:S(2)}) collective-permute-start(bf16[3,32,1024]{2,1,0:T(8,128)(2,1)} %fusion.73), channel_id=1, source_target_pairs={{0,4},{1,5},{2,6},{3,7},{4,0},{5,1},{6,2},{7,3},{8,12},{9,13},{10,... | collective-permute-start | bytes 589832 | tf_op jit(solution)/shard_map/ppermute | solution.py:310
  7.5 35.4 %collective-permute-start.6 = (bf16[3,32,1024]{2,1,0:T(8,128)(2,1)}, bf16[3,32,1024]{2,1,0:T(8,128)(2,1)S(1)}, u32[]{:S(2)}, u32[]{:S(2)}) collective-permute-start(bf16[3,32,1024]{2,1,0:T(8,128)(2,1)} %fusion.73), channel_id=1, source_target_pairs={{0,2},{1,3},{2,4},{3,5},{4,6},{5,7},{6,0},{7,1},{8,10},{9,11},{10,... | collective-permute-start | bytes 589832 | tf_op jit(solution)/shard_map/ppermute | solution.py:310
  35.2 34.8 %collective-permute-start.14 = (bf16[128,1024]{1,0:T(8,128)(2,1)S(1)}, bf16[128,1024]{1,0:T(8,128)(2,1)S(1)}, u32[]{:S(2)}, u32[]{:S(2)}) collective-permute-start(bf16[128,1024]{1,0:T(8,128)(2,1)S(1)} %copy-done.29), channel_id=1, source_target_pairs={{0,4},{1,5},{2,6},{3,7},{4,0},{5,1},{6,2},{7,3},{8,12},{9,13},{10,... | collective-permute-start | bytes 786440 | tf_op jit(solution)/shard_map/ppermute | solution.py:310
  37.9 37.1 %collective-permute-start.15 = (bf16[128,1024]{1,0:T(8,128)(2,1)S(1)}, bf16[128,1024]{1,0:T(8,128)(2,1)S(1)}, u32[]{:S(2)}, u32[]{:S(2)}) collective-permute-start(bf16[128,1024]{1,0:T(8,128)(2,1)S(1)} %copy-done.29), channel_id=1, source_target_pairs={{0,2},{1,3},{2,4},{3,5},{4,6},{5,7},{6,0},{7,1},{8,10},{9,11},{10,... | collective-permute-start | bytes 786440 | tf_op jit(solution)/shard_map/ppermute | solution.py:310
  40.7 31.8 %collective-permute-start.18 = (bf16[128,1024]{1,0:T(8,128)(2,1)}, bf16[128,1024]{1,0:T(8,128)(2,1)S(1)}, u32[]{:S(2)}, u32[]{:S(2)}) collective-permute-start(bf16[128,1024]{1,0:T(8,128)(2,1)} %bitcast.58), channel_id=1, source_target_pairs={{0,6},{1,7},{2,0},{3,1},{4,2},{5,3},{6,4},{7,5},{8,14},{9,15},{10,... | collective-permute-start | bytes 786440 | tf_op jit(solution)/shard_map/ppermute | solution.py:310
  42.8 148.6 %collective-permute-start.22 = (bf16[128,1024]{1,0:T(8,128)(2,1)}, bf16[128,1024]{1,0:T(8,128)(2,1)S(1)}, u32[]{:S(2)}, u32[]{:S(2)}) collective-permute-start(bf16[128,1024]{1,0:T(8,128)(2,1)} %bitcast.58), channel_id=1, source_target_pairs={{0,4},{1,5},{2,6},{3,7},{4,0},{5,1},{6,2},{7,3},{8,12},{9,13},{10,... | collective-permute-start | bytes 786440 | tf_op jit(solution)/shard_map/ppermute | solution.py:310
  43.8 148.9 %collective-permute-start.23 = (bf16[128,1024]{1,0:T(8,128)(2,1)}, bf16[128,1024]{1,0:T(8,128)(2,1)S(1)}, u32[]{:S(2)}, u32[]{:S(2)}) collective-permute-start(bf16[128,1024]{1,0:T(8,128)(2,1)} %bitcast.58), channel_id=1, source_target_pairs={{0,2},{1,3},{2,4},{3,5},{4,6},{5,7},{6,0},{7,1},{8,10},{9,11},{10,... | collective-permute-start | bytes 786440 | tf_op jit(solution)/shard_map/ppermute | solution.py:310
  79.8 123.6 %collective-permute-start.31 = (bf16[128,1024]{1,0:T(8,128)(2,1)}, bf16[128,1024]{1,0:T(8,128)(2,1)S(1)}, u32[]{:S(2)}, u32[]{:S(2)}) collective-permute-start(bf16[128,1024]{1,0:T(8,128)(2,1)} %constant_dynamic-slice_fusion.1), channel_id=1, source_target_pairs={{0,4},{1,5},{2,6},{3,7},{4,0},{5,1},{6,2},{7,3},{8,12},{9,13},{10,... | collective-permute-start | bytes 786440 | tf_op jit(solution)/shard_map/ppermute | solution.py:310
  104.6 99.0 %collective-permute-start.32 = (bf16[128,1024]{1,0:T(8,128)(2,1)}, bf16[128,1024]{1,0:T(8,128)(2,1)S(1)}, u32[]{:S(2)}, u32[]{:S(2)}) collective-permute-start(bf16[128,1024]{1,0:T(8,128)(2,1)} %constant_dynamic-slice_fusion.1), channel_id=1, source_target_pairs={{0,2},{1,3},{2,4},{3,5},{4,6},{5,7},{6,0},{7,1},{8,10},{9,11},{10,... | collective-permute-start | bytes 786440 | tf_op jit(solution)/shard_map/ppermute | solution.py:310
  119.1 85.0 %collective-permute-start.19 = (bf16[2,128,1024]{2,1,0:T(8,128)(2,1)S(1)}, bf16[2,128,1024]{2,1,0:T(8,128)(2,1)S(1)}, u32[]{:S(2)}, u32[]{:S(2)}) collective-permute-start(bf16[2,128,1024]{2,1,0:T(8,128)(2,1)S(1)} %pad_maximum_fusion.14), channel_id=1, source_target_pairs={{0,8},{8,0},{16,24},{24,16},{1,9},{9,1},{17,25},{25,17},{2,10},{10... | collective-permute-start | bytes 1572872 | tf_op jit(solution)/shard_map/ppermute | solution.py:320
  203.5 71.5 %collective-permute-start.16 = (bf16[1024,1024]{1,0:T(8,128)(2,1)S(1)}, bf16[1024,1024]{1,0:T(8,128)(2,1)S(1)}, u32[]{:S(2)}, u32[]{:S(2)}) collective-permute-start(bf16[1024,1024]{1,0:T(8,128)(2,1)S(1)} %convolution_convert_fusion.4), channel_id=1, source_target_pairs={{0,1},{1,0},{2,3},{3,2},{4,5},{5,4},{6,7},{7,6},{8,9},{9,8},{10,11... | collective-permute-start | bytes 6291464 | tf_op jit(solution)/shard_map/ppermute | solution.py:304
  205.7 35.1 %collective-permute-start.21 = (bf16[2,128,1024]{2,1,0:T(8,128)(2,1)S(1)}, bf16[2,128,1024]{2,1,0:T(8,128)(2,1)S(1)}, u32[]{:S(2)}, u32[]{:S(2)}) collective-permute-start(bf16[2,128,1024]{2,1,0:T(8,128)(2,1)S(1)} %collective-permute-done.19), channel_id=1, source_target_pairs={{0,16},{8,24},{16,0},{24,8},{1,17},{9,25},{17,1},{25,9},{2,18},{10... | collective-permute-start | bytes 1572872 | tf_op jit(solution)/shard_map/ppermute | solution.py:320
  336.0 26.8 %collective-permute-start.61 = (bf16[2,2,128,1024]{3,2,1,0:T(8,128)(2,1)S(1)}, bf16[2,2,128,1024]{3,2,1,0:T(8,128)(2,1)S(1)}, u32[]{:S(2)}, u32[]{:S(2)}) collective-permute-start(bf16[2,2,128,1024]{3,2,1,0:T(8,128)(2,1)S(1)} %bitcast.384), channel_id=1, source_target_pairs={{0,8},{8,0},{16,24},{24,16},{1,9},{9,1},{17,25},{25,17},{2,10},{10... | collective-permute-start | bytes 3145736 | tf_op jit(solution)/shard_map/ppermute | solution.py:320
  349.8 33.2 %collective-permute-start.68 = (bf16[2,2,128,1024]{3,2,1,0:T(8,128)(2,1)S(1)}, bf16[2,2,128,1024]{3,2,1,0:T(8,128)(2,1)S(1)}, u32[]{:S(2)}, u32[]{:S(2)}) collective-permute-start(bf16[2,2,128,1024]{3,2,1,0:T(8,128)(2,1)S(1)} %bitcast.385), channel_id=1, source_target_pairs={{0,16},{8,24},{16,0},{24,8},{1,17},{9,25},{17,1},{25,9},{2,18},{10... | collective-permute-start | bytes 3145736 | tf_op jit(solution)/shard_map/ppermute | solution.py:320
  350.3 34.9 %collective-permute-start.71 = (bf16[2,2,128,1024]{3,2,1,0:T(8,128)(2,1)S(1)}, bf16[2,2,128,1024]{3,2,1,0:T(8,128)(2,1)S(1)}, u32[]{:S(2)}, u32[]{:S(2)}) collective-permute-start(bf16[2,2,128,1024]{3,2,1,0:T(8,128)(2,1)S(1)} %bitcast.383), channel_id=1, source_target_pairs={{0,8},{8,0},{16,24},{24,16},{1,9},{9,1},{17,25},{25,17},{2,10},{10... | collective-permute-start | bytes 3145736 | tf_op jit(solution)/shard_map/ppermute | solution.py:320
  358.6 89.7 %collective-permute-start.38 = (bf16[1024,1024]{1,0:T(8,128)(2,1)S(1)}, bf16[1024,1024]{1,0:T(8,128)(2,1)S(1)}, u32[]{:S(2)}, u32[]{:S(2)}) collective-permute-start(bf16[1024,1024]{1,0:T(8,128)(2,1)S(1)} %fusion.53), channel_id=1, source_target_pairs={{0,1},{1,0},{2,3},{3,2},{4,5},{5,4},{6,7},{7,6},{8,9},{9,8},{10,11... | collective-permute-start | bytes 6291464 | tf_op jit(solution)/shard_map/ppermute | solution.py:304
  361.0 34.8 %collective-permute-start.59 = (bf16[1,2,128,1024]{3,2,1,0:T(8,128)(2,1)S(1)}, bf16[1,2,128,1024]{3,2,1,0:T(8,128)(2,1)S(1)}, u32[]{:S(2)}, u32[]{:S(2)}) collective-permute-start(bf16[1,2,128,1024]{3,2,1,0:T(8,128)(2,1)S(1)} %slice.897), channel_id=1, source_target_pairs={{0,8},{8,0},{16,24},{24,16},{1,9},{9,1},{17,25},{25,17},{2,10},{10... | collective-permute-start | bytes 1572872 | tf_op jit(solution)/shard_map/ppermute | solution.py:320
  363.3 35.2 %collective-permute-start.62 = (bf16[1,2,128,1024]{3,2,1,0:T(8,128)(2,1)S(1)}, bf16[1,2,128,1024]{3,2,1,0:T(8,128)(2,1)S(1)}, u32[]{:S(2)}, u32[]{:S(2)}) collective-permute-start(bf16[1,2,128,1024]{3,2,1,0:T(8,128)(2,1)S(1)} %slice.903), channel_id=1, source_target_pairs={{0,16},{8,24},{16,0},{24,8},{1,17},{9,25},{17,1},{25,9},{2,18},{10... | collective-permute-start | bytes 1572872 | tf_op jit(solution)/shard_map/ppermute | solution.py:320
  405.6 28.6 %collective-permute-start.64 = (bf16[128,1024]{1,0:T(8,128)(2,1)S(1)}, bf16[128,1024]{1,0:T(8,128)(2,1)S(1)}, u32[]{:S(2)}, u32[]{:S(2)}) collective-permute-start(bf16[128,1024]{1,0:T(8,128)(2,1)S(1)} %get-tuple-element.125), channel_id=1, source_target_pairs={{0,6},{1,7},{2,0},{3,1},{4,2},{5,3},{6,4},{7,5},{8,14},{9,15},{10,... | collective-permute-start | bytes 786440 | tf_op jit(solution)/shard_map/ppermute | solution.py:310
  410.4 34.0 %collective-permute-start.73 = (bf16[128,1024]{1,0:T(8,128)(2,1)S(1)}, bf16[128,1024]{1,0:T(8,128)(2,1)S(1)}, u32[]{:S(2)}, u32[]{:S(2)}) collective-permute-start(bf16[128,1024]{1,0:T(8,128)(2,1)S(1)} %get-tuple-element.122), channel_id=1, source_target_pairs={{0,4},{1,5},{2,6},{3,7},{4,0},{5,1},{6,2},{7,3},{8,12},{9,13},{10,... | collective-permute-start | bytes 786440 | tf_op jit(solution)/shard_map/ppermute | solution.py:310
  444.4 41.5 %collective-permute-start.36 = (bf16[1024,1024]{1,0:T(8,128)(2,1)}, bf16[1024,1024]{1,0:T(8,128)(2,1)}, u32[]{:S(2)}, u32[]{:S(2)}) collective-permute-start(bf16[1024,1024]{1,0:T(8,128)(2,1)} %fusion.50), channel_id=1, source_target_pairs={{0,1},{1,0},{2,3},{3,2},{4,5},{5,4},{6,7},{7,6},{8,9},{9,8},{10,11... | collective-permute-start | bytes 6291464 | tf_op jit(solution)/shard_map/ppermute | solution.py:304
  612.5 36.0 %collective-permute-start.51 = (bf16[2,2,4,32,1024]{4,3,2,1,0:T(8,128)(2,1)}, bf16[2,2,4,32,1024]{4,3,2,1,0:T(8,128)(2,1)S(1)}, u32[]{:S(2)}, u32[]{:S(2)}) collective-permute-start(bf16[2,2,4,32,1024]{4,3,2,1,0:T(8,128)(2,1)} %bitcast.101), channel_id=1, source_target_pairs={{0,8},{8,0},{16,24},{24,16},{1,9},{9,1},{17,25},{25,17},{2,10},{10... | collective-permute-start | bytes 3145736 | tf_op jit(solution)/shard_map/ppermute | solution.py:320
  629.7 60.8 %collective-permute-start.40 = (bf16[1024,1024]{1,0:T(8,128)(2,1)}, bf16[1024,1024]{1,0:T(8,128)(2,1)}, u32[]{:S(2)}, u32[]{:S(2)}) collective-permute-start(bf16[1024,1024]{1,0:T(8,128)(2,1)} %fusion.47), channel_id=1, source_target_pairs={{0,1},{1,0},{2,3},{3,2},{4,5},{5,4},{6,7},{7,6},{8,9},{9,8},{10,11... | collective-permute-start | bytes 6291464 | tf_op jit(solution)/shard_map/ppermute | solution.py:304
  (110 other events, 2464.3 us)

commit v2 on v1

v2 whole, which is shorter than its diff:
```python
import functools

import jax
import jax.numpy as jnp
from jax import lax
from jax.experimental import pallas as pl
from jax.experimental.pallas import tpu as pltpu
from jax.sharding import PartitionSpec as P

HD = 64
PAIR = 128
REACH = 1024
EPSILON = 1e-05
MASKED_SCORE = -1e30
FORWARD_VMEM = 44 * 1024 * 1024
BACKWARD_VMEM = 52 * 1024 * 1024
FORWARD_FLOPS = 20_000_000_000
BACKWARD_FLOPS = 40_000_000_000
NT = (((1,), (1,)), ((), ()))
TN = (((0,), (0,)), ((), ()))


def row_norm(values):
    mean = jnp.mean(values, axis=1, keepdims=True)
    centred = values - mean
    spread = jnp.mean(centred * centred, axis=1, keepdims=True)
    inverse = lax.rsqrt(spread + EPSILON)
    return (centred * inverse, inverse)


def norm_backward(upstream, normed, inverse, gain):
    scaled = upstream * gain
    mean_plain = jnp.mean(scaled, axis=1, keepdims=True)
    mean_cross = jnp.mean(scaled * normed, axis=1, keepdims=True)
    result = inverse * (scaled - mean_plain - normed * mean_cross)
    return (result, jnp.sum(upstream * normed, axis=0), jnp.sum(upstream, axis=0))


def dot_nt(left, right):
    return lax.dot_general(left, right, NT, preferred_element_type=jnp.float32)


def dot_nn(left, right):
    return jnp.dot(left, right, preferred_element_type=jnp.float32)


def dot_tn(left, right):
    return lax.dot_general(left, right, TN, preferred_element_type=jnp.float32)


def make_strip(line_ref, strips, begin=0):
    for h in range(strips.shape[0]):
        spread = jnp.broadcast_to(line_ref[begin + h : begin + h + 1, :], strips.shape[1:])
        strips[h] = pltpu.roll(spread, 0, 1, stride=1, stride_axis=0)


def strip_line(strip):
    rows, span = strip.shape
    while rows > 1:
        rows //= 2
        strip = strip[:rows] + pltpu.roll(strip[rows : 2 * rows], span - rows, 1)
    return strip


def strip_at(t, u, rows, block):
    return pl.ds(pl.multiple_of(t * block + (block - u * rows), rows), block)


def strip_tile(strips, h, t, block):
    rows = strips.shape[1]
    parts = [strips[h, :, strip_at(t, u, rows, block)] for u in range(block // rows)]
    return jnp.concatenate(parts, axis=0)


def add_to_strip(strips, h, t, tile):
    rows, block = strips.shape[1], tile.shape[0]
    for u in range(block // rows):
        strips[h, :, strip_at(t, u, rows, block)] += tile[u * rows : (u + 1) * rows]


def place_of(index, me, per_slot):
    return ((index // per_slot) ^ me) * per_slot + index % per_slot


def head_lanes(block, h):
    lanes = lax.broadcasted_iota(jnp.int32, block.shape, 1)
    return jnp.where((lanes // HD) == h, block, jnp.zeros_like(block))


def columns_of(p, kind):
    return slice((3 * p + kind) * PAIR, (3 * p + kind + 1) * PAIR)


def attend_kernel(scalars, x_ref, first_ref, line_ref, out_ref, lse_ref, strips, v_t, kept, *, block, per_slot):
    i = pl.program_id(0)
    me = scalars[0]
    low = scalars[1 + i]
    heads = strips.shape[0]
    pairs = heads // 2

    @pl.when(i == 0)
    def _():
        make_strip(line_ref, strips)
        for p in range(pairs):
            v_t[p * PAIR : (p + 1) * PAIR] = x_ref[:, columns_of(p, 2)].T

    rows = pl.ds(pl.multiple_of(place_of(i, me, per_slot) * block, block), block)
    own = [head_lanes(x_ref[rows, columns_of(h // 2, 0)], h % 2) for h in range(heads)]
    first = first_ref[pl.ds(i, 1), :]
    key_index = lax.broadcasted_iota(jnp.int32, (block, block), 0)

    def rows_of(t):
        return pl.ds(pl.multiple_of(place_of(i - t, me, per_slot) * block, block), block)

    def fold(value):
        return value.reshape(block // 8, 8, block)

    def score_step(t, tops):
        here = rows_of(t)
        allowed = key_index >= (first - (i - t) * block)
        result = []
        for h in range(heads):
            scores = dot_nt(x_ref[here, columns_of(h // 2, 1)], own[h]) + strip_tile(strips, h, t, block)
            scores = jnp.where(allowed, scores, MASKED_SCORE)
            kept[h, t] = scores
            result.append(jnp.maximum(tops[h], jnp.max(fold(scores), axis=0)))
        return tuple(result)

    def value_step(t, carry):
        here = rows_of(t)
        result = []
        for h in range(heads):
            total, acc = carry[h]
            expo = jnp.exp(kept[h, t] - tops[h])
            total = total + jnp.sum(fold(expo), axis=0)
            acc = acc + dot_nn(v_t[h * HD : (h + 1) * HD, here], expo.astype(jnp.bfloat16))
            result.append((total, acc))
        return tuple(result)

    tops = lax.fori_loop(
        0, i - low + 1, score_step, (jnp.full((8, block), MASKED_SCORE, jnp.float32),) * heads
    )
    tops = [jnp.max(top, axis=0, keepdims=True) for top in tops]
    zero = (jnp.zeros((8, block), jnp.float32), jnp.zeros((HD, block), jnp.float32))
    done = lax.fori_loop(0, i - low + 1, value_step, (zero,) * heads)
    totals = [jnp.sum(total, axis=0, keepdims=True) for total, _ in done]
    for p in range(pairs):
        both = jnp.concatenate([done[h][1] / totals[h] for h in (2 * p, 2 * p + 1)], axis=0)
        out_ref[rows, p * PAIR : (p + 1) * PAIR] = both.T.astype(jnp.bfloat16)
    lse_ref[pl.ds(i, 1)] = jnp.concatenate([tops[h] + jnp.log(totals[h]) for h in range(heads)], axis=0)[None]


def attend_back_kernel(
    scalars,
    x_ref,
    mixed_ref,
    up_ref,
    first_ref,
    line_ref,
    lse_ref,
    grad_ref,
    sums_ref,
    strips,
    sums,
    k_t,
    dk,
    dv,
    *,
    block,
    per_slot,
    begin,
):
    i = pl.program_id(0)
    me = scalars[0]
    low = scalars[1 + i]
    heads = strips.shape[0]
    pairs = heads // 2

    def columns(p, kind):
        return slice((3 * (p + begin) + kind) * PAIR, (3 * (p + begin) + kind + 1) * PAIR)

    def wide_columns(p):
        return slice((p + begin) * PAIR, (p + begin + 1) * PAIR)

    @pl.when(i == 0)
    def _():
        make_strip(line_ref, strips, 2 * begin)
        for p in range(pairs):
            k_t[p * PAIR : (p + 1) * PAIR] = x_ref[:, columns(p, 1)].T
        dk[...] = jnp.zeros_like(dk)
        dv[...] = jnp.zeros_like(dv)
        sums[...] = jnp.zeros_like(sums)

    rows = pl.ds(pl.multiple_of(place_of(i, me, per_slot) * block, block), block)
    own_q = [head_lanes(x_ref[rows, columns(h // 2, 0)], h % 2) for h in range(heads)]
    own_up = [head_lanes(up_ref[rows, wide_columns(h // 2)], h % 2) for h in range(heads)]
    picks = lax.broadcasted_iota(jnp.int32, (8, PAIR), 1) // HD == lax.broadcasted_iota(jnp.int32, (8, PAIR), 0)
    picks = picks.astype(jnp.bfloat16)
    deltas = []
    for p in range(pairs):
        span = wide_columns(p)
        product = up_ref[rows, span].astype(jnp.float32) * mixed_ref[rows, span].astype(jnp.float32)
        high = product.astype(jnp.bfloat16)
        rest = (product - high.astype(jnp.float32)).astype(jnp.bfloat16)
        both = dot_nt(picks, high) + dot_nt(picks, rest)
        deltas += [both[0:1], both[1:2]]
    first = first_ref[pl.ds(i, 1), :]
    key_index = lax.broadcasted_iota(jnp.int32, (block, block), 0)

    def step(t, carry):
        here = pl.ds(pl.multiple_of(place_of(i - t, me, per_slot) * block, block), block)
        allowed = key_index >= (first - (i - t) * block)
        dq = []
        for p in range(pairs):
            span = slice(p * PAIR, (p + 1) * PAIR)
            keys = x_ref[here, columns(p, 1)]
            values = x_ref[here, columns(p, 2)]
            dk_new = dk[here, span]
            dv_new = dv[here, span]
            for h in (2 * p, 2 * p + 1):
                scores = dot_nt(keys, own_q[h]) + strip_tile(strips, h, t, block)
                scores = jnp.where(allowed, scores, MASKED_SCORE)
                probs = jnp.exp(scores - lse_ref[i, 2 * begin + h : 2 * begin + h + 1, :])
                score_grad = probs * (dot_nt(values, own_up[h]) - deltas[h])
                add_to_strip(sums, h, t, score_grad)
                low_grad = score_grad.astype(jnp.bfloat16)
                dv_new = dv_new + dot_nn(probs.astype(jnp.bfloat16), own_up[h])
                dk_new = dk_new + dot_nn(low_grad, own_q[h])
                dq.append(carry[h] + dot_nn(k_t[h * HD : (h + 1) * HD, here], low_grad))
            dk[here, span] = dk_new
            dv[here, span] = dv_new
        return tuple(dq)

    dq = lax.fori_loop(0, i - low + 1, step, (jnp.zeros((HD, block), jnp.float32),) * heads)
    for p in range(pairs):
        both = jnp.concatenate(dq[2 * p : 2 * p + 2], axis=0).T * (HD ** (-0.5))
        grad_ref[rows, columns_of(p, 0)] = both.astype(jnp.bfloat16)

    @pl.when(i == pl.num_programs(0) - 1)
    def _():
        for p in range(pairs):
            span = slice(p * PAIR, (p + 1) * PAIR)
            grad_ref[:, columns_of(p, 1)] = dk[:, span].astype(jnp.bfloat16)
            grad_ref[:, columns_of(p, 2)] = dv[:, span].astype(jnp.bfloat16)
        for h in range(heads):
            sums_ref[h : h + 1, :] = strip_line(sums[h])


WHOLE = pl.BlockSpec(memory_space=pltpu.VMEM)


def ignoring(kernel, first, count):
    def body(*refs):
        kernel(*refs[:first], *refs[first + count :])

    return body


def attend(joined, first, lines, scalars, block, per_slot, waits):
    length = joined.shape[0]
    heads, span = lines.shape
    blocks = length // block
    strip = pltpu.VMEM((heads, min(128, block), span), jnp.float32)
    grid_spec = pltpu.PrefetchScalarGridSpec(
        num_scalar_prefetch=1,
        grid=(blocks,),
        in_specs=[WHOLE] * 3 + [ANYWHERE] * len(waits),
        out_specs=[WHOLE] * 2,
        scratch_shapes=[
            strip,
            pltpu.VMEM((heads * HD, length), jnp.bfloat16),
            pltpu.VMEM((heads, span // block - 1, block, block), jnp.float32),
        ],
    )
    return pl.pallas_call(
        ignoring(functools.partial(attend_kernel, block=block, per_slot=per_slot), 4, len(waits)),
        grid_spec=grid_spec,
        out_shape=[
            jax.ShapeDtypeStruct((length, heads * HD), jnp.bfloat16),
            jax.ShapeDtypeStruct((blocks, heads, block), jnp.float32),
        ],
        compiler_params=pltpu.CompilerParams(vmem_limit_bytes=FORWARD_VMEM),
        cost_estimate=pl.CostEstimate(flops=FORWARD_FLOPS, bytes_accessed=8 * length * heads * HD, transcendentals=0),
    )(scalars, joined, first, lines, *waits)


def attend_back(joined, mixed, upstream, first, lines, lse, scalars, block, per_slot, begin, end, waits):
    length = joined.shape[0]
    span = lines.shape[1]
    heads = 2 * (end - begin)
    blocks = length // block
    strip = pltpu.VMEM((heads, min(128, block), span), jnp.float32)
    grid_spec = pltpu.PrefetchScalarGridSpec(
        num_scalar_prefetch=1,
        grid=(blocks,),
        in_specs=[WHOLE] * 6 + [ANYWHERE] * len(waits),
        out_specs=[WHOLE] * 2,
        scratch_shapes=[
            strip,
            strip,
            pltpu.VMEM((heads * HD, length), jnp.bfloat16),
            pltpu.VMEM((length, heads * HD), jnp.float32),
            pltpu.VMEM((length, heads * HD), jnp.float32),
        ],
    )
    return pl.pallas_call(
        ignoring(
            functools.partial(attend_back_kernel, block=block, per_slot=per_slot, begin=begin), 7, len(waits)
        ),
        grid_spec=grid_spec,
        out_shape=[
            jax.ShapeDtypeStruct((length, 3 * heads * HD), jnp.bfloat16),
            jax.ShapeDtypeStruct((heads, span), jnp.float32),
        ],
        compiler_params=pltpu.CompilerParams(vmem_limit_bytes=BACKWARD_VMEM),
        cost_estimate=pl.CostEstimate(
            flops=BACKWARD_FLOPS // 8 * heads, bytes_accessed=20 * length * heads * HD, transcendentals=0
        ),
    )(scalars, joined, mixed, upstream, first, lines, lse, *waits)


class Net:
    def __init__(self, wide, narrow, group):
        self.wide, self.narrow, self.group = wide, narrow, group
        self.ring = narrow // group
        self.bits = wide.bit_length() - 1

    def from_group(self, value, s):
        if s == 0:
            return value
        return lax.ppermute(value, "narrow", [(i, i ^ s) for i in range(self.narrow)])

    def from_ring(self, value, r):
        return self.from_group(value, r * self.group)

    def from_wide(self, value, s):
        if s == 0:
            return value
        return lax.ppermute(value, "wide", [(i, i ^ s) for i in range(self.wide)])

    def bit_order(self, turn):
        return [(b + turn) % self.bits for b in range(self.bits)]

    def halves(self):
        cut = max(self.ring // 2, 1)
        return [list(range(cut)), list(range(cut, self.ring))]

    def ring_slots(self, quarter):
        return [self.from_ring(quarter, r) for r in range(self.ring)]

    def ring_doubling(self, own):
        slots = [own]
        r = 1
        while r < self.ring:
            away = self.from_ring(jnp.stack(slots, axis=0), r)
            slots = slots + [away[k] for k in range(r)]
            r *= 2
        return slots

    def spread(self, unit, turn):
        pieces, steps = {0: unit}, []
        for b in self.bit_order(turn):
            steps.append({s ^ (1 << b): self.from_wide(piece, 1 << b) for s, piece in pieces.items()})
            pieces.update(steps[-1])
        return [pieces[s] for s in range(self.wide)]

    def spread_doubling(self, unit, turn):
        order, pieces = [0], [unit]
        for b in self.bit_order(turn):
            away = self.from_wide(jnp.stack(pieces, axis=0), 1 << b)
            order = order + [s ^ (1 << b) for s in order]
            pieces = pieces + [away[k] for k in range(len(pieces))]
        return [pieces[order.index(s)] for s in range(self.wide)]

    def share(self, own):
        me = lax.axis_index("wide")
        pieces = [self.from_wide(own, s) for s in range(self.wide)]
        for b in range(self.bits):
            swap = (me >> b) & 1 == 1
            pieces = [jnp.where(swap, pieces[s ^ (1 << b)], piece) for s, piece in enumerate(pieces)]
        return pieces

    def total(self, value):
        value = value + sum(self.from_group(value, s) for s in range(1, self.group))
        value = value + sum(self.from_ring(value, r) for r in range(1, self.ring))
        return value + sum(self.from_wide(value, s) for s in range(1, self.wide))


ANYWHERE = pl.BlockSpec(memory_space=pl.ANY)


def hold_kernel(*refs):
    pass


def after(value, *others):
    values, tree = jax.tree.flatten(value)
    waits = jax.tree.leaves(others)
    if len(values) + len(waits) < 2 or not values:
        return value
    held = pl.pallas_call(
        hold_kernel,
        in_specs=[ANYWHERE] * (len(values) + len(waits)),
        out_specs=[ANYWHERE] * len(values),
        out_shape=[jax.ShapeDtypeStruct(one.shape, one.dtype) for one in values],
        input_output_aliases={k: k for k in range(len(values))},
    )(*values, *waits)
    return jax.tree.unflatten(tree, held)


def add_low(kept, arrived):
    return (kept.astype(jnp.float32) + arrived.astype(jnp.float32)).astype(jnp.bfloat16)


class WideSum:
    def __init__(self, net, value, turn):
        self.net = net
        self.bits = list(reversed(net.bit_order(turn)))
        self.value = value.reshape((2,) * net.bits + value.shape[1:])
        self.left = list(range(net.bits - 1, -1, -1))
        self.sent = False

    def send(self):
        self.sent = True
        bit = self.bits.pop(0)
        axis = self.left.index(bit)
        self.left.pop(axis)
        self.kept = lax.index_in_dim(self.value, 0, axis, keepdims=False)
        self.arrived = self.net.from_wide(lax.index_in_dim(self.value, 1, axis, keepdims=False), 1 << bit)
        return self

    def add(self, *others):
        self.value = add_low(self.kept, after(self.arrived, *others))
        self.sent = False
        return self

    def finish(self):
        if self.sent:
            self.add()
        while self.bits:
            self.send().add()
        return self.value


class RingSum:
    def __init__(self, net, values):
        self.net, self.values = net, list(values)
        self.sent = False

    def send(self):
        self.sent = True
        keep = len(self.values) // 2
        self.arrived = self.net.from_ring(jnp.stack(self.values[keep:], axis=0), keep)
        return self

    def add(self, *others):
        arrived = after(self.arrived, *others)
        self.sent = False
        keep = len(self.values) // 2
        self.values = [add_low(value, arrived[k]) for k, value in enumerate(self.values[:keep])]
        return self

    def finish(self):
        if self.sent:
            self.add()
        while len(self.values) > 1:
            self.send().add()
        return self.values[0]


def assemble_kernel(*refs, plan):
    out_ref = refs[-1]
    for ref, source, rows, begin in plan:
        out_ref[begin : begin + rows, :] = refs[ref][source]


def assemble(arrays, plan, rows, waits=()):
    return pl.pallas_call(
        ignoring(functools.partial(assemble_kernel, plan=plan), len(arrays), len(waits)),
        in_specs=[WHOLE] * len(arrays) + [ANYWHERE] * len(waits),
        out_specs=WHOLE,
        out_shape=jax.ShapeDtypeStruct((rows, arrays[0].shape[-1]), arrays[0].dtype),
        compiler_params=pltpu.CompilerParams(vmem_limit_bytes=24 * 1024 * 1024),
    )(*arrays, *waits)


def on_device(
    inputs,
    seg_ids,
    buckets,
    norm1_gain,
    norm1_shift,
    w_query,
    w_key,
    w_value,
    w_out,
    norm2_gain,
    norm2_shift,
    w_up,
    w_down,
    rel_table,
    out_grad,
    *,
    wide,
    narrow,
):
    bf16, f32 = jnp.bfloat16, jnp.float32
    tokens, width = inputs.shape
    length = seg_ids.shape[1]
    group = length // tokens
    net = Net(wide, narrow, group)
    ring = net.ring
    head_rows = w_query.shape[0]
    heads_here = rel_table.shape[1]
    piece_rows = head_rows // wide
    scale = HD ** (-0.5)
    block = min(256, tokens)
    per_slot = tokens // block
    blocks = length // block
    reach_blocks = min(blocks, -(-REACH // block) + 1)
    me_wide = lax.axis_index("wide")
    me_narrow = lax.axis_index("narrow")
    me_group = me_narrow % group
    me_ring = me_narrow // group
    halves = net.halves()

    def my_part(shard, axis=0):
        size = shard.shape[axis] // wide
        return lax.dynamic_slice_in_dim(shard, me_wide * size, size, axis)

    def all_group(own):
        return jnp.concatenate([own] + [net.from_group(own, s) for s in range(1, group)], axis=0)

    def away_parts(parts_of):
        return [net.from_group(parts_of(s).astype(bf16), s) for s in range(1, group)]

    def slot(value, s):
        return value[s * tokens : (s + 1) * tokens]

    def add_parts(own, away):
        for part in away:
            own = own + part.astype(f32)
        return own

    table_low = []
    left = rel_table
    for _ in range(3):
        table_low.append(lax.reduce_precision(left, 8, 7))
        left = left - table_low[-1]
    table_flat = jnp.stack(table_low, axis=0).astype(bf16).reshape(-1)
    table_row = jnp.pad(table_flat, (0, 16 * width - table_flat.size)).reshape(16, width)
    attention_quarter = my_part(jnp.stack([w_query, w_key, w_value, w_out], axis=0), 1).reshape(-1, width)
    first_slots = net.ring_slots(jnp.concatenate([attention_quarter, table_row], axis=0))
    attention_rows = attention_quarter.shape[0]
    table_slots = [
        rows[attention_rows][: table_flat.size].reshape((3,) + rel_table.shape).astype(f32).sum(0)
        for rows in first_slots
    ]
    attention_units = [
        jnp.stack([first_slots[r][:attention_rows].reshape(4, piece_rows, width) for r in places], axis=0)
        for places in halves
    ]
    attention_pieces = [net.spread_doubling(unit, turn) for turn, unit in enumerate(attention_units)]

    ffn_own = jnp.concatenate([my_part(w_up, 1).T, my_part(w_down)], axis=0)
    unit = ffn_own.shape[0] // 2
    own_out = {1 << b: net.from_wide(ffn_own, 1 << b) for b in range(net.bits)}

    values_in = inputs.astype(f32)
    normed1, inverse1 = row_norm(values_in)
    a1_own = (normed1 * norm1_gain + norm1_shift).astype(bf16)
    a1_away = [net.from_group(a1_own, s) for s in range(1, group)]
    a1 = jnp.concatenate([a1_own] + a1_away, axis=0)
    ffn_slots = net.ring_slots(after(ffn_own, first_slots[1:], a1_away, list(own_out.values())))

    per_pair = PAIR // head_rows
    pairs = ring // per_pair
    order = [
        (p * per_pair + r, t, s)
        for p in range(pairs)
        for t in range(3)
        for r in range(per_pair)
        for s in range(wide)
    ] + [(r, 3, s) for r in range(ring) for s in range(wide)]
    place_in_half = {r: (half, at) for half, places in enumerate(halves) for at, r in enumerate(places)}
    plan = []
    for at, (r, t, s) in enumerate(order):
        half, place = place_in_half[r]
        plan.append((half * wide + s, (place, t), piece_rows, at * piece_rows))
    w_attention = assemble(attention_pieces[0] + attention_pieces[1], plan, len(order) * piece_rows)
    w_joined = w_attention[: 3 * ring * head_rows]
    w_out_full = w_attention[3 * ring * head_rows :]
    column_kind = (jnp.arange(w_joined.shape[0]) // PAIR) % 3
    column_scale = jnp.where(column_kind == 0, jnp.asarray(scale, f32), jnp.asarray(1.0, f32))
    joined = (dot_nt(a1, w_joined) * column_scale).astype(bf16)
    dy = all_group(out_grad)

    reach = reach_blocks * block
    one_hot = (buckets[:reach, None] == jnp.arange(rel_table.shape[0])[None, :]).astype(f32)

    def head_of(r, h):
        return ((me_wide ^ (h * (HD // piece_rows))) * piece_rows) // HD

    table_here = jnp.concatenate(
        [
            lax.dynamic_slice_in_dim(table_slots[r], head_of(r, h), 1, 1)
            for r in range(ring)
            for h in range(heads_here)
        ],
        axis=1,
    )
    line = jnp.dot(one_hot, table_here, precision=lax.Precision.HIGHEST, preferred_element_type=f32).T
    lines = jnp.concatenate([jnp.full((line.shape[0], block), MASKED_SCORE, f32), line], axis=1)

    segments = lax.dynamic_slice_in_dim(seg_ids, me_ring, 1, 0)[0]
    first = jnp.sum((segments[None, :] < segments[:, None]).astype(jnp.int32), axis=1)
    scalars = jnp.concatenate([me_group[None], first[::block] // block]).astype(jnp.int32)
    first = first.reshape(blocks, block)

    mixed, lse = attend(joined, first, lines, scalars, block, per_slot, ffn_slots[1:])

    ffn_pieces, first_hops, second_hops = [], [], []
    for k in range(2):
        own = [rows[k * unit : (k + 1) * unit] for rows in ffn_slots]
        bits = net.bit_order(k)
        pieces = {0: jnp.stack(own, axis=0)}
        for at, b in enumerate(bits):
            away = {}
            for s, piece in pieces.items():
                if s == 0:
                    rest = net.from_wide(jnp.stack(own[1:], axis=0), 1 << b)
                    (first_hops if at == 0 else second_hops).append(rest)
                    away[1 << b] = jnp.concatenate([own_out[1 << b][None, k * unit : (k + 1) * unit], rest], axis=0)
                else:
                    away[s ^ (1 << b)] = net.from_wide(piece, 1 << b)
            pieces.update(away)
        ffn_pieces.append([pieces[s] for s in range(wide)])
    mixed = after(mixed, first_hops)

    attended_away = away_parts(lambda s: dot_nn(slot(mixed, s), w_out_full))
    attended = add_parts(dot_nn(slot(mixed, 0), w_out_full), attended_away)
    hidden_state = values_in + attended
    normed2, inverse2 = row_norm(hidden_state)
    a2_own = (normed2 * norm2_gain + norm2_shift).astype(bf16)
    a2_own = after(a2_own, second_hops)
    a2 = all_group(a2_own)

    w_up_t, w_down_full = (jnp.concatenate(pieces, axis=0).reshape(-1, width) for pieces in ffn_pieces)
    up = dot_nt(a2, w_up_t)
    gelu_value, gelu_pull = jax.vjp(jax.nn.gelu, up)
    active = gelu_value.astype(bf16)
    up_grad = gelu_pull(dot_nt(dy, w_down_full))[0].astype(bf16)
    normed2_part = [dot_nn(slot(up_grad, s), w_up_t).astype(bf16) for s in range(1, group)]
    normed2_away = [net.from_group(part, s + 1) for s, part in enumerate(normed2_part)]
    grad_down = dot_tn(active, dy).astype(bf16)
    up_grad = after(up_grad, grad_down, normed2_part)
    normed2_own = dot_nn(slot(up_grad, 0), w_up_t)

    def wide_sums(grad):
        value = grad.reshape(wide, ring, -1, width)
        return [
            WideSum(net, value[:, places[0] : places[-1] + 1], turn).send() for turn, places in enumerate(halves)
        ]

    def step(many, *others):
        for one in many:
            one.add(*others)
        for one in many:
            if one.bits:
                one.send()

    def arrive(value, *many):
        many = [one for one in many if one.sent]
        held = after([value] + [one.arrived for one in many])
        for one, arrived in zip(many, held[1:]):
            one.arrived = arrived
        return held[0]

    def ring_sum(many):
        return RingSum(net, [value[at] for value in (one.finish() for one in many) for at in range(value.shape[0])])

    down_sums = wide_sums(grad_down)

    normed2_grad = add_parts(normed2_own, after(normed2_away, grad_down))
    back2, grad_gain2, grad_shift2 = norm_backward(normed2_grad, normed2, inverse2, norm2_gain)
    state_grad = out_grad.astype(f32) + back2
    state_low = state_grad.astype(bf16)
    state_away = [net.from_group(state_low, s) for s in range(1, group)]
    grad_up = dot_tn(arrive(after(up_grad, state_low), *down_sums), a2).astype(bf16)
    state_away = after(state_away, grad_up)
    up_sums = wide_sums(grad_up)
    step(down_sums)
    state_whole = jnp.concatenate([state_low] + state_away, axis=0)
    mixed_grad = dot_nt(state_whole, w_out_full).astype(bf16)
    grad_out = dot_tn(mixed, state_whole).astype(bf16)

    def grads_of(begin, end, waits):
        return attend_back(
            joined, mixed, mixed_grad, first, lines, lse, scalars, block, per_slot, begin, end, waits
        )

    def attention_sums(grads, begin, end):
        grad_part = dot_tn(grads, a1).astype(bf16)
        grad_part = grad_part.reshape(end - begin, 3, per_pair, wide, piece_rows, width)
        result = []
        for r in range(begin * per_pair, end * per_pair):
            grad_qkv = grad_part[r // per_pair - begin, :, r % per_pair]
            grad_o = grad_out[r * head_rows : (r + 1) * head_rows].reshape(1, wide, piece_rows, width)
            value = jnp.moveaxis(jnp.concatenate([grad_qkv, grad_o], axis=0), 1, 0)
            result.append(WideSum(net, value, r % 2).send())
        return grad_part, result

    cut = pairs // 2
    grads, line_sums = grads_of(cut, pairs, [one.kept for one in down_sums])
    grads = arrive(grads, *down_sums, *up_sums)
    all_grads, all_lines = [grads], [line_sums]
    step(down_sums)
    step(up_sums)
    down_ring = ring_sum(down_sums).send()
    part, far_sums = attention_sums(grads, cut, pairs)
    near_sums, up_ring, far_ring = [], None, None
    for p in reversed(range(cut)):
        flying = up_sums + far_sums + near_sums + [down_ring]
        grads, line_sums = grads_of(p, p + 1, [part])
        grads = arrive(grads, *(flying + [ring for ring in (up_ring, far_ring) if ring is not None]))
        all_grads, all_lines = [grads] + all_grads, [line_sums] + all_lines
        if up_ring is None:
            step(up_sums)
            up_ring = ring_sum(up_sums).send()
            step(far_sums)
        elif far_ring is None:
            far_ring = RingSum(net, [None] * cut * per_pair + [one.finish() for one in far_sums]).send()
        if down_ring.sent:
            down_ring.add()
        if len(down_ring.values) > 1:
            down_ring.send()
        step(near_sums)
        part, sums = attention_sums(grads, p, p + 1)
        near_sums = sums + near_sums
    if far_ring is None:
        far_ring = RingSum(net, [None] * cut * per_pair + [one.finish() for one in far_sums]).send()
    w_late, active_late = after((w_joined, active), part)

    def normed1_part(s):
        total, at = None, 0
        for grads in all_grads:
            part = dot_nn(slot(grads, s), w_late[at : at + grads.shape[1]])
            total = part if total is None else total + part
            at += grads.shape[1]
        return total

    normed1_away = away_parts(normed1_part)
    normed1_own = normed1_part(0)

    normed1_grad = add_parts(normed1_own, normed1_away)
    back1, grad_gain1, grad_shift1 = norm_backward(normed1_grad, normed1, inverse1, norm1_gain)
    input_grad = state_grad + back1

    line_grad = jnp.concatenate(all_lines, axis=0)[:, block:]
    table_grad = jnp.dot(line_grad, one_hot, precision=lax.Precision.HIGHEST, preferred_element_type=f32)
    all_heads = heads_here * narrow
    head_ids = jnp.stack(
        [
            ((me_ring ^ r) * group + me_group) * heads_here + head_of(r, h)
            for r in range(ring)
            for h in range(heads_here)
        ]
    )
    placed = (jnp.arange(all_heads)[:, None] == head_ids[None, :]).astype(f32)
    table_all = jnp.dot(placed, table_grad, precision=lax.Precision.HIGHEST, preferred_element_type=f32)

    small = jnp.concatenate([grad_gain1, grad_shift1, grad_gain2, grad_shift2, table_all.reshape(-1)])
    pad = -small.shape[0] % 1024
    small = net.total(jnp.pad(small, (0, pad)).reshape(-1, 128)).reshape(-1)
    gain1, shift1, gain2, shift2 = (small[k * width : (k + 1) * width] for k in range(4))
    table_sum = small[4 * width : 4 * width + table_all.size].reshape(table_all.shape)
    table_out = lax.dynamic_slice_in_dim(table_sum, me_narrow * heads_here, heads_here, 0).T

    feed_away = away_parts(lambda s: dot_nn(slot(active_late, s), w_down_full))
    feed = add_parts(dot_nn(slot(active_late, 0), w_down_full), feed_away)
    out = (hidden_state + feed).astype(bf16)

    far_ring.values[: len(near_sums)] = [one.finish() for one in near_sums]
    ffn_part = jnp.concatenate([down_ring.finish(), up_ring.finish()], axis=0)
    ffn_all = net.share(ffn_part)
    down_all = jnp.concatenate([part[:unit] for part in ffn_all], axis=0).astype(f32)
    up_all = jnp.concatenate([part[unit:] for part in ffn_all], axis=0).T.astype(f32)
    attention_all = net.share(far_ring.finish())
    attention_all = jnp.concatenate(attention_all, axis=1).astype(f32)
    return (
        out,
        input_grad,
        gain1,
        shift1,
        attention_all[0],
        attention_all[1],
        attention_all[2],
        attention_all[3],
        gain2,
        shift2,
        up_all,
        down_all,
        table_out,
    )


def _xor_rows(matrix, me, count):
    rows = matrix.shape[0] // count
    return [lax.dynamic_slice_in_dim(matrix, (me ^ s) * rows, rows, 0) for s in range(count)]


def solution(mesh):
    placed = (
        P(("wide", "narrow"), None),
        P("wide", None),
        P(),
        P(),
        P(),
        P("narrow", None),
        P("narrow", None),
        P("narrow", None),
        P("narrow", None),
        P(),
        P(),
        P(None, "narrow"),
        P("narrow", None),
        P(None, "narrow"),
        P(("wide", "narrow"), None),
    )
    return jax.shard_map(
        functools.partial(on_device, wide=mesh.shape["wide"], narrow=mesh.shape["narrow"]),
        mesh=mesh,
        in_specs=placed,
        out_specs=(
            P(("wide", "narrow"), None),
            P(("wide", "narrow"), None),
            P(),
            P(),
            P("narrow", None),
            P("narrow", None),
            P("narrow", None),
            P("narrow", None),
            P(),
            P(),
            P(None, "narrow"),
            P("narrow", None),
            P(None, "narrow"),
        ),
        check_vma=False,
    )
```

time: 732 us -> 590 us (0.81)
  starting transfers between devices: 193 us -> 85.7 us
  waiting for transfers between devices: 140 us -> 103 us
  Pallas kernels: 131 us -> 101 us
  other arithmetic: 45.4 us -> 61 us
  matrix products: 146 us -> 161 us
    ppermute x36 -> x24, starting transfers between devices: 93.9 us -> 36.8 us  [from_group(): lax.ppermute(value, 'narrow', [(i, i ^ s) for i in range(self.narrow)])]
    ppermute x42 -> x37, starting transfers between devices: 99.2 us -> 48.9 us  [from_wide(): return lax.ppermute(value, 'wide', [(i, i ^ s) for i in range(self.wide)])]
    ppermute x42 -> x37, waiting for transfers between devices: 107 us -> 72.6 us  [from_wide(): return lax.ppermute(value, 'wide', [(i, i ^ s) for i in range(self.wide)])]
    pallas_call x2 -> x17, Pallas kernels: 131 us -> 101 us  [the longest x3 76.3 us: attend_back(): pl.pallas_call(ignoring(functools.partial(attend_back_kernel, block=block...]
    convert_element_type x20 -> x26, other arithmetic: 18.5 us -> 33.2 us  [the longest x17 22 us: add_low(): (kept.astype(jnp.float32) + arrived.astype(jnp.float32)).astype(jnp.bfloa...]
    slice x9 -> x16, local copies, waits for them, and re-layouts: 2.49 us -> 14.1 us  [the longest x4 3.7 us: send(): lax.index_in_dim(self.value, 1, axis, keepdims=False)]
    squeeze x6 -> x15, local copies, waits for them, and re-layouts: 0.95 us -> 10.4 us  [the longest x12 6.48 us: send(): lax.index_in_dim(self.value, 1, axis, keepdims=False)]
    unnamed x213 -> x209, local copies, waits for them, and re-layouts: 41.3 us -> 33.3 us
  transfers between devices with their start and end apart: 78 -> 61, of which waited for: 27 -> 18; matrix products, arithmetic and copies ran while one was open for 22% -> 37% of each run, Pallas kernels for 9% -> 17%
where the time goes in v2:
time: 590 us; the launch traced here: 583 us
  matrix products  161 us (27%)
  waiting for transfers between devices  103 us (17%)
  Pallas kernels  101 us (17%)
  starting transfers between devices  85.7 us (15%)
  local copies, waits for them, and re-layouts  69.4 us (12%)
  other arithmetic  61 us (10%)
    pallas_call x3, Pallas kernels, attend_back(): pl.pallas_call(ignoring(functools.partial(attend_back_kernel, block=block...  76.3 us
    ppermute x37, waiting for transfers between devices, from_wide(): return lax.ppermute(value, 'wide', [(i, i ^ s) for i in range(self.wide)])  72.6 us
    dot_general x4, matrix products, dot_nt(): return lax.dot_general(left, right, NT, preferred_element_type=jnp.float32)  57.6 us
    dot_general x12, matrix products, dot_nn(): return jnp.dot(left, right, preferred_element_type=jnp.float32)  56.6 us
    ppermute x37, starting transfers between devices, from_wide(): return lax.ppermute(value, 'wide', [(i, i ^ s) for i in range(self.wide)])  48.9 us
    dot_general x6, matrix products, dot_tn(): return lax.dot_general(left, right, TN, preferred_element_type=jnp.float32)  45.8 us
    ppermute x24, starting transfers between devices, from_group(): lax.ppermute(value, 'narrow', [(i, i ^ s) for i in range(self.narrow)])  36.8 us
    unnamed x209, local copies, waits for them, and re-layouts  33.3 us
  transfers between devices with their start and end apart: 61, of which 18 were waited for; matrix products, arithmetic and copies ran while one was open for 37% of the time, Pallas kernels for 17%

profile of v2, /device:TPU:0, one launch (start us, length us, event | category | flops | bytes accessed | tf_op | source)
XLA Modules:
  0.0 582.8 jit_solution(7405801193253984653)
XLA Ops:
  38.3 9.5 %collective-permute-done.6 = bf16[1,2,4,32,1024]{4,3,2,1,0:T(8,128)(2,1)S(1)} collective-permute-done((bf16[1,2,4,32,1024]{4,3,2,1,0:T(8,128)(2,1)}, bf16[1,2,4,32,1024]{4,3,2,1,0:T(8,128)(2,1)S(1)}, u32[]{:S(2)}, u32[]{:S(2)}) %collective-permute-start.6) | collective-permute-done | bytes 524320 | tf_op jit(solution)/shard_map/ppermute | solution.py:339
  58.0 17.0 %collective-permute-done.7 = bf16[2,2,4,32,1024]{4,3,2,1,0:T(8,128)(2,1)} collective-permute-done((bf16[2,2,4,32,1024]{4,3,2,1,0:T(8,128)(2,1)}, bf16[2,2,4,32,1024]{4,3,2,1,0:T(8,128)(2,1)}, u32[]{:S(2)}, u32[]{:S(2)}) %collective-permute-start.7) | collective-permute-done | bytes 1048608 | tf_op jit(solution)/shard_map/ppermute | solution.py:339
  87.7 10.1 %multiply_convert_fusion.1.refs_1_ = bf16[2048,1536]{1,0:T(8,128)(2,1)S(1)} fusion(f32[1536]{0:T(1024)S(1)} %fusion.104, bf16[1024,1024]{1,0:T(8,128)(2,1)} %collective-permute-done.refs_4_, bf16[1024,1024]{1,0:T(8,128)(2,1)} %fusion.14, bf16[2048,1024]{1,0:T(8,128)(2,1)} %copy-done.2), kind=kOutput, calls=%fused_computation.11 | convolution fusion | flops 6457131008 | bytes 13637632 | tf_op jit(solution)/shard_map/dot_general | solution.py:40
  105.9 16.6 %collective-permute-done.11.refs_5_ = bf16[256,1024]{1,0:T(8,128)(2,1)S(1)} collective-permute-done((bf16[256,1024]{1,0:T(8,128)(2,1)}, bf16[256,1024]{1,0:T(8,128)(2,1)S(1)}, u32[]{:S(2)}, u32[]{:S(2)}) %collective-permute-start.11) | collective-permute-done | bytes 524320 | tf_op jit(solution)/shard_map/ppermute | solution.py:331
  128.6 24.0 %shard_map.248 = (bf16[2048,512]{1,0:T(8,128)(2,1)S(1)}, f32[8,8,256]{2,1,0:T(8,128)S(1)}) custom-call(s32[9]{0:T(128)S(1)} %pad_add_fusion.refs_0_, bf16[2048,1536]{1,0:T(8,128)(2,1)S(1)} %multiply_convert_fusion.1.refs_1_, s32[8,256]{1,0:T(8,128)S(1)} %reshape.259.refs_2_.refs_4_, f32[8,1536]{1,0:T(8,128)S(1)} %concatenate.75.refs_3_.refs_5_, ...), custom_call_target="tpu_custom_call" | custom-call | flops 20000000000 | bytes 8388608 | tf_op jit(solution)/shard_map/pallas_call | solution.py:275
  175.7 14.0 %collective-permute-done.19 = bf16[4,128,1024]{2,1,0:T(8,128)(2,1)S(1)} collective-permute-done((bf16[4,128,1024]{2,1,0:T(8,128)(2,1)S(1)}, bf16[4,128,1024]{2,1,0:T(8,128)(2,1)S(1)}, u32[]{:S(2)}, u32[]{:S(2)}) %collective-permute-start.19) | collective-permute-done | bytes 1048608 | tf_op jit(solution)/shard_map/ppermute | solution.py:339
  198.7 15.3 %fusion.131 = f32[2048,2048]{1,0:T(8,128)} fusion(bf16[2048,1024]{1,0:T(8,128)(2,1)} %copy-done.64, bf16[2048,1024]{1,0:T(8,128)(2,1)} %bitcast.331), kind=kOutput, calls=%fused_computation.332 | convolution fusion | flops 8589934592 | bytes 25165824 | tf_op jit(solution)/shard_map/dot_general | solution.py:40
  214.0 26.0 %fusion.6 = (bf16[2048,2048]{1,0:T(8,128)(2,1)}, bf16[2048,2048]{1,0:T(8,128)(2,1)}) fusion(f32[2048,2048]{1,0:T(8,128)} %fusion.131, bf16[2048,1024]{1,0:T(8,128)(2,1)S(1)} %bitcast.329, bf16[1024,1024]{1,0:T(8,128)(2,1)} %collective-permute-done.18, bf16[1024,1024]{1,0:T(8,128)(2,1)S(1)} %copy-done.30), kind=kOutput, calls=%fused_computation.8 | convolution fusion | flops 8690597888 | bytes 41943040 | tf_op jit(solution)/shard_map/dot_general | solution.py:40
  240.0 8.1 %fusion.38.refs_2_ = bf16[1024,1024]{1,0:T(8,128)(2,1)} fusion(bf16[2048,1024]{1,0:T(8,128)(2,1)S(1)} %bitcast.330, bf16[2048,2048]{1,0:T(8,128)(2,1)} %get-tuple-element.151.refs_0_), kind=kOutput, calls=%fused_computation.65 | convolution fusion | flops 4296015872 | bytes 10485760 | tf_op jit(solution)/shard_map/dot_general | solution.py:44
  248.7 11.1 %convolution_convert_fusion.1.refs_1_ = bf16[2048,1024]{1,0:T(8,128)(2,1)} fusion(bf16[2048,2048]{1,0:T(8,128)(2,1)S(1)} %copy-done.27, bf16[2048,1024]{1,0:T(8,128)(2,1)S(1)} %copy-done.65), kind=kOutput, calls=%fused_computation.51 | convolution fusion | flops 8592031744 | bytes 16777216 | tf_op jit(solution)/shard_map/dot_general | solution.py:48
  267.3 11.4 %multiply_reduce_fusion = (f32[1024]{0:T(1024)}, f32[1024]{0:T(1024)S(1)}, f32[1024]{0:T(1024)S(1)}, f32[1024]{0:T(1024)}, f32[1024,1024]{1,0:T(8,128)S(1)}) fusion(f32[1024,1024]{1,0:T(8,128)} %copy-done.18, f32[1024]{0:T(1024)S(1)} %add_rsqrt_fusion, f32[1024]{0:T(1024)S(1)} %broadcast_multiply_fusion.4, f32[1024]{0:T(1024)S(1)} %copy-done.84, ...), kind=kOutput, calls=%fused_computation.36 | convolution fusion | flops 4306497536 | bytes 18903040 | tf_op jit(solution)/shard_map/dot_general | solution.py:44
  282.3 8.2 %collective-permute-done.25.refs_2_ = bf16[2,2,128,1024]{3,2,1,0:T(8,128)(2,1)} collective-permute-done((bf16[2,2,128,1024]{3,2,1,0:T(8,128)(2,1)}, bf16[2,2,128,1024]{3,2,1,0:T(8,128)(2,1)}, u32[]{:S(2)}, u32[]{:S(2)}) %collective-permute-start.25) | collective-permute-done | bytes 1048608 | tf_op jit(solution)/shard_map/ppermute | solution.py:339
  290.9 13.1 %convolution_convert_fusion.refs_1_ = bf16[2048,1024]{1,0:T(8,128)(2,1)S(1)} fusion(bf16[2048,2048]{1,0:T(8,128)(2,1)} %get-tuple-element.44, bf16[1024,1024]{1,0:T(8,128)(2,1)} %collective-permute-done.18, bf16[1024,1024]{1,0:T(8,128)(2,1)} %shard_map.250), kind=kOutput, calls=%fused_computation.50 | convolution fusion | flops 8600420352 | bytes 16777216 | tf_op jit(solution)/shard_map/dot_general | solution.py:48
  317.0 6.2 %convolution_convert_fusion.2.refs_3_ = bf16[2048,512]{1,0:T(8,128)(2,1)} fusion(bf16[1024,1024]{1,0:T(8,128)(2,1)} %shard_map.255, bf16[1024,1024]{1,0:T(8,128)(2,1)} %get-tuple-element.147.refs_1_, bf16[2048,1024]{1,0:T(8,128)(2,1)} %copy-done.2), kind=kOutput, calls=%fused_computation.54 | convolution fusion | flops 2156920832 | bytes 7340032 | tf_op jit(solution)/shard_map/dot_general | solution.py:40
  323.2 34.2 %shard_map.256 = (bf16[2048,768]{1,0:T(8,128)(2,1)}, f32[4,1536]{1,0:T(4,128)S(1)}) custom-call(s32[9]{0:T(128)S(1)} %copy-done.13, bf16[2048,1536]{1,0:T(8,128)(2,1)} %copy-done.14, bf16[2048,512]{1,0:T(8,128)(2,1)} %shard_map.249.refs_2_, bf16[2048,512]{1,0:T(8,128)(2,1)} %convolution_convert_fusion.2.refs_3_, s32[8,256]{1,0:T(8,128)S(1)} %copy-done.11, ...), custom_call_target="tpu_custom_call" | custom-call | flops 20000000000 | bytes 10485760 | tf_op jit(solution)/shard_map/pallas_call | solution.py:306
  364.6 14.1 %collective-permute-start.34 = (bf16[2,128,1024]{2,1,0:T(8,128)(2,1)S(1)}, bf16[2,128,1024]{2,1,0:T(8,128)(2,1)S(1)}, u32[]{:S(2)}, u32[]{:S(2)}) collective-permute-start(bf16[2,128,1024]{2,1,0:T(8,128)(2,1)S(1)} %add_convert_fusion.8), channel_id=1, source_target_pairs={{0,4},{1,5},{2,6},{3,7},{4,0},{5,1},{6,2},{7,3},{8,12},{9,13},{10,... | collective-permute-start | bytes 1572872 | tf_op jit(solution)/shard_map/ppermute | solution.py:331
  380.7 6.6 %convolution_convert_fusion.4 = bf16[768,1024]{1,0:T(8,128)(2,1)S(1)} fusion(bf16[2048,768]{1,0:T(8,128)(2,1)} %get-tuple-element.49, bf16[1024,1024]{1,0:T(8,128)(2,1)} %collective-permute-done.refs_4_, bf16[1024,1024]{1,0:T(8,128)(2,1)} %fusion.14), kind=kOutput, calls=%fused_computation.67 | convolution fusion | flops 3230400512 | bytes 8912896 | tf_op jit(solution)/shard_map/dot_general | solution.py:48
  397.2 20.4 %shard_map.258 = (bf16[2048,384]{1,0:T(8,128)(2,1)S(1)}, f32[2,1536]{1,0:T(2,128)S(1)}) custom-call(s32[9]{0:T(128)S(1)} %copy-done.13, bf16[2048,1536]{1,0:T(8,128)(2,1)} %copy-done.14, bf16[2048,512]{1,0:T(8,128)(2,1)} %shard_map.249.refs_2_, bf16[2048,512]{1,0:T(8,128)(2,1)} %convolution_convert_fusion.2.refs_3_, s32[8,256]{1,0:T(8,128)S(1)} %copy-done.11, ...), custom_call_target="tpu_custom_call" | custom-call | flops 10000000000 | bytes 5242880 | tf_op jit(solution)/shard_map/pallas_call | solution.py:306
  439.0 21.7 %shard_map.260 = (bf16[2048,384]{1,0:T(8,128)(2,1)}, f32[2,1536]{1,0:T(2,128)S(1)}) custom-call(s32[9]{0:T(128)S(1)} %copy-done.13, bf16[2048,1536]{1,0:T(8,128)(2,1)} %copy-done.14, bf16[2048,512]{1,0:T(8,128)(2,1)} %shard_map.249.refs_2_, bf16[2048,512]{1,0:T(8,128)(2,1)} %convolution_convert_fusion.2.refs_3_, s32[8,256]{1,0:T(8,128)S(1)} %copy-done.11, ...), custom_call_target="tpu_custom_call" | custom-call | flops 10000000000 | bytes 5242880 | tf_op jit(solution)/shard_map/pallas_call | solution.py:306
  464.3 5.4 convolution_convert_fusion.5
  491.7 5.9 %fusion.35 = bf16[1024,1024]{1,0:T(8,128)(2,1)} fusion(bf16[2048,1024]{1,0:T(8,128)(2,1)S(1)} %bitcast.332, bf16[2048,2048]{1,0:T(8,128)(2,1)S(1)} %bitcast.295), kind=kOutput, calls=%fused_computation.64 | convolution fusion | flops 4296015872 | bytes 10485760 | tf_op jit(solution)/shard_map/dot_general | solution.py:44
  511.3 13.4 %collective-permute-done.49 = bf16[2,4,32,1024]{3,2,1,0:T(8,128)(2,1)S(1)} collective-permute-done((bf16[2,4,32,1024]{3,2,1,0:T(8,128)(2,1)S(1)}, bf16[2,4,32,1024]{3,2,1,0:T(8,128)(2,1)S(1)}, u32[]{:S(2)}, u32[]{:S(2)}) %collective-permute-start.49) | collective-permute-done | bytes 524320 | tf_op jit(solution)/shard_map/ppermute | solution.py:339
  552.9 6.2 %fusion.19 = (f32[1024]{0:T(1024)S(1)}, f32[1024]{0:T(1024)S(1)}, f32[1024]{0:T(1024)S(1)}, f32[1024]{0:T(1024)S(1)}, f32[1024,1024]{1,0:T(8,128)S(1)}) fusion(bf16[1024,1024]{1,0:T(8,128)(2,1)S(1)} %copy-done.17, f32[1024]{0:T(1024)S(1)} %copy-done.76, f32[1024]{0:T(1024)S(1)} %copy-done.74, f32[1024]{0:T(1024)S(1)} %copy-done.78, ...), kind=kLoop, calls=%fused_computation.27 | loop fusion | flops 14675968 | bytes 21000192 | tf_op jit(solution)/shard_map/reduce_sum | solution.py:36
  559.8 7.2 %add_convert_fusion.1 = bf16[1024,1024]{1,0:T(8,128)(2,1)} fusion(f32[1024,1024]{1,0:T(8,128)S(1)} %copy-done.20, bf16[1024,1024]{1,0:T(8,128)(2,1)} %collective-permute-done.40, bf16[2048,1024]{1,0:T(8,128)(2,1)S(1)} %bitcast.333, bf16[2048,2048]{1,0:T(8,128)(2,1)S(1)} %bitcast.297), kind=kOutput, calls=%fused_computation.39 | convolution fusion | flops 4299161600 | bytes 16777216 | tf_op jit(solution)/shard_map/dot_general | solution.py:44
  (495 shorter events, 254.5 us)
Async XLA Ops:
  3.5 31.2 %collective-permute-start.1 = (bf16[144,1024]{1,0:T(8,128)(2,1)}, bf16[144,1024]{1,0:T(8,128)(2,1)S(1)}, u32[]{:S(2)}, u32[]{:S(2)}) collective-permute-start(bf16[144,1024]{1,0:T(8,128)(2,1)} %pad_maximum_fusion.22), channel_id=1, source_target_pairs={{0,2},{1,3},{2,0},{3,1},{4,6},{5,7},{6,4},{7,5},{8,10},{9,11},{10,... | collective-permute-start | bytes 884744 | tf_op jit(solution)/shard_map/ppermute | solution.py:331
  12.8 42.4 %collective-permute-start.8 = (bf16[256,1024]{1,0:T(8,128)(2,1)}, bf16[256,1024]{1,0:T(8,128)(2,1)}, u32[]{:S(2)}, u32[]{:S(2)}) collective-permute-start(bf16[256,1024]{1,0:T(8,128)(2,1)} %pad_maximum_fusion.19.refs_0_), channel_id=1, source_target_pairs={{0,8},{8,0},{16,24},{24,16},{1,9},{9,1},{17,25},{25,17},{2,10},{10... | collective-permute-start | bytes 1572872 | tf_op jit(solution)/shard_map/ppermute | solution.py:339
  14.5 42.5 %collective-permute-start.9 = (bf16[256,1024]{1,0:T(8,128)(2,1)}, bf16[256,1024]{1,0:T(8,128)(2,1)}, u32[]{:S(2)}, u32[]{:S(2)}) collective-permute-start(bf16[256,1024]{1,0:T(8,128)(2,1)} %pad_maximum_fusion.19.refs_0_), channel_id=1, source_target_pairs={{0,16},{8,24},{16,0},{24,8},{1,17},{9,25},{17,1},{25,9},{2,18},{10... | collective-permute-start | bytes 1572872 | tf_op jit(solution)/shard_map/ppermute | solution.py:339
  30.4 52.9 %collective-permute-start = (bf16[1024,1024]{1,0:T(8,128)(2,1)}, bf16[1024,1024]{1,0:T(8,128)(2,1)}, u32[]{:S(2)}, u32[]{:S(2)}) collective-permute-start(bf16[1024,1024]{1,0:T(8,128)(2,1)} %fusion.14), channel_id=1, source_target_pairs={{0,1},{1,0},{2,3},{3,2},{4,5},{5,4},{6,7},{7,6},{8,9},{9,8},{10,11... | collective-permute-start | bytes 6291464 | tf_op jit(solution)/shard_map/ppermute | solution.py:331
  55.3 45.3 %collective-permute-start.20 = (bf16[1024,1024]{1,0:T(8,128)(2,1)}, bf16[1024,1024]{1,0:T(8,128)(2,1)}, u32[]{:S(2)}, u32[]{:S(2)}) collective-permute-start(bf16[1024,1024]{1,0:T(8,128)(2,1)} %param.29), channel_id=1, source_target_pairs={{0,1},{1,0},{2,3},{3,2},{4,5},{5,4},{6,7},{7,6},{8,9},{9,8},{10,11... | collective-permute-start | bytes 6291464 | tf_op jit(solution)/shard_map/ppermute | solution.py:331
  84.1 38.4 %collective-permute-start.11 = (bf16[256,1024]{1,0:T(8,128)(2,1)}, bf16[256,1024]{1,0:T(8,128)(2,1)S(1)}, u32[]{:S(2)}, u32[]{:S(2)}) collective-permute-start(bf16[256,1024]{1,0:T(8,128)(2,1)} %shard_map.247), channel_id=1, source_target_pairs={{0,4},{1,5},{2,6},{3,7},{4,0},{5,1},{6,2},{7,3},{8,12},{9,13},{10,... | collective-permute-start | bytes 1572872 | tf_op jit(solution)/shard_map/ppermute | solution.py:331
  86.3 36.2 %collective-permute-start.12 = (bf16[256,1024]{1,0:T(8,128)(2,1)}, bf16[256,1024]{1,0:T(8,128)(2,1)S(1)}, u32[]{:S(2)}, u32[]{:S(2)}) collective-permute-start(bf16[256,1024]{1,0:T(8,128)(2,1)} %shard_map.247), channel_id=1, source_target_pairs={{0,6},{1,7},{2,4},{3,5},{4,2},{5,3},{6,0},{7,1},{8,14},{9,15},{10,... | collective-permute-start | bytes 1572872 | tf_op jit(solution)/shard_map/ppermute | solution.py:331
  123.6 30.4 %collective-permute-start.14 = (bf16[3,128,1024]{2,1,0:T(8,128)(2,1)}, bf16[3,128,1024]{2,1,0:T(8,128)(2,1)S(1)}, u32[]{:S(2)}, u32[]{:S(2)}) collective-permute-start(bf16[3,128,1024]{2,1,0:T(8,128)(2,1)} %pad_maximum_fusion.16), channel_id=1, source_target_pairs={{0,16},{8,24},{16,0},{24,8},{1,17},{9,25},{17,1},{25,9},{2,18},{10... | collective-permute-start | bytes 2359304 | tf_op jit(solution)/shard_map/ppermute | solution.py:339
  125.1 44.5 %collective-permute-start.17 = (bf16[3,128,1024]{2,1,0:T(8,128)(2,1)}, bf16[3,128,1024]{2,1,0:T(8,128)(2,1)}, u32[]{:S(2)}, u32[]{:S(2)}) collective-permute-start(bf16[3,128,1024]{2,1,0:T(8,128)(2,1)} %pad_maximum_fusion.16), channel_id=1, source_target_pairs={{0,8},{8,0},{16,24},{24,16},{1,9},{9,1},{17,25},{25,17},{2,10},{10... | collective-permute-start | bytes 2359304 | tf_op jit(solution)/shard_map/ppermute | solution.py:339
  128.1 46.4 %collective-permute-start.16 = (bf16[3,128,1024]{2,1,0:T(8,128)(2,1)}, bf16[3,128,1024]{2,1,0:T(8,128)(2,1)}, u32[]{:S(2)}, u32[]{:S(2)}) collective-permute-start(bf16[3,128,1024]{2,1,0:T(8,128)(2,1)} %pad_maximum_fusion.15), channel_id=1, source_target_pairs={{0,16},{8,24},{16,0},{24,8},{1,17},{9,25},{17,1},{25,9},{2,18},{10... | collective-permute-start | bytes 2359304 | tf_op jit(solution)/shard_map/ppermute | solution.py:339
  158.1 31.7 %collective-permute-start.15 = (bf16[1024,1024]{1,0:T(8,128)(2,1)S(1)}, bf16[1024,1024]{1,0:T(8,128)(2,1)S(1)}, u32[]{:S(2)}, u32[]{:S(2)}) collective-permute-start(bf16[1024,1024]{1,0:T(8,128)(2,1)S(1)} %convolution_convert_fusion.3), channel_id=1, source_target_pairs={{0,1},{1,0},{2,3},{3,2},{4,5},{5,4},{6,7},{7,6},{8,9},{9,8},{10,11... | collective-permute-start | bytes 6291464 | tf_op jit(solution)/shard_map/ppermute | solution.py:331
  167.8 29.8 %collective-permute-start.21 = (bf16[4,128,1024]{2,1,0:T(8,128)(2,1)S(1)}, bf16[4,128,1024]{2,1,0:T(8,128)(2,1)S(1)}, u32[]{:S(2)}, u32[]{:S(2)}) collective-permute-start(bf16[4,128,1024]{2,1,0:T(8,128)(2,1)S(1)} %pad_maximum_fusion.12), channel_id=1, source_target_pairs={{0,8},{8,0},{16,24},{24,16},{1,9},{9,1},{17,25},{25,17},{2,10},{10... | collective-permute-start | bytes 3145736 | tf_op jit(solution)/shard_map/ppermute | solution.py:339
  282.3 34.7 %collective-permute-start.23 = (bf16[1024,1024]{1,0:T(8,128)(2,1)}, bf16[1024,1024]{1,0:T(8,128)(2,1)}, u32[]{:S(2)}, u32[]{:S(2)}) collective-permute-start(bf16[1024,1024]{1,0:T(8,128)(2,1)} %get-tuple-element.147.refs_1_), channel_id=1, source_target_pairs={{0,1},{1,0},{2,3},{3,2},{4,5},{5,4},{6,7},{7,6},{8,9},{9,8},{10,11... | collective-permute-start | bytes 6291464 | tf_op jit(solution)/shard_map/ppermute | solution.py:331
  309.0 53.4 %collective-permute-start.27 = (bf16[2,128,1024]{2,1,0:T(8,128)(2,1)}, bf16[2,128,1024]{2,1,0:T(8,128)(2,1)S(1)}, u32[]{:S(2)}, u32[]{:S(2)}) collective-permute-start(bf16[2,128,1024]{2,1,0:T(8,128)(2,1)} %get-tuple-element.171), channel_id=1, source_target_pairs={{0,16},{8,24},{16,0},{24,8},{1,17},{9,25},{17,1},{25,9},{2,18},{10... | collective-permute-start | bytes 1572872 | tf_op jit(solution)/shard_map/ppermute | solution.py:339
  313.3 49.1 %collective-permute-start.26 = (bf16[2,128,1024]{2,1,0:T(8,128)(2,1)}, bf16[2,128,1024]{2,1,0:T(8,128)(2,1)}, u32[]{:S(2)}, u32[]{:S(2)}) collective-permute-start(bf16[2,128,1024]{2,1,0:T(8,128)(2,1)} %get-tuple-element.173), channel_id=1, source_target_pairs={{0,8},{8,0},{16,24},{24,16},{1,9},{9,1},{17,25},{25,17},{2,10},{10... | collective-permute-start | bytes 1572872 | tf_op jit(solution)/shard_map/ppermute | solution.py:339
  315.9 46.5 %collective-permute-start.29 = (bf16[2,2,128,1024]{3,2,1,0:T(8,128)(2,1)}, bf16[2,2,128,1024]{3,2,1,0:T(8,128)(2,1)}, u32[]{:S(2)}, u32[]{:S(2)}) collective-permute-start(bf16[2,2,128,1024]{3,2,1,0:T(8,128)(2,1)} %slice_bitcast_fusion.1), channel_id=1, source_target_pairs={{0,8},{8,0},{16,24},{24,16},{1,9},{9,1},{17,25},{25,17},{2,10},{10... | collective-permute-start | bytes 3145736 | tf_op jit(solution)/shard_map/ppermute | solution.py:339
  316.4 46.0 %collective-permute-start.28 = (bf16[2,2,128,1024]{3,2,1,0:T(8,128)(2,1)}, bf16[2,2,128,1024]{3,2,1,0:T(8,128)(2,1)}, u32[]{:S(2)}, u32[]{:S(2)}) collective-permute-start(bf16[2,2,128,1024]{3,2,1,0:T(8,128)(2,1)} %slice.533), channel_id=1, source_target_pairs={{0,16},{8,24},{16,0},{24,8},{1,17},{9,25},{17,1},{25,9},{2,18},{10... | collective-permute-start | bytes 3145736 | tf_op jit(solution)/shard_map/ppermute | solution.py:339
  364.6 55.4 %collective-permute-start.34 = (bf16[2,128,1024]{2,1,0:T(8,128)(2,1)S(1)}, bf16[2,128,1024]{2,1,0:T(8,128)(2,1)S(1)}, u32[]{:S(2)}, u32[]{:S(2)}) collective-permute-start(bf16[2,128,1024]{2,1,0:T(8,128)(2,1)S(1)} %add_convert_fusion.8), channel_id=1, source_target_pairs={{0,4},{1,5},{2,6},{3,7},{4,0},{5,1},{6,2},{7,3},{8,12},{9,13},{10,... | collective-permute-start | bytes 1572872 | tf_op jit(solution)/shard_map/ppermute | solution.py:331
  387.7 32.4 %collective-permute-start.33 = (bf16[2,4,32,1024]{3,2,1,0:T(8,128)(2,1)S(1)}, bf16[2,4,32,1024]{3,2,1,0:T(8,128)(2,1)S(1)}, u32[]{:S(2)}, u32[]{:S(2)}) collective-permute-start(bf16[2,4,32,1024]{3,2,1,0:T(8,128)(2,1)S(1)} %slice_bitcast_fusion.13), channel_id=1, source_target_pairs={{0,8},{8,0},{16,24},{24,16},{1,9},{9,1},{17,25},{25,17},{2,10},{10... | collective-permute-start | bytes 1572872 | tf_op jit(solution)/shard_map/ppermute | solution.py:339
  390.2 29.9 %collective-permute-start.32 = (bf16[2,4,32,1024]{3,2,1,0:T(8,128)(2,1)S(1)}, bf16[2,4,32,1024]{3,2,1,0:T(8,128)(2,1)S(1)}, u32[]{:S(2)}, u32[]{:S(2)}) collective-permute-start(bf16[2,4,32,1024]{3,2,1,0:T(8,128)(2,1)S(1)} %slice.542), channel_id=1, source_target_pairs={{0,16},{8,24},{16,0},{24,8},{1,17},{9,25},{17,1},{25,9},{2,18},{10... | collective-permute-start | bytes 1572872 | tf_op jit(solution)/shard_map/ppermute | solution.py:339
  423.8 39.6 %collective-permute-start.39 = (bf16[2,128,1024]{2,1,0:T(8,128)(2,1)}, bf16[2,128,1024]{2,1,0:T(8,128)(2,1)}, u32[]{:S(2)}, u32[]{:S(2)}) collective-permute-start(bf16[2,128,1024]{2,1,0:T(8,128)(2,1)} %fusion.56), channel_id=1, source_target_pairs={{0,4},{1,5},{2,6},{3,7},{4,0},{5,1},{6,2},{7,3},{8,12},{9,13},{10,... | collective-permute-start | bytes 1572872 | tf_op jit(solution)/shard_map/ppermute | solution.py:331
  427.5 35.9 %collective-permute-start.38 = (bf16[1,128,1024]{2,1,0:T(8,128)(2,1)}, bf16[1,128,1024]{2,1,0:T(8,128)(2,1)}, u32[]{:S(2)}, u32[]{:S(2)}) collective-permute-start(bf16[1,128,1024]{2,1,0:T(8,128)(2,1)} %add_convert_fusion.14), channel_id=1, source_target_pairs={{0,2},{1,3},{2,0},{3,1},{4,6},{5,7},{6,4},{7,5},{8,10},{9,11},{10,... | collective-permute-start | bytes 786440 | tf_op jit(solution)/shard_map/ppermute | solution.py:331
  433.1 30.3 %collective-permute-start.37 = (bf16[2,4,32,1024]{3,2,1,0:T(8,128)(2,1)}, bf16[2,4,32,1024]{3,2,1,0:T(8,128)(2,1)S(1)}, u32[]{:S(2)}, u32[]{:S(2)}) collective-permute-start(bf16[2,4,32,1024]{3,2,1,0:T(8,128)(2,1)} %slice_bitcast_fusion.11), channel_id=1, source_target_pairs={{0,8},{8,0},{16,24},{24,16},{1,9},{9,1},{17,25},{25,17},{2,10},{10... | collective-permute-start | bytes 1572872 | tf_op jit(solution)/shard_map/ppermute | solution.py:339
  503.3 29.2 %collective-permute-start.58 = (bf16[256,1024]{1,0:T(8,128)(2,1)S(1)}, bf16[256,1024]{1,0:T(8,128)(2,1)S(1)}, u32[]{:S(2)}, u32[]{:S(2)}) collective-permute-start(bf16[256,1024]{1,0:T(8,128)(2,1)S(1)} %pad_maximum_fusion.21), channel_id=1, source_target_pairs={{0,24},{8,16},{16,8},{24,0},{1,25},{9,17},{17,9},{25,1},{2,26},{10... | collective-permute-start | bytes 1572872 | tf_op jit(solution)/shard_map/ppermute | solution.py:339
  (133 other events, 1760.2 us)

commit v3 on v2

v3 whole, which is shorter than its diff:
```python
import functools

import jax
import jax.numpy as jnp
from jax import lax
from jax.experimental import pallas as pl
from jax.experimental.pallas import tpu as pltpu
from jax.sharding import PartitionSpec as P

HD = 64
PAIR = 128
REACH = 1024
EPSILON = 1e-05
MASKED_SCORE = -1e30
ROOT = (2.0 / 3.141592653589793) ** 0.5
VMEM = 60 * 1024 * 1024
LIGHT = pl.CostEstimate(flops=1, bytes_accessed=1, transcendentals=0)
NT = (((1,), (1,)), ((), ()))
TN = (((0,), (0,)), ((), ()))


def row_norm(values):
    mean = jnp.mean(values, axis=1, keepdims=True)
    centred = values - mean
    spread = jnp.mean(centred * centred, axis=1, keepdims=True)
    inverse = lax.rsqrt(spread + EPSILON)
    return (centred * inverse, inverse)


def norm_backward(upstream, normed, inverse, gain):
    scaled = upstream * gain
    mean_plain = jnp.mean(scaled, axis=1, keepdims=True)
    mean_cross = jnp.mean(scaled * normed, axis=1, keepdims=True)
    result = inverse * (scaled - mean_plain - normed * mean_cross)
    return (result, jnp.sum(upstream * normed, axis=0), jnp.sum(upstream, axis=0))


def dot_nt(left, right):
    return lax.dot_general(left, right, NT, preferred_element_type=jnp.float32)


def dot_nn(left, right):
    return jnp.dot(left, right, preferred_element_type=jnp.float32)


def dot_tn(left, right):
    return lax.dot_general(left, right, TN, preferred_element_type=jnp.float32)


def make_strip(line_ref, strips, begin=0):
    for h in range(strips.shape[0]):
        spread = jnp.broadcast_to(line_ref[begin + h : begin + h + 1, :], strips.shape[1:])
        strips[h] = pltpu.roll(spread, 0, 1, stride=1, stride_axis=0)


def strip_line(strip):
    rows, span = strip.shape
    while rows > 1:
        rows //= 2
        strip = strip[:rows] + pltpu.roll(strip[rows : 2 * rows], span - rows, 1)
    return strip


def strip_at(t, u, rows, block):
    return pl.ds(pl.multiple_of(t * block + (block - u * rows), rows), block)


def strip_tile(strips, h, t, block):
    rows = strips.shape[1]
    parts = [strips[h, :, strip_at(t, u, rows, block)] for u in range(block // rows)]
    return jnp.concatenate(parts, axis=0)


def add_to_strip(strips, h, t, tile):
    rows, block = strips.shape[1], tile.shape[0]
    for u in range(block // rows):
        strips[h, :, strip_at(t, u, rows, block)] += tile[u * rows : (u + 1) * rows]


def place_of(index, me, per_slot):
    return ((index // per_slot) ^ me) * per_slot + index % per_slot


def head_lanes(block, h):
    lanes = lax.broadcasted_iota(jnp.int32, block.shape, 1)
    return jnp.where((lanes // HD) == h, block, jnp.zeros_like(block))


def columns_of(p, kind):
    return slice((3 * p + kind) * PAIR, (3 * p + kind + 1) * PAIR)


def attend_kernel(scalars, x_ref, first_ref, line_ref, out_ref, lse_ref, strips, v_t, kept, *, block, per_slot):
    i = pl.program_id(0)
    me = scalars[0]
    low = scalars[1 + i]
    heads = strips.shape[0]
    pairs = heads // 2

    @pl.when(i == 0)
    def _():
        make_strip(line_ref, strips)
        for p in range(pairs):
            v_t[p * PAIR : (p + 1) * PAIR] = x_ref[:, columns_of(p, 2)].T

    rows = pl.ds(pl.multiple_of(place_of(i, me, per_slot) * block, block), block)
    own = [head_lanes(x_ref[rows, columns_of(h // 2, 0)], h % 2) for h in range(heads)]
    first = first_ref[pl.ds(i, 1), :]
    key_index = lax.broadcasted_iota(jnp.int32, (block, block), 0)

    def rows_of(t):
        return pl.ds(pl.multiple_of(place_of(i - t, me, per_slot) * block, block), block)

    def fold(value):
        return value.reshape(block // 8, 8, block)

    def score_step(t, tops):
        here = rows_of(t)
        allowed = key_index >= (first - (i - t) * block)
        result = []
        for h in range(heads):
            scores = dot_nt(x_ref[here, columns_of(h // 2, 1)], own[h]) + strip_tile(strips, h, t, block)
            scores = jnp.where(allowed, scores, MASKED_SCORE)
            kept[h, t] = scores
            result.append(jnp.maximum(tops[h], jnp.max(fold(scores), axis=0)))
        return tuple(result)

    def value_step(t, carry):
        here = rows_of(t)
        result = []
        for h in range(heads):
            total, acc = carry[h]
            expo = jnp.exp(kept[h, t] - tops[h])
            total = total + jnp.sum(fold(expo), axis=0)
            acc = acc + dot_nn(v_t[h * HD : (h + 1) * HD, here], expo.astype(jnp.bfloat16))
            result.append((total, acc))
        return tuple(result)

    tops = lax.fori_loop(
        0, i - low + 1, score_step, (jnp.full((8, block), MASKED_SCORE, jnp.float32),) * heads
    )
    tops = [jnp.max(top, axis=0, keepdims=True) for top in tops]
    zero = (jnp.zeros((8, block), jnp.float32), jnp.zeros((HD, block), jnp.float32))
    done = lax.fori_loop(0, i - low + 1, value_step, (zero,) * heads)
    totals = [jnp.sum(total, axis=0, keepdims=True) for total, _ in done]
    for p in range(pairs):
        both = jnp.concatenate([done[h][1] / totals[h] for h in (2 * p, 2 * p + 1)], axis=0)
        out_ref[rows, p * PAIR : (p + 1) * PAIR] = both.T.astype(jnp.bfloat16)
    lse_ref[pl.ds(i, 1)] = jnp.concatenate([tops[h] + jnp.log(totals[h]) for h in range(heads)], axis=0)[None]


def attend_back_kernel(
    scalars,
    x_ref,
    mixed_ref,
    up_ref,
    first_ref,
    line_ref,
    lse_ref,
    grad_ref,
    sums_ref,
    strips,
    sums,
    k_t,
    dk,
    dv,
    *,
    block,
    per_slot,
    begin,
):
    i = pl.program_id(0)
    me = scalars[0]
    low = scalars[1 + i]
    heads = strips.shape[0]
    pairs = heads // 2

    def columns(p, kind):
        return slice((3 * (p + begin) + kind) * PAIR, (3 * (p + begin) + kind + 1) * PAIR)

    def wide_columns(p):
        return slice((p + begin) * PAIR, (p + begin + 1) * PAIR)

    @pl.when(i == 0)
    def _():
        make_strip(line_ref, strips, 2 * begin)
        for p in range(pairs):
            k_t[p * PAIR : (p + 1) * PAIR] = x_ref[:, columns(p, 1)].T
        dk[...] = jnp.zeros_like(dk)
        dv[...] = jnp.zeros_like(dv)
        sums[...] = jnp.zeros_like(sums)

    rows = pl.ds(pl.multiple_of(place_of(i, me, per_slot) * block, block), block)
    own_q = [head_lanes(x_ref[rows, columns(h // 2, 0)], h % 2) for h in range(heads)]
    own_up = [head_lanes(up_ref[rows, wide_columns(h // 2)], h % 2) for h in range(heads)]
    picks = lax.broadcasted_iota(jnp.int32, (8, PAIR), 1) // HD == lax.broadcasted_iota(jnp.int32, (8, PAIR), 0)
    picks = picks.astype(jnp.bfloat16)
    deltas = []
    for p in range(pairs):
        span = wide_columns(p)
        product = up_ref[rows, span].astype(jnp.float32) * mixed_ref[rows, span].astype(jnp.float32)
        high = product.astype(jnp.bfloat16)
        rest = (product - high.astype(jnp.float32)).astype(jnp.bfloat16)
        both = dot_nt(picks, high) + dot_nt(picks, rest)
        deltas += [both[0:1], both[1:2]]
    first = first_ref[pl.ds(i, 1), :]
    key_index = lax.broadcasted_iota(jnp.int32, (block, block), 0)

    def step(t, carry):
        here = pl.ds(pl.multiple_of(place_of(i - t, me, per_slot) * block, block), block)
        allowed = key_index >= (first - (i - t) * block)
        dq = []
        for p in range(pairs):
            span = slice(p * PAIR, (p + 1) * PAIR)
            keys = x_ref[here, columns(p, 1)]
            values = x_ref[here, columns(p, 2)]
            dk_new = dk[here, span]
            dv_new = dv[here, span]
            for h in (2 * p, 2 * p + 1):
                scores = dot_nt(keys, own_q[h]) + strip_tile(strips, h, t, block)
                scores = jnp.where(allowed, scores, MASKED_SCORE)
                probs = jnp.exp(scores - lse_ref[i, 2 * begin + h : 2 * begin + h + 1, :])
                score_grad = probs * (dot_nt(values, own_up[h]) - deltas[h])
                add_to_strip(sums, h, t, score_grad)
                low_grad = score_grad.astype(jnp.bfloat16)
                dv_new = dv_new + dot_nn(probs.astype(jnp.bfloat16), own_up[h])
                dk_new = dk_new + dot_nn(low_grad, own_q[h])
                dq.append(carry[h] + dot_nn(k_t[h * HD : (h + 1) * HD, here], low_grad))
            dk[here, span] = dk_new
            dv[here, span] = dv_new
        return tuple(dq)

    dq = lax.fori_loop(0, i - low + 1, step, (jnp.zeros((HD, block), jnp.float32),) * heads)
    for p in range(pairs):
        both = jnp.concatenate(dq[2 * p : 2 * p + 2], axis=0).T * (HD ** (-0.5))
        grad_ref[rows, columns_of(p, 0)] = both.astype(jnp.bfloat16)

    @pl.when(i == pl.num_programs(0) - 1)
    def _():
        for p in range(pairs):
            span = slice(p * PAIR, (p + 1) * PAIR)
            grad_ref[:, columns_of(p, 1)] = dk[:, span].astype(jnp.bfloat16)
            grad_ref[:, columns_of(p, 2)] = dv[:, span].astype(jnp.bfloat16)
        for h in range(heads):
            sums_ref[h : h + 1, :] = strip_line(sums[h])


WHOLE = pl.BlockSpec(memory_space=pltpu.VMEM)
ANYWHERE = pl.BlockSpec(memory_space=pl.ANY)


def ignoring(kernel, first, count):
    def body(*refs):
        kernel(*refs[:first], *refs[first + count :])

    return body


def attend(joined, first, lines, scalars, block, per_slot, waits):
    length = joined.shape[0]
    heads, span = lines.shape
    blocks = length // block
    strip = pltpu.VMEM((heads, min(128, block), span), jnp.float32)
    grid_spec = pltpu.PrefetchScalarGridSpec(
        num_scalar_prefetch=1,
        grid=(blocks,),
        in_specs=[WHOLE] * 3 + [ANYWHERE] * len(waits),
        out_specs=[WHOLE] * 2,
        scratch_shapes=[
            strip,
            pltpu.VMEM((heads * HD, length), jnp.bfloat16),
            pltpu.VMEM((heads, span // block - 1, block, block), jnp.float32),
        ],
    )
    return pl.pallas_call(
        ignoring(functools.partial(attend_kernel, block=block, per_slot=per_slot), 4, len(waits)),
        grid_spec=grid_spec,
        out_shape=[
            jax.ShapeDtypeStruct((length, heads * HD), jnp.bfloat16),
            jax.ShapeDtypeStruct((blocks, heads, block), jnp.float32),
        ],
        compiler_params=pltpu.CompilerParams(vmem_limit_bytes=VMEM),
        cost_estimate=LIGHT,
    )(scalars, joined, first, lines, *waits)


def attend_back(joined, mixed, upstream, first, lines, lse, scalars, block, per_slot, begin, end, waits):
    length = joined.shape[0]
    span = lines.shape[1]
    heads = 2 * (end - begin)
    blocks = length // block
    strip = pltpu.VMEM((heads, min(128, block), span), jnp.float32)
    grid_spec = pltpu.PrefetchScalarGridSpec(
        num_scalar_prefetch=1,
        grid=(blocks,),
        in_specs=[WHOLE] * 6 + [ANYWHERE] * len(waits),
        out_specs=[WHOLE] * 2,
        scratch_shapes=[
            strip,
            strip,
            pltpu.VMEM((heads * HD, length), jnp.bfloat16),
            pltpu.VMEM((length, heads * HD), jnp.float32),
            pltpu.VMEM((length, heads * HD), jnp.float32),
        ],
    )
    return pl.pallas_call(
        ignoring(
            functools.partial(attend_back_kernel, block=block, per_slot=per_slot, begin=begin), 7, len(waits)
        ),
        grid_spec=grid_spec,
        out_shape=[
            jax.ShapeDtypeStruct((length, 3 * heads * HD), jnp.bfloat16),
            jax.ShapeDtypeStruct((heads, span), jnp.float32),
        ],
        compiler_params=pltpu.CompilerParams(vmem_limit_bytes=VMEM),
        cost_estimate=LIGHT,
    )(scalars, joined, mixed, upstream, first, lines, lse, *waits)


def hidden_kernel(*refs, slots, blocks, chunk):
    a2_refs, dy_refs = refs[:slots], refs[slots : 2 * slots]
    up_ref, down_ref, act_ref, up_grad_ref = refs[2 * slots : 2 * slots + 4]
    back_refs = refs[2 * slots + 4 :]
    for s in range(slots):

        @pl.when(pl.program_id(0) // blocks == s)
        def _(s=s):
            tokens = a2_refs[s][...]
            grads = dy_refs[s][...]
            total = jnp.zeros(tokens.shape, jnp.float32)
            for begin in range(0, up_ref.shape[0], chunk):
                rows = slice(begin, begin + chunk)
                x = dot_nt(tokens, up_ref[rows, :])
                square = x * x
                bend = jnp.tanh(x * (ROOT + ROOT * 0.044715 * square))
                half = 0.5 + 0.5 * bend
                act_ref[:, rows] = (x * half).astype(jnp.bfloat16)
                slope = half + 0.5 * x * (1.0 - bend * bend) * (ROOT + 3.0 * ROOT * 0.044715 * square)
                up_grad = (dot_nt(grads, down_ref[rows, :]) * slope).astype(jnp.bfloat16)
                up_grad_ref[:, rows] = up_grad
                total = total + dot_nn(up_grad, up_ref[rows, :])
            back_refs[s][...] = total.astype(jnp.bfloat16)


def hidden_units(a2, dy, w_up_t, w_down):
    tokens, width = a2[0].shape
    slots = len(a2)
    units = w_up_t.shape[0]
    block = min(256, tokens)
    blocks = tokens // block
    unit_block = pl.BlockSpec((block, units), lambda i: (i, 0))
    by_slot = [
        pl.BlockSpec((block, width), functools.partial(lambda i, s: (spot_in(i, s, blocks), 0), s=s))
        for s in range(slots)
    ]
    return pl.pallas_call(
        functools.partial(hidden_kernel, slots=slots, blocks=blocks, chunk=min(512, units)),
        grid=(slots * blocks,),
        in_specs=by_slot + by_slot + [WHOLE, WHOLE],
        out_specs=[unit_block, unit_block] + by_slot,
        out_shape=[jax.ShapeDtypeStruct((slots * tokens, units), jnp.bfloat16)] * 2
        + [jax.ShapeDtypeStruct((tokens, width), jnp.bfloat16)] * slots,
        compiler_params=pltpu.CompilerParams(vmem_limit_bytes=VMEM),
        cost_estimate=LIGHT,
    )(*a2, *dy, w_up_t, w_down)


def norm_back_kernel(*refs, parts):
    values_ref, add_ref, gain_ref = refs[:3]
    part_refs = refs[3 : 3 + parts]
    out_ref, low_ref, sums_ref = refs[3 + parts :]
    values = values_ref[...].astype(jnp.float32)
    normed, inverse = row_norm(values)
    upstream = part_refs[0][...].astype(jnp.float32)
    for ref in part_refs[1:]:
        upstream = upstream + ref[...].astype(jnp.float32)
    result, gain_grad, shift_grad = norm_backward(upstream, normed, inverse, gain_ref[...])
    result = result + add_ref[...].astype(jnp.float32)
    out_ref[...] = result
    low_ref[...] = result.astype(jnp.bfloat16)

    @pl.when(pl.program_id(0) == 0)
    def _():
        sums_ref[...] = jnp.zeros_like(sums_ref)

    sums_ref[0:1, :] += gain_grad[None]
    sums_ref[1:2, :] += shift_grad[None]


def norm_back(values, add, gain, parts, waits=()):
    tokens, width = values.shape
    block = min(256, tokens)
    rows = pl.BlockSpec((block, width), lambda i: (i, 0))
    result, low, sums = pl.pallas_call(
        ignoring(functools.partial(norm_back_kernel, parts=len(parts)), 3 + len(parts), len(waits)),
        grid=(tokens // block,),
        in_specs=[rows, rows, pl.BlockSpec((1, width), lambda i: (0, 0))]
        + [rows] * len(parts)
        + [ANYWHERE] * len(waits),
        out_specs=[rows, rows, pl.BlockSpec((8, width), lambda i: (0, 0))],
        out_shape=[
            jax.ShapeDtypeStruct((tokens, width), jnp.float32),
            jax.ShapeDtypeStruct((tokens, width), jnp.bfloat16),
            jax.ShapeDtypeStruct((8, width), jnp.float32),
        ],
        compiler_params=pltpu.CompilerParams(vmem_limit_bytes=VMEM),
        cost_estimate=LIGHT,
    )(values, add, gain[None], *parts, *waits)
    return result, low, sums[0], sums[1]


def spot_in(i, slot, blocks):
    return jnp.clip(i - slot * blocks, 0, blocks - 1)


def project_kernel(*refs, blocks):
    weight_ref, scale_ref, out_ref = refs[-3:]
    for s, ref in enumerate(refs[:-3]):

        @pl.when(pl.program_id(0) // blocks == s)
        def _(ref=ref):
            out_ref[...] = (dot_nt(ref[...], weight_ref[...]) * scale_ref[...]).astype(jnp.bfloat16)


def project(slots, weight, scale):
    tokens, width = slots[0].shape
    rows = min(256, tokens)
    blocks = tokens // rows
    units = weight.shape[0]
    return pl.pallas_call(
        functools.partial(project_kernel, blocks=blocks),
        grid=(len(slots) * blocks,),
        in_specs=[
            pl.BlockSpec((rows, width), functools.partial(lambda i, s: (spot_in(i, s, blocks), 0), s=s))
            for s in range(len(slots))
        ]
        + [WHOLE, WHOLE],
        out_specs=pl.BlockSpec((rows, units), lambda i: (i, 0)),
        out_shape=jax.ShapeDtypeStruct((len(slots) * tokens, units), jnp.bfloat16),
        compiler_params=pltpu.CompilerParams(vmem_limit_bytes=VMEM),
        cost_estimate=LIGHT,
    )(*slots, weight, scale)


def product_kernel(*refs, parts, added):
    weight_ref, out_ref = refs[parts], refs[-1]
    total = None
    at = 0
    for ref in refs[:parts]:
        depth = ref.shape[1]
        part = dot_nn(ref[...], weight_ref[at : at + depth, :])
        total = part if total is None else total + part
        at += depth
    for ref in refs[parts + 1 : parts + 1 + added]:
        total = total + ref[...].astype(jnp.float32)
    out_ref[...] = total.astype(out_ref.dtype)


def product(parts, slot, tokens, weight, addends, dtype, waits=()):
    rows = min(256, tokens)
    blocks = tokens // rows
    width = weight.shape[1]
    own = pl.BlockSpec((rows, width), lambda i: (i, 0))
    return pl.pallas_call(
        ignoring(
            functools.partial(product_kernel, parts=len(parts), added=len(addends)),
            len(parts) + 1 + len(addends),
            len(waits),
        ),
        grid=(blocks,),
        in_specs=[pl.BlockSpec((rows, part.shape[1]), lambda i: (slot * blocks + i, 0)) for part in parts]
        + [WHOLE]
        + [own] * len(addends)
        + [ANYWHERE] * len(waits),
        out_specs=own,
        out_shape=jax.ShapeDtypeStruct((tokens, width), dtype),
        compiler_params=pltpu.CompilerParams(vmem_limit_bytes=VMEM),
        cost_estimate=LIGHT,
    )(*parts, weight, *addends, *waits)


def unit_grads_kernel(me_ref, x_ref, *refs, slots, runs):
    outs = refs[slots:]
    tokens = refs[0].shape[0]
    total = None
    for k, ref in enumerate(refs[:slots]):
        part = dot_tn(x_ref[k * tokens : (k + 1) * tokens, :], ref[...])
        total = part if total is None else total + part
    low = total.astype(jnp.bfloat16)
    if len(outs) == 1:
        outs[0][...] = low
        return
    for s, ref in enumerate(outs):

        @pl.when(pl.program_id(0) // runs == s)
        def _(ref=ref):
            ref[...] = low


def unit_grads(x, slots, me, wide, split, waits=()):
    tokens, units = x.shape
    width = slots[0].shape[1]
    each = units // wide
    rows = min(256, each)
    runs = each // rows
    if split:
        out_specs = [
            pl.BlockSpec((rows, width), functools.partial(lambda i, m, s: (spot_in(i, s, runs), 0), s=s))
            for s in range(wide)
        ]
        out_shape = [jax.ShapeDtypeStruct((each, width), jnp.bfloat16)] * wide
    else:
        out_specs = pl.BlockSpec((rows, width), lambda i, m: (i, 0))
        out_shape = jax.ShapeDtypeStruct((units, width), jnp.bfloat16)
    grid_spec = pltpu.PrefetchScalarGridSpec(
        num_scalar_prefetch=1,
        grid=(units // rows,),
        in_specs=[pl.BlockSpec((tokens, rows), lambda i, m: (0, ((i // runs) ^ m[0]) * runs + i % runs))]
        + [WHOLE] * len(slots)
        + [ANYWHERE] * len(waits),
        out_specs=out_specs,
    )
    return pl.pallas_call(
        ignoring(
            functools.partial(unit_grads_kernel, slots=len(slots), runs=runs), 2 + len(slots), len(waits)
        ),
        grid_spec=grid_spec,
        out_shape=out_shape,
        compiler_params=pltpu.CompilerParams(vmem_limit_bytes=VMEM),
        cost_estimate=LIGHT,
    )(me, x, *slots, *waits)


def head_grads_kernel(me_ref, grads_ref, mixed_ref, *refs, group, wide):
    outs, low = refs[2 * group : 2 * group + wide], refs[-1]

    def give(left_ref, slots):
        tokens = slots[0].shape[0]
        total = None
        for k, ref in enumerate(slots):
            part = dot_tn(left_ref[k * tokens : (k + 1) * tokens, :], ref[...])
            total = part if total is None else total + part
        return total.astype(jnp.bfloat16)

    low[: 3 * PAIR] = give(grads_ref, refs[:group])
    low[3 * PAIR :] = give(mixed_ref, refs[group : 2 * group])
    rows = PAIR // wide
    for t in range(4):
        for s, ref in enumerate(outs):
            begin = pl.multiple_of(t * PAIR + (me_ref[0] ^ s) * rows, rows)
            ref[0, t] = low[pl.ds(begin, rows), :]


def head_grads(grads, mixed, a1, states, me, begin, wide):
    length = grads.shape[0]
    width = a1[0].shape[1]
    pairs = grads.shape[1] // (3 * PAIR)
    rows = PAIR // wide
    grid_spec = pltpu.PrefetchScalarGridSpec(
        num_scalar_prefetch=1,
        grid=(pairs,),
        in_specs=[
            pl.BlockSpec((length, 3 * PAIR), lambda p, m: (0, p)),
            pl.BlockSpec((length, PAIR), lambda p, m: (0, begin + p)),
        ]
        + [WHOLE] * (2 * len(states)),
        out_specs=[pl.BlockSpec((1, 4, rows, width), lambda p, m: (p, 0, 0, 0))] * wide,
        scratch_shapes=[pltpu.VMEM((4 * PAIR, width), jnp.bfloat16)],
    )
    return pl.pallas_call(
        functools.partial(head_grads_kernel, group=len(states), wide=wide),
        grid_spec=grid_spec,
        out_shape=[jax.ShapeDtypeStruct((pairs, 4, rows, width), jnp.bfloat16)] * wide,
        compiler_params=pltpu.CompilerParams(vmem_limit_bytes=VMEM),
        cost_estimate=LIGHT,
    )(me, grads, mixed, *a1, *states)


class Net:
    def __init__(self, wide, narrow, group):
        self.wide, self.narrow, self.group = wide, narrow, group
        self.ring = narrow // group

    def from_group(self, value, s):
        return lax.ppermute(value, "narrow", [(i, i ^ s) for i in range(self.narrow)])

    def from_ring(self, value, r):
        return self.from_group(value, r * self.group)

    def from_wide(self, value, s):
        return lax.ppermute(value, "wide", [(i, i ^ s) for i in range(self.wide)])

    def bit_order(self, turn):
        bits = self.wide.bit_length() - 1
        return [1 << ((b + turn) % bits) for b in range(bits)]

    def hops(self, unit, turn):
        return {bit: self.from_wide(unit, bit) for bit in self.bit_order(turn)}

    def spread(self, unit, turn, hops):
        pieces = {0: unit}
        for bit in self.bit_order(turn):
            more = {s ^ bit: self.from_wide(piece, bit) for s, piece in pieces.items() if s}
            pieces.update(more)
            pieces[bit] = hops[bit]
        return [pieces[s] for s in range(self.wide)]

    def scatter_wide(self, parts):
        return [parts[0]] + [self.from_wide(parts[s], s) for s in range(1, self.wide)]

    def spread_doubling(self, unit, turn):
        order, pieces = [0], [unit]
        for bit in self.bit_order(turn):
            away = self.from_wide(jnp.stack(pieces, axis=0), bit)
            order = order + [s ^ bit for s in order]
            pieces = pieces + [away[k] for k in range(len(pieces))]
        return [pieces[order.index(s)] for s in range(self.wide)]

    def swap_wide(self, parts):
        return lax.all_to_all(parts, "wide", 0, 0, tiled=True)

    def gather_wide(self, own):
        return self.swap_wide(jnp.broadcast_to(own[None], (self.wide,) + own.shape))

    def ring_slots(self, own):
        return [own] + [self.from_ring(own, r) for r in range(1, self.ring)]

    def total(self, value):
        value = value + sum(self.from_group(value, s) for s in range(1, self.group))
        value = value + sum(self.from_ring(value, r) for r in range(1, self.ring))
        return value + sum(self.from_wide(value, s) for s in range(1, self.wide))


def by_xor(parts, me):
    bit = 1
    while bit < len(parts):
        swap = me & bit != 0
        parts = [jnp.where(swap, parts[k ^ bit], part) for k, part in enumerate(parts)]
        bit *= 2
    return parts


def hold_kernel(*refs):
    pass


def after(value, *others):
    values, tree = jax.tree.flatten(value)
    waits = jax.tree.leaves(others)
    if len(values) + len(waits) < 2 or not values:
        return value
    held = pl.pallas_call(
        hold_kernel,
        in_specs=[ANYWHERE] * (len(values) + len(waits)),
        out_specs=[ANYWHERE] * len(values),
        out_shape=[jax.ShapeDtypeStruct(one.shape, one.dtype) for one in values],
        input_output_aliases={k: k for k in range(len(values))},
        cost_estimate=LIGHT,
    )(*values, *waits)
    return jax.tree.unflatten(tree, held)


def sum_low(parts):
    return jnp.sum(parts.astype(jnp.float32), axis=0).astype(jnp.bfloat16)


class RingSum:
    def __init__(self, net, parts):
        self.net, self.parts = net, list(parts)

    def send(self):
        keep = len(self.parts) // 2
        self.gone = jnp.stack(self.parts[keep:], axis=0)
        self.arrived = self.net.from_ring(self.gone, keep)
        return self

    def add(self):
        keep = len(self.parts) // 2
        self.parts = [sum_low(jnp.stack([part, self.arrived[k]])) for k, part in enumerate(self.parts[:keep])]
        return self


def place_rows_kernel(me_ref, *refs, order, rows, wide):
    sources, out_ref = refs[:-1], refs[-1]
    places = {}
    for at, (r, t, w) in enumerate(order):
        places[r, t, w] = at
    half = sources[0].shape[0]
    for r, t, w in order:
        ref = sources[(r // half) * wide + w]
        at = jnp.int32(0)
        true_r, true_w = me_ref[0] ^ r, me_ref[1] ^ w
        first_r = {k: places[k, t, 0] for k in {key[0] for key in places}}
        for k, begin in first_r.items():
            at = jnp.where(true_r == k, begin, at)
        begin = pl.multiple_of((at + true_w) * rows, rows)
        out_ref[pl.ds(begin, rows), :] = ref[r % half, t * rows : (t + 1) * rows]


def place_rows(me, sources, order, rows, wide, waits=()):
    return pl.pallas_call(
        ignoring(
            functools.partial(place_rows_kernel, order=order, rows=rows, wide=wide), 1 + len(sources), len(waits)
        ),
        in_specs=[pl.BlockSpec(memory_space=pltpu.SMEM)] + [WHOLE] * len(sources) + [ANYWHERE] * len(waits),
        out_specs=WHOLE,
        out_shape=jax.ShapeDtypeStruct((len(order) * rows, sources[0].shape[-1]), sources[0].dtype),
        compiler_params=pltpu.CompilerParams(vmem_limit_bytes=VMEM),
        cost_estimate=LIGHT,
    )(me, *sources, *waits)


def place_units_kernel(me_ref, *refs, ring, wide):
    sources, out_ref = refs[:wide], refs[wide]
    unit = out_ref.shape[0] // (ring * wide)
    for s, ref in enumerate(sources):
        for r in range(ring):
            begin = pl.multiple_of(((me_ref[1] ^ s) * ring + (me_ref[0] ^ r)) * unit, unit)
            out_ref[pl.ds(begin, unit), :] = ref[r]


def place_units(me, pieces, ring):
    wide = len(pieces)
    unit, width = pieces[0].shape[1:]
    return pl.pallas_call(
        functools.partial(place_units_kernel, ring=ring, wide=wide),
        in_specs=[pl.BlockSpec(memory_space=pltpu.SMEM)] + [WHOLE] * wide,
        out_specs=WHOLE,
        out_shape=jax.ShapeDtypeStruct((wide * ring * unit, width), pieces[0].dtype),
        compiler_params=pltpu.CompilerParams(vmem_limit_bytes=VMEM),
        cost_estimate=LIGHT,
    )(me, *pieces)


def on_device(
    inputs,
    seg_ids,
    buckets,
    norm1_gain,
    norm1_shift,
    w_query,
    w_key,
    w_value,
    w_out,
    norm2_gain,
    norm2_shift,
    w_up,
    w_down,
    rel_table,
    out_grad,
    *,
    wide,
    narrow,
):
    bf16, f32 = jnp.bfloat16, jnp.float32
    tokens, width = inputs.shape
    length = seg_ids.shape[1]
    group = length // tokens
    net = Net(wide, narrow, group)
    ring = net.ring
    head_rows = w_query.shape[0]
    heads_here = rel_table.shape[1]
    piece_rows = head_rows // wide
    scale = HD ** (-0.5)
    block = min(256, tokens)
    per_slot = tokens // block
    blocks = length // block
    reach_blocks = min(blocks, -(-REACH // block) + 1)
    me_wide = lax.axis_index("wide")
    me_narrow = lax.axis_index("narrow")
    me_group = me_narrow % group
    me_ring = me_narrow // group

    def my_part(shard, axis=0):
        size = shard.shape[axis] // wide
        return lax.dynamic_slice_in_dim(shard, me_wide * size, size, axis)

    def slot(value, s):
        return value[s * tokens : (s + 1) * tokens]

    table_low = []
    left = rel_table
    for _ in range(3):
        table_low.append(lax.reduce_precision(left, 8, 7))
        left = left - table_low[-1]
    table_flat = jnp.stack(table_low, axis=0).astype(bf16).reshape(-1)
    table_row = jnp.pad(table_flat, (0, 16 * width - table_flat.size)).reshape(16, width)
    attention_quarter = my_part(jnp.stack([w_query, w_key, w_value, w_out], axis=0), 1).reshape(-1, width)
    attention_rows = attention_quarter.shape[0]
    first_parts = net.ring_slots(jnp.concatenate([attention_quarter, table_row], axis=0))
    tables = [
        jnp.sum(part[attention_rows, : table_flat.size].reshape((3,) + rel_table.shape).astype(f32), axis=0)
        for part in first_parts
    ]
    tables = by_xor(tables, me_ring)
    cut_ring = ring // 2
    attention_pieces = [
        net.spread_doubling(jnp.stack([part[:attention_rows] for part in half], axis=0), turn)
        for turn, half in enumerate([first_parts[:cut_ring], first_parts[cut_ring:]])
    ]
    ffn_own = jnp.concatenate([my_part(w_up, 1).T, my_part(w_down)], axis=0)
    unit = ffn_own.shape[0] // 2

    values_in = inputs.astype(f32)
    normed1, inverse1 = row_norm(values_in)
    a1_own = (normed1 * norm1_gain + norm1_shift).astype(bf16)
    a1_away = [net.from_group(a1_own, s) for s in range(1, group)]
    a1 = [a1_own] + a1_away
    dy_away = [net.from_group(out_grad, s) for s in range(1, group)]
    dy = [out_grad] + dy_away
    ffn_slots = net.ring_slots(after(ffn_own, first_parts[1:]))
    ffn_units = [jnp.stack([rows[k * unit : (k + 1) * unit] for rows in ffn_slots], axis=0) for k in range(2)]
    ffn_hops = [net.hops(units, k) for k, units in enumerate(ffn_units)]

    per_pair = PAIR // head_rows
    pairs = ring // per_pair
    order = [
        (p * per_pair + r, t, w)
        for p in range(pairs)
        for t in range(3)
        for r in range(per_pair)
        for w in range(wide)
    ] + [(r, 3, w) for r in range(ring) for w in range(wide)]
    cut_at = 3 * ring * wide

    me = jnp.stack([me_ring, me_wide]).astype(jnp.int32)
    sources = attention_pieces[0] + attention_pieces[1]
    w_joined = place_rows(me, sources, order[:cut_at], piece_rows, wide, dy_away + ffn_units)
    w_out_full = place_rows(me, sources, order[cut_at:], piece_rows, wide)
    column_kind = (jnp.arange(w_joined.shape[0]) // PAIR) % 3
    column_scale = jnp.where(column_kind == 0, jnp.asarray(scale, f32), jnp.asarray(1.0, f32))
    joined = project(a1, w_joined, column_scale[None])

    reach = reach_blocks * block
    one_hot = (buckets[:reach, None] == jnp.arange(rel_table.shape[0])[None, :]).astype(f32)

    table_here = jnp.concatenate([tables[r] for r in range(ring)], axis=1)
    line = jnp.dot(one_hot, table_here, precision=lax.Precision.HIGHEST, preferred_element_type=f32).T
    lines = jnp.concatenate([jnp.full((line.shape[0], block), MASKED_SCORE, f32), line], axis=1)

    segments = lax.dynamic_slice_in_dim(seg_ids, me_ring, 1, 0)[0]
    first = jnp.sum((segments[None, :] < segments[:, None]).astype(jnp.int32), axis=1)
    scalars = jnp.concatenate([me_group[None], first[::block] // block]).astype(jnp.int32)
    first = first.reshape(blocks, block)

    mixed, lse = attend(joined, first, lines, scalars, block, per_slot, ffn_units)
    mixed, ffn_hops = after((mixed, ffn_hops))
    ffn_pieces = [net.spread(units, k, ffn_hops[k]) for k, units in enumerate(ffn_units)]

    attended_part = [product([mixed], s, tokens, w_out_full, [], bf16) for s in range(1, group)]
    attended_away = [net.from_group(part, s + 1) for s, part in enumerate(attended_part)]
    hidden_state = product([mixed], 0, tokens, w_out_full, [inputs] + attended_away, f32)
    normed2, inverse2 = row_norm(hidden_state)
    a2_own = (normed2 * norm2_gain + norm2_shift).astype(bf16)
    a2_own, ffn_pieces = after((a2_own, ffn_pieces))
    a2 = [a2_own] + [net.from_group(a2_own, s) for s in range(1, group)]

    w_up_t, w_down_full = (place_units(me, pieces, ring) for pieces in ffn_pieces)
    active, up_grad, *normed2_part = hidden_units(a2, dy, w_up_t, w_down_full)
    normed2_away = [net.from_group(normed2_part[s], s) for s in range(1, group)]
    here = jnp.zeros((1,), jnp.int32)
    down_grads = unit_grads(active, dy, here, wide, False).reshape(wide, -1, width)
    down_parts = net.swap_wide(down_grads)
    state_grad, state_low, grad_gain2, grad_shift2 = norm_back(
        hidden_state, out_grad, norm2_gain, [normed2_part[0]] + normed2_away, [down_grads]
    )
    state_away = [net.from_group(state_low, s) for s in range(1, group)]
    up_grads = unit_grads(up_grad, a2, me[1:], wide, True, [state_low])
    states = [state_low] + after(state_away, up_grads)
    mixed_grad = project(states, w_out_full, jnp.ones((1, w_out_full.shape[0]), f32))
    feed_part = [product([active], s, tokens, w_down_full, [], bf16, [mixed_grad]) for s in range(1, group)]
    feed_away = [net.from_group(rows, s + 1) for s, rows in enumerate(feed_part)]

    def grads_of(begin, end, waits):
        return attend_back(
            joined, mixed, mixed_grad, first, lines, lse, scalars, block, per_slot, begin, end, waits
        )

    def attention_grads(grads, begin, end, place):
        if per_pair == 1 and piece_rows % 16 == 0:
            return head_grads(grads, mixed, a1, states, place, begin, wide)
        grad_part = sum(dot_tn(slot(grads, s), rows) for s, rows in enumerate(a1)).astype(bf16).reshape(end - begin, 3, per_pair, wide, piece_rows, width)
        grad_part = jnp.transpose(grad_part, (3, 0, 2, 1, 4, 5)).reshape(wide, -1, 3, piece_rows, width)
        columns = slice(begin * PAIR, end * PAIR)
        grad_out = sum(dot_tn(slot(mixed, s)[:, columns], state) for s, state in enumerate(states)).astype(bf16)
        grad_out = jnp.moveaxis(grad_out.reshape(-1, wide, 1, piece_rows, width), 1, 0)
        whole = jnp.concatenate([grad_part, grad_out], axis=2)
        return by_xor([whole[w] for w in range(wide)], place[0])

    cut = pairs // 2
    up_parts = net.scatter_wide(up_grads)
    grads_a, lines_a = grads_of(0, cut, list(up_grads) + feed_part)
    grads_a, down_parts = after((grads_a, down_parts))
    head_a = attention_grads(grads_a, 0, cut, me[1:])
    head_a, up_parts = after((head_a, up_parts))
    parts_a = net.scatter_wide(head_a)
    down_low = sum_low(down_parts).reshape(ring, -1, width)
    up_low = sum_low(jnp.stack(up_parts)).reshape(ring, -1, width)
    ffn_low = jnp.concatenate([down_low, up_low], axis=1)
    ffn_ring = RingSum(net, by_xor([ffn_low[z] for z in range(ring)], me_ring)).send()
    grads_b, lines_b = grads_of(cut, pairs, list(head_a) + [ffn_ring.gone])
    grads_b, ffn_ring.arrived, parts_a = after((grads_b, ffn_ring.arrived, parts_a))
    ffn_ring.add().send()
    head_b = attention_grads(grads_b, cut, pairs, me[1:])
    parts_b = net.scatter_wide(head_b)
    all_grads, all_lines = [grads_a, grads_b], [lines_a, lines_b]

    w_late = after(w_joined, head_b, ffn_ring.gone)

    normed1_part = [product(all_grads, s, tokens, w_late, [], bf16) for s in range(1, group)]
    normed1_away = [net.from_group(part, s + 1) for s, part in enumerate(normed1_part)]
    w_late, ffn_ring.arrived = after((w_late, ffn_ring.arrived), normed1_part)
    normed1_own = product(all_grads, 0, tokens, w_late, [], f32)
    parts_b = after(parts_b, normed1_own)
    head_low = jnp.concatenate([sum_low(jnp.stack(parts_a)), sum_low(jnp.stack(parts_b))], axis=0)
    head_ring = RingSum(net, by_xor([head_low[z] for z in range(ring)], me_ring)).send()
    ffn_part = after(ffn_ring.add().parts[0], head_ring.gone)
    ffn_pieces = [net.from_wide(ffn_part, s) for s in range(1, wide)]
    out = product(
        [active], 0, tokens, w_down_full, [hidden_state] + feed_away, bf16, [head_ring.gone, ffn_part]
    )
    input_grad, _, grad_gain1, grad_shift1 = norm_back(
        inputs, state_grad, norm1_gain, [normed1_own] + normed1_away, [out] + ffn_pieces
    )

    line_grad = jnp.concatenate(all_lines, axis=0)[:, block:]
    table_grad = jnp.dot(line_grad, one_hot, precision=lax.Precision.HIGHEST, preferred_element_type=f32)
    all_heads = heads_here * narrow
    head_ids = jnp.stack([(r * group + me_group) * heads_here + h for r in range(ring) for h in range(heads_here)])
    placed = (jnp.arange(all_heads)[:, None] == head_ids[None, :]).astype(f32)
    table_all = jnp.dot(placed, table_grad, precision=lax.Precision.HIGHEST, preferred_element_type=f32)

    small = jnp.concatenate([grad_gain1, grad_shift1, grad_gain2, grad_shift2, table_all.reshape(-1)])
    pad = -small.shape[0] % 1024
    small_own = small
    small = jnp.pad(small, (0, pad)).reshape(-1, 128)
    small = small + sum(net.from_group(small, s) for s in range(1, group))
    small = small + sum(net.from_wide(small, s) for s in range(1, wide))
    head_ring.arrived = after(head_ring.arrived, small_own)
    head_ring.add().send()
    small, head_gone = after((small, head_ring.gone))
    small = small + sum(net.from_ring(small, r) for r in range(1, ring))
    small = small.reshape(-1)
    gain1, shift1, gain2, shift2 = (small[k * width : (k + 1) * width] for k in range(4))
    table_sum = small[4 * width : 4 * width + table_all.size].reshape(table_all.shape)
    table_out = lax.dynamic_slice_in_dim(table_sum, me_narrow * heads_here, heads_here, 0).T

    attention_part = head_ring.add().parts[0]
    attention_part = jnp.broadcast_to(after(attention_part, small_own)[None], (wide,) + attention_part.shape)
    ffn_pieces = after(ffn_pieces, attention_part)
    ffn_all = jnp.stack(by_xor([ffn_part] + ffn_pieces, me_wide), axis=0)
    down_all = ffn_all[:, :unit].reshape(-1, width).astype(f32)
    up_all = ffn_all[:, unit:].reshape(-1, width).T.astype(f32)
    attention_all = net.swap_wide(attention_part)
    attention_all = jnp.moveaxis(attention_all, 1, 0).reshape(4, head_rows, width).astype(f32)
    return (
        out,
        input_grad,
        gain1,
        shift1,
        attention_all[0],
        attention_all[1],
        attention_all[2],
        attention_all[3],
        gain2,
        shift2,
        up_all,
        down_all,
        table_out,
    )


def solution(mesh):
    placed = (
        P(("wide", "narrow"), None),
        P("wide", None),
        P(),
        P(),
        P(),
        P("narrow", None),
        P("narrow", None),
        P("narrow", None),
        P("narrow", None),
        P(),
        P(),
        P(None, "narrow"),
        P("narrow", None),
        P(None, "narrow"),
        P(("wide", "narrow"), None),
    )
    return jax.shard_map(
        functools.partial(on_device, wide=mesh.shape["wide"], narrow=mesh.shape["narrow"]),
        mesh=mesh,
        in_specs=placed,
        out_specs=(
            P(("wide", "narrow"), None),
            P(("wide", "narrow"), None),
            P(),
            P(),
            P("narrow", None),
            P("narrow", None),
            P("narrow", None),
            P("narrow", None),
            P(),
            P(),
            P(None, "narrow"),
            P("narrow", None),
            P(None, "narrow"),
        ),
        check_vma=False,
    )
```

time: 590 us -> 541 us (0.917)
  Pallas kernels: 101 us -> 294 us
  matrix products: 161 us -> 1.08 us
  local copies, waits for them, and re-layouts: 69.4 us -> 37 us
  waiting for transfers between devices: 103 us -> 78.1 us
  starting transfers between devices: 85.7 us -> 69.1 us
  other arithmetic: 61 us -> 52.4 us
    pallas_call x1 -> x19, Pallas kernels: 0.28 us -> 188 us  [the longest x6 45 us: product(): pl.pallas_call(ignoring(functools.partial(product_kernel, parts=len(parts...]
    dot_general x22 -> x0, matrix products: 160 us -> none  [the longest x4 57.6 us: dot_nt(): return lax.dot_general(left, right, NT, preferred_element_type=jnp.float32)]
    ppermute x37 -> x25, waiting for transfers between devices: 72.6 us -> 27.7 us  [from_wide(): return lax.ppermute(value, 'wide', [(i, i ^ s) for i in range(self.wide)])]
    convert_element_type x24 -> x7, other arithmetic: 29 us -> 5.61 us  [the longest x4 2.11 us: on_device(): part[attention_rows, :table_flat.size].reshape((3,) + rel_table.shape)]
    unnamed x209 -> x77, local copies, waits for them, and re-layouts: 33.3 us -> 10.7 us
    ppermute x37 -> x25, starting transfers between devices: 48.9 us -> 31.2 us  [from_wide(): return lax.ppermute(value, 'wide', [(i, i ^ s) for i in range(self.wide)])]
    ppermute x24 -> x22, waiting for transfers between devices: 30 us -> 45.9 us  [from_group(): lax.ppermute(value, 'narrow', [(i, i ^ s) for i in range(self.narrow)])]
    slice x16 -> x4, local copies, waits for them, and re-layouts: 14.1 us -> 3.2 us  [the longest x2 1.68 us: norm_back(): return (result, low, sums[0], sums[1])]
  transfers between devices with their start and end apart: 61 -> 49, of which waited for: 18 -> 16; matrix products, arithmetic and copies ran while one was open for 37% -> 13% of each run, Pallas kernels for 17% -> 47%
where the time goes in v3:
time: 541 us; the launch traced here: 533 us
  Pallas kernels  294 us (54%)
  waiting for transfers between devices  78.1 us (14%)
  starting transfers between devices  69.1 us (13%)
  other arithmetic  52.4 us (10%)
  local copies, waits for them, and re-layouts  37 us (7%)
    pallas_call x2, Pallas kernels, attend_back(): pl.pallas_call(ignoring(functools.partial(attend_back_kernel, block=block...  74.7 us
    ppermute x22, waiting for transfers between devices, from_group(): lax.ppermute(value, 'narrow', [(i, i ^ s) for i in range(self.narrow)])  45.9 us
    pallas_call x6, Pallas kernels, product(): pl.pallas_call(ignoring(functools.partial(product_kernel, parts=len(parts...  45 us
    pallas_call x1, Pallas kernels, hidden_units(): pl.pallas_call(functools.partial(hidden_kernel, slots=slots, blocks=block...  39.2 us
    ppermute x25, starting transfers between devices, from_wide(): return lax.ppermute(value, 'wide', [(i, i ^ s) for i in range(self.wide)])  31.2 us
    pallas_call x1, Pallas kernels, attend(): pl.pallas_call(ignoring(functools.partial(attend_kernel, block=block, per...  30.8 us
    pallas_call x2, Pallas kernels, unit_grads(): pl.pallas_call(ignoring(functools.partial(unit_grads_kernel, slots=len(sl...  29.5 us
    ppermute x22, starting transfers between devices, from_group(): lax.ppermute(value, 'narrow', [(i, i ^ s) for i in range(self.narrow)])  28.2 us
  transfers between devices with their start and end apart: 49, of which 16 were waited for; matrix products, arithmetic and copies ran while one was open for 13% of the time, Pallas kernels for 47%

profile of v3, /device:TPU:0, one launch (start us, length us, event | category | flops | bytes accessed | tf_op | source)
XLA Modules:
  0.0 532.9 jit_solution(5206551022895657308)
XLA Ops:
  20.0 7.9 %collective-permute-done.1.refs_1_ = bf16[144,1024]{1,0:T(8,128)(2,1)} collective-permute-done((bf16[144,1024]{1,0:T(8,128)(2,1)}, bf16[144,1024]{1,0:T(8,128)(2,1)}, u32[]{:S(2)}, u32[]{:S(2)}) %collective-permute-start.1) | collective-permute-done | bytes 294944 | tf_op jit(solution)/shard_map/ppermute | solution.py:585
  59.2 26.3 %collective-permute-done.10 = bf16[256,1024]{1,0:T(8,128)(2,1)} collective-permute-done((bf16[256,1024]{1,0:T(8,128)(2,1)}, bf16[256,1024]{1,0:T(8,128)(2,1)}, u32[]{:S(2)}, u32[]{:S(2)}) %collective-permute-start.10) | collective-permute-done | bytes 524320 | tf_op jit(solution)/shard_map/ppermute | solution.py:585
  106.0 12.6 %shard_map.248.refs_1_ = bf16[2048,1536]{1,0:T(8,128)(2,1)} custom-call(bf16[1024,1024]{1,0:T(8,128)(2,1)} %fusion.5.refs_0_, bf16[1024,1024]{1,0:T(8,128)(2,1)} %collective-permute-done.refs_1_, bf16[1536,1024]{1,0:T(8,128)(2,1)} %shard_map.247.refs_2_.refs_0_, f32[1,1536]{1,0:T(1,128)} %compare_select_fusion.refs_3_), custom_call_target="tpu_custom_call" | custom-call | flops 1 | bytes 1 | tf_op jit(solution)/shard_map/pallas_call | solution.py:430
  121.8 30.8 %shard_map.249 = (bf16[2048,512]{1,0:T(8,128)(2,1)}, f32[8,8,256]{2,1,0:T(8,128)}) custom-call(s32[9]{0:T(128)} %pad_add_fusion.refs_0_, bf16[2048,1536]{1,0:T(8,128)(2,1)} %shard_map.248.refs_1_, s32[8,256]{1,0:T(8,128)} %reshape.221.refs_2_.refs_4_, f32[8,1536]{1,0:T(8,128)} %concatenate.28.refs_3_.refs_5_, bf16[4,128,1024]{2,1,0:T(8,128)(2,1)} %copy-done.6, ...), custom_call_target="tpu_custom_call" | custom-call | flops 1 | bytes 1 | tf_op jit(solution)/shard_map/pallas_call | solution.py:275
  161.9 6.2 %shard_map.253.refs_0_.refs_2_ = f32[1024,1024]{1,0:T(8,128)} custom-call(bf16[2048,512]{1,0:T(8,128)(2,1)} %get-tuple-element.81.refs_0_.refs_2_.mixed_ref, bf16[512,1024]{1,0:T(8,128)(2,1)} %shard_map.251.refs_1_.refs_2_, bf16[1024,1024]{1,0:T(8,128)(2,1)} %refs_0_.1, bf16[1024,1024]{1,0:T(8,128)(2,1)} %collective-permute-done.16.refs_3_), custom_call_target="tpu_custom_call" | custom-call | flops 1 | bytes 1 | tf_op jit(solution)/shard_map/pallas_call | solution.py:464
  176.0 7.2 %collective-permute-done.17.refs_4_ = bf16[4,128,1024]{2,1,0:T(8,128)(2,1)S(1)} collective-permute-done((bf16[4,128,1024]{2,1,0:T(8,128)(2,1)}, bf16[4,128,1024]{2,1,0:T(8,128)(2,1)S(1)}, u32[]{:S(2)}, u32[]{:S(2)}) %collective-permute-start.17) | collective-permute-done | bytes 1048608 | tf_op jit(solution)/shard_map/ppermute | solution.py:591
  195.7 39.2 %shard_map.257 = (bf16[2048,2048]{1,0:T(8,128)(2,1)}, bf16[2048,2048]{1,0:T(8,128)(2,1)}, bf16[1024,1024]{1,0:T(8,128)(2,1)}, bf16[1024,1024]{1,0:T(8,128)(2,1)}) custom-call(bf16[1024,1024]{1,0:T(8,128)(2,1)} %get-tuple-element.86.refs_0_.refs_2_, bf16[1024,1024]{1,0:T(8,128)(2,1)} %copy-done.9, bf16[1024,1024]{1,0:T(8,128)(2,1)} %refs_1_.1, ...), custom_call_target="tpu_custom_call" | custom-call | flops 1 | bytes 1 | tf_op jit(solution)/shard_map/pallas_call | solution.py:356
  235.4 14.1 %shard_map.258 = bf16[2048,1024]{1,0:T(8,128)(2,1)} custom-call(s32[1]{0:T(128)} %constant.105.clone.1.refs_0_, bf16[2048,2048]{1,0:T(8,128)(2,1)} %get-tuple-element.95.refs_1_.refs_0_, bf16[1024,1024]{1,0:T(8,128)(2,1)} %refs_1_.1, bf16[1024,1024]{1,0:T(8,128)(2,1)} %collective-permute-done.8.refs_9_.refs_3_), custom_call_target="tpu_custom_call" | custom-call | flops 1 | bytes 1 | tf_op jit(solution)/shard_map/pallas_call | solution.py:523
  249.6 5.3 all-to-all-start
  256.2 8.3 %shard_map.259 = (f32[1024,1024]{1,0:T(8,128)}, bf16[1024,1024]{1,0:T(8,128)(2,1)}, f32[8,1024]{1,0:T(8,128)}) custom-call(f32[1024,1024]{1,0:T(8,128)} %shard_map.253.refs_0_.refs_2_, bf16[1024,1024]{1,0:T(8,128)(2,1)} %refs_1_.1, f32[1,1024]{1,0:T(1,128)} %bitcast.138, bf16[1024,1024]{1,0:T(8,128)(2,1)} %get-tuple-element.96.refs_3_, ...), custom_call_target="tpu_custom_call" | custom-call | flops 1 | bytes 1 | tf_op jit(solution)/shard_map/pallas_call | solution.py:394
  264.7 15.3 %shard_map.260 = (bf16[512,1024]{1,0:T(8,128)(2,1)}, bf16[512,1024]{1,0:T(8,128)(2,1)}, bf16[512,1024]{1,0:T(8,128)(2,1)}, bf16[512,1024]{1,0:T(8,128)(2,1)}) custom-call(s32[1]{0:T(128)} %bitcast.3.refs_0_.me_ref, bf16[2048,2048]{1,0:T(8,128)(2,1)} %get-tuple-element.99.refs_1_, bf16[1024,1024]{1,0:T(8,128)(2,1)} %get-tuple-element.86.refs_0_.refs_2_, ...), custom_call_target="tpu_custom_call" | custom-call | flops 1 | bytes 1 | tf_op jit(solution)/shard_map/pallas_call | solution.py:523
  285.4 8.3 %shard_map.262.refs_2_.refs_3_ = bf16[2048,512]{1,0:T(8,128)(2,1)} custom-call(bf16[1024,1024]{1,0:T(8,128)(2,1)} %get-tuple-element.98.refs_4_.refs_0_.refs_2_, bf16[1024,1024]{1,0:T(8,128)(2,1)} %shard_map.261.refs_1_.refs_3_, bf16[512,1024]{1,0:T(8,128)(2,1)} %shard_map.251.refs_1_.refs_2_, f32[1,512]{1,0:T(1,128)} %broadcast_in_dim.22.refs_3_), custom_call_target="tpu_custom_call" | custom-call | flops 1 | bytes 1 | tf_op jit(solution)/shard_map/pallas_call | solution.py:430
  293.7 8.6 %shard_map.263.refs_11_ = bf16[1024,1024]{1,0:T(8,128)(2,1)} custom-call(bf16[2048,2048]{1,0:T(8,128)(2,1)} %get-tuple-element.95.refs_1_.refs_0_, bf16[2048,1024]{1,0:T(8,128)(2,1)} %shard_map.256.refs_5_.refs_1_, bf16[2048,512]{1,0:T(8,128)(2,1)} %shard_map.262.refs_2_.refs_3_), custom_call_target="tpu_custom_call" | custom-call | flops 1 | bytes 1 | tf_op jit(solution)/shard_map/pallas_call | solution.py:464
  302.3 37.4 %shard_map.264 = (bf16[2048,768]{1,0:T(8,128)(2,1)}, f32[4,1536]{1,0:T(4,128)}) custom-call(s32[9]{0:T(128)} %pad_add_fusion.refs_0_, bf16[2048,1536]{1,0:T(8,128)(2,1)} %shard_map.248.refs_1_, bf16[2048,512]{1,0:T(8,128)(2,1)} %get-tuple-element.81.refs_0_.refs_2_.mixed_ref, bf16[2048,512]{1,0:T(8,128)(2,1)} %shard_map.262.refs_2_.refs_3_, ...), custom_call_target="tpu_custom_call" | custom-call | flops 1 | bytes 1 | tf_op jit(solution)/shard_map/pallas_call | solution.py:306
  339.7 10.1 %shard_map.266 = (bf16[2,4,32,1024]{3,2,1,0:T(8,128)(2,1)}, bf16[2,4,32,1024]{3,2,1,0:T(8,128)(2,1)}, bf16[2,4,32,1024]{3,2,1,0:T(8,128)(2,1)}, bf16[2,4,32,1024]{3,2,1,0:T(8,128)(2,1)}) custom-call(s32[1]{0:T(128)} %bitcast.3.refs_0_.me_ref, bf16[2048,768]{1,0:T(8,128)(2,1)} %get-tuple-element.106.grads_ref.refs_0_, ...), custom_call_target="tpu_custom_call" | custom-call | flops 1 | bytes 1 | tf_op jit(solution)/shard_map/pallas_call | solution.py:570
  358.5 11.0 %collective-permute-start.26 = (bf16[2,256,1024]{2,1,0:T(8,128)(2,1)S(1)}, bf16[2,256,1024]{2,1,0:T(8,128)(2,1)}, u32[]{:S(2)}, u32[]{:S(2)}) collective-permute-start(bf16[2,256,1024]{2,1,0:T(8,128)(2,1)S(1)} %pad_maximum_fusion.5.refs_11_), channel_id=1, source_target_pairs={{0,4},{1,5},{2,6},{3,7},{4,0},{5,1},{6,2},{7,3},{8,12},{9,13},{10,... | collective-permute-start | bytes 3145736 | tf_op jit(solution)/shard_map/ppermute | solution.py:585
  374.1 37.3 %shard_map.268 = (bf16[2048,768]{1,0:T(8,128)(2,1)}, f32[4,1536]{1,0:T(4,128)}) custom-call(s32[9]{0:T(128)} %pad_add_fusion.refs_0_, bf16[2048,1536]{1,0:T(8,128)(2,1)} %shard_map.248.refs_1_, bf16[2048,512]{1,0:T(8,128)(2,1)} %get-tuple-element.81.refs_0_.refs_2_.mixed_ref, bf16[2048,512]{1,0:T(8,128)(2,1)} %shard_map.262.refs_2_.refs_3_, ...), custom_call_target="tpu_custom_call" | custom-call | flops 1 | bytes 1 | tf_op jit(solution)/shard_map/pallas_call | solution.py:306
  416.5 10.0 %shard_map.270 = (bf16[2,4,32,1024]{3,2,1,0:T(8,128)(2,1)}, bf16[2,4,32,1024]{3,2,1,0:T(8,128)(2,1)}, bf16[2,4,32,1024]{3,2,1,0:T(8,128)(2,1)}, bf16[2,4,32,1024]{3,2,1,0:T(8,128)(2,1)}) custom-call(s32[1]{0:T(128)} %bitcast.3.refs_0_.me_ref, bf16[2048,768]{1,0:T(8,128)(2,1)} %get-tuple-element.125.grads_ref.refs_1_, ...), custom_call_target="tpu_custom_call" | custom-call | flops 1 | bytes 1 | tf_op jit(solution)/shard_map/pallas_call | solution.py:570
  431.0 7.3 %shard_map.272.refs_2_ = bf16[1024,1024]{1,0:T(8,128)(2,1)} custom-call(bf16[2048,768]{1,0:T(8,128)(2,1)} %get-tuple-element.106.grads_ref.refs_0_, bf16[2048,768]{1,0:T(8,128)(2,1)} %get-tuple-element.125.grads_ref.refs_1_, bf16[1536,1024]{1,0:T(8,128)(2,1)} %shard_map.271.refs_2_.refs_0_), custom_call_target="tpu_custom_call" | custom-call | flops 1 | bytes 1 | tf_op jit(solution)/shard_map/pallas_call | solution.py:464
  440.3 7.7 %shard_map.274.refs_4_.refs_3_ = f32[1024,1024]{1,0:T(8,128)} custom-call(bf16[2048,768]{1,0:T(8,128)(2,1)} %get-tuple-element.106.grads_ref.refs_0_, bf16[2048,768]{1,0:T(8,128)(2,1)} %get-tuple-element.125.grads_ref.refs_1_, bf16[1536,1024]{1,0:T(8,128)(2,1)} %get-tuple-element.131.refs_2_), custom_call_target="tpu_custom_call" | custom-call | flops 1 | bytes 1 | tf_op jit(solution)/shard_map/pallas_call | solution.py:464
  448.0 6.3 %collective-permute-done.31.refs_2_ = bf16[2,4,32,1024]{3,2,1,0:T(8,128)(2,1)} collective-permute-done((bf16[2,4,32,1024]{3,2,1,0:T(8,128)(2,1)}, bf16[2,4,32,1024]{3,2,1,0:T(8,128)(2,1)}, u32[]{:S(2)}, u32[]{:S(2)}) %collective-permute-start.31) | collective-permute-done | bytes 524320 | tf_op jit(solution)/shard_map/ppermute | solution.py:591
  464.2 10.5 %shard_map.277.refs_5_ = bf16[1024,1024]{1,0:T(8,128)(2,1)} custom-call(bf16[2048,2048]{1,0:T(8,128)(2,1)} %get-tuple-element.95.refs_1_.refs_0_, bf16[2048,1024]{1,0:T(8,128)(2,1)} %shard_map.256.refs_5_.refs_1_, f32[1024,1024]{1,0:T(8,128)} %shard_map.253.refs_0_.refs_2_, bf16[1024,1024]{1,0:T(8,128)(2,1)} %collective-permute-done.22.refs_3_, ...), custom_call_target="tpu_custom_call" | custom-call | flops 1 | bytes 1 | tf_op jit(solution)/shard_map/pallas_call | solution.py:464
  475.1 8.9 %collective-permute-done.36.refs_7_.refs_1_ = bf16[256,1024]{1,0:T(8,128)(2,1)S(1)} collective-permute-done((bf16[256,1024]{1,0:T(8,128)(2,1)}, bf16[256,1024]{1,0:T(8,128)(2,1)S(1)}, u32[]{:S(2)}, u32[]{:S(2)}) %collective-permute-start.36) | collective-permute-done | bytes 524320 | tf_op jit(solution)/shard_map/ppermute | solution.py:591
  485.0 8.9 %shard_map.278 = (f32[1024,1024]{1,0:T(8,128)}, bf16[1024,1024]{1,0:T(8,128)(2,1)}, f32[8,1024]{1,0:T(8,128)}) custom-call(bf16[1024,1024]{1,0:T(8,128)(2,1)} %refs_0_.1, f32[1024,1024]{1,0:T(8,128)} %get-tuple-element.137.refs_1_, f32[1,1024]{1,0:T(1,128)} %bitcast.137, f32[1024,1024]{1,0:T(8,128)} %shard_map.274.refs_4_.refs_3_, ...), custom_call_target="tpu_custom_call" | custom-call | flops 1 | bytes 1 | tf_op jit(solution)/shard_map/pallas_call | solution.py:394
  (289 shorter events, 185.8 us)
Async XLA Ops:
  3.5 27.9 %collective-permute-start.5 = (bf16[144,1024]{1,0:T(8,128)(2,1)}, bf16[144,1024]{1,0:T(8,128)(2,1)}, u32[]{:S(2)}, u32[]{:S(2)}) collective-permute-start(bf16[144,1024]{1,0:T(8,128)(2,1)} %pad_maximum_fusion.11), channel_id=1, source_target_pairs={{0,6},{1,7},{2,4},{3,5},{4,2},{5,3},{6,0},{7,1},{8,14},{9,15},{10,... | collective-permute-start | bytes 884744 | tf_op jit(solution)/shard_map/ppermute | solution.py:585
  8.6 25.4 %collective-permute-start.4 = (bf16[144,1024]{1,0:T(8,128)(2,1)}, bf16[144,1024]{1,0:T(8,128)(2,1)}, u32[]{:S(2)}, u32[]{:S(2)}) collective-permute-start(bf16[144,1024]{1,0:T(8,128)(2,1)} %pad_maximum_fusion.11), channel_id=1, source_target_pairs={{0,4},{1,5},{2,6},{3,7},{4,0},{5,1},{6,2},{7,3},{8,12},{9,13},{10,... | collective-permute-start | bytes 884744 | tf_op jit(solution)/shard_map/ppermute | solution.py:585
  9.2 84.5 %collective-permute-start.8 = (bf16[1024,1024]{1,0:T(8,128)(2,1)}, bf16[1024,1024]{1,0:T(8,128)(2,1)}, u32[]{:S(2)}, u32[]{:S(2)}) collective-permute-start(bf16[1024,1024]{1,0:T(8,128)(2,1)} %refs_1_.1), channel_id=1, source_target_pairs={{0,1},{1,0},{2,3},{3,2},{4,5},{5,4},{6,7},{7,6},{8,9},{9,8},{10,11... | collective-permute-start | bytes 6291464 | tf_op jit(solution)/shard_map/ppermute | solution.py:585
  41.4 44.1 %collective-permute-start.10 = (bf16[256,1024]{1,0:T(8,128)(2,1)}, bf16[256,1024]{1,0:T(8,128)(2,1)}, u32[]{:S(2)}, u32[]{:S(2)}) collective-permute-start(bf16[256,1024]{1,0:T(8,128)(2,1)} %shard_map.246), channel_id=1, source_target_pairs={{0,4},{1,5},{2,6},{3,7},{4,0},{5,1},{6,2},{7,3},{8,12},{9,13},{10,... | collective-permute-start | bytes 1572872 | tf_op jit(solution)/shard_map/ppermute | solution.py:585
  44.0 43.7 %collective-permute-start.9 = (bf16[256,1024]{1,0:T(8,128)(2,1)}, bf16[256,1024]{1,0:T(8,128)(2,1)}, u32[]{:S(2)}, u32[]{:S(2)}) collective-permute-start(bf16[256,1024]{1,0:T(8,128)(2,1)} %shard_map.246), channel_id=1, source_target_pairs={{0,2},{1,3},{2,0},{3,1},{4,6},{5,7},{6,4},{7,5},{8,10},{9,11},{10,... | collective-permute-start | bytes 1572872 | tf_op jit(solution)/shard_map/ppermute | solution.py:585
  49.2 42.4 %collective-permute-start.3 = (bf16[2,2,128,1024]{3,2,1,0:T(8,128)(2,1)}, bf16[2,2,128,1024]{3,2,1,0:T(8,128)(2,1)}, u32[]{:S(2)}, u32[]{:S(2)}) collective-permute-start(bf16[2,2,128,1024]{3,2,1,0:T(8,128)(2,1)} %pad_maximum_fusion.1), channel_id=1, source_target_pairs={{0,16},{8,24},{16,0},{24,8},{1,17},{9,25},{17,1},{25,9},{2,18},{10... | collective-permute-start | bytes 3145736 | tf_op jit(solution)/shard_map/ppermute | solution.py:591
  56.7 35.4 %collective-permute-start.7 = (bf16[2,2,128,1024]{3,2,1,0:T(8,128)(2,1)}, bf16[2,2,128,1024]{3,2,1,0:T(8,128)(2,1)}, u32[]{:S(2)}, u32[]{:S(2)}) collective-permute-start(bf16[2,2,128,1024]{3,2,1,0:T(8,128)(2,1)} %pad_maximum_fusion.2), channel_id=1, source_target_pairs={{0,8},{8,0},{16,24},{24,16},{1,9},{9,1},{17,25},{25,17},{2,10},{10... | collective-permute-start | bytes 3145736 | tf_op jit(solution)/shard_map/ppermute | solution.py:591
  89.9 62.7 %collective-permute-start.13 = (bf16[4,128,1024]{2,1,0:T(8,128)(2,1)S(1)}, bf16[4,128,1024]{2,1,0:T(8,128)(2,1)}, u32[]{:S(2)}, u32[]{:S(2)}) collective-permute-start(bf16[4,128,1024]{2,1,0:T(8,128)(2,1)S(1)} %pad_maximum_fusion.3.refs_10_.refs_4_.refs_1_), channel_id=1, source_target_pairs={{0,16},{8,24},{16,0},{24,8},{1,17},{9,25},{17,1},{25,9},{2,18},{10... | collective-permute-start | bytes 3145736 | tf_op jit(solution)/shard_map/ppermute | solution.py:591
  91.6 61.0 %collective-permute-start.12 = (bf16[4,128,1024]{2,1,0:T(8,128)(2,1)S(1)}, bf16[4,128,1024]{2,1,0:T(8,128)(2,1)}, u32[]{:S(2)}, u32[]{:S(2)}) collective-permute-start(bf16[4,128,1024]{2,1,0:T(8,128)(2,1)S(1)} %pad_maximum_fusion.3.refs_10_.refs_4_.refs_1_), channel_id=1, source_target_pairs={{0,8},{8,0},{16,24},{24,16},{1,9},{9,1},{17,25},{25,17},{2,10},{10... | collective-permute-start | bytes 3145736 | tf_op jit(solution)/shard_map/ppermute | solution.py:591
  92.1 60.5 %collective-permute-start.15 = (bf16[4,128,1024]{2,1,0:T(8,128)(2,1)}, bf16[4,128,1024]{2,1,0:T(8,128)(2,1)}, u32[]{:S(2)}, u32[]{:S(2)}) collective-permute-start(bf16[4,128,1024]{2,1,0:T(8,128)(2,1)} %pad_maximum_fusion.4.refs_11_.refs_5_), channel_id=1, source_target_pairs={{0,16},{8,24},{16,0},{24,8},{1,17},{9,25},{17,1},{25,9},{2,18},{10... | collective-permute-start | bytes 3145736 | tf_op jit(solution)/shard_map/ppermute | solution.py:591
  93.7 58.9 %collective-permute-start.14 = (bf16[4,128,1024]{2,1,0:T(8,128)(2,1)}, bf16[4,128,1024]{2,1,0:T(8,128)(2,1)}, u32[]{:S(2)}, u32[]{:S(2)}) collective-permute-start(bf16[4,128,1024]{2,1,0:T(8,128)(2,1)} %pad_maximum_fusion.4.refs_11_.refs_5_), channel_id=1, source_target_pairs={{0,8},{8,0},{16,24},{24,16},{1,9},{9,1},{17,25},{25,17},{2,10},{10... | collective-permute-start | bytes 3145736 | tf_op jit(solution)/shard_map/ppermute | solution.py:591
  157.4 25.8 %collective-permute-start.17 = (bf16[4,128,1024]{2,1,0:T(8,128)(2,1)}, bf16[4,128,1024]{2,1,0:T(8,128)(2,1)S(1)}, u32[]{:S(2)}, u32[]{:S(2)}) collective-permute-start(bf16[4,128,1024]{2,1,0:T(8,128)(2,1)} %get-tuple-element.82.refs_2_), channel_id=1, source_target_pairs={{0,16},{8,24},{16,0},{24,8},{1,17},{9,25},{17,1},{25,9},{2,18},{10... | collective-permute-start | bytes 3145736 | tf_op jit(solution)/shard_map/ppermute | solution.py:591
  158.9 25.5 %collective-permute-start.18 = (bf16[4,128,1024]{2,1,0:T(8,128)(2,1)}, bf16[4,128,1024]{2,1,0:T(8,128)(2,1)S(1)}, u32[]{:S(2)}, u32[]{:S(2)}) collective-permute-start(bf16[4,128,1024]{2,1,0:T(8,128)(2,1)} %get-tuple-element.85.refs_7_), channel_id=1, source_target_pairs={{0,8},{8,0},{16,24},{24,16},{1,9},{9,1},{17,25},{25,17},{2,10},{10... | collective-permute-start | bytes 3145736 | tf_op jit(solution)/shard_map/ppermute | solution.py:591
  249.6 90.1 %all-to-all-start = ((bf16[4,512,1024]{2,1,0:T(8,128)(2,1)}), bf16[4,512,1024]{2,1,0:T(8,128)(2,1)}, u32[]{:S(2)}, u32[]{:S(2)}) async-start(bf16[4,512,1024]{2,1,0:T(8,128)(2,1)} %bitcast.113), calls=%async_computation | async-start | bytes 8388608 | tf_op jit(solution)/shard_map/all_to_all | solution.py:620
  280.0 74.1 %collective-permute-start.23 = (bf16[512,1024]{1,0:T(8,128)(2,1)}, bf16[512,1024]{1,0:T(8,128)(2,1)S(1)}, u32[]{:S(2)}, u32[]{:S(2)}) collective-permute-start(bf16[512,1024]{1,0:T(8,128)(2,1)} %get-tuple-element.101.refs_2_.refs_8_), channel_id=1, source_target_pairs={{0,8},{8,0},{16,24},{24,16},{1,9},{9,1},{17,25},{25,17},{2,10},{10... | collective-permute-start | bytes 3145736 | tf_op jit(solution)/shard_map/ppermute | solution.py:591
  282.0 72.2 %collective-permute-start.24 = (bf16[512,1024]{1,0:T(8,128)(2,1)}, bf16[512,1024]{1,0:T(8,128)(2,1)}, u32[]{:S(2)}, u32[]{:S(2)}) collective-permute-start(bf16[512,1024]{1,0:T(8,128)(2,1)} %get-tuple-element.102.refs_3_.refs_9_), channel_id=1, source_target_pairs={{0,16},{8,24},{16,0},{24,8},{1,17},{9,25},{17,1},{25,9},{2,18},{10... | collective-permute-start | bytes 3145736 | tf_op jit(solution)/shard_map/ppermute | solution.py:591
  283.5 70.7 %collective-permute-start.25 = (bf16[512,1024]{1,0:T(8,128)(2,1)}, bf16[512,1024]{1,0:T(8,128)(2,1)}, u32[]{:S(2)}, u32[]{:S(2)}) collective-permute-start(bf16[512,1024]{1,0:T(8,128)(2,1)} %get-tuple-element.103.refs_4_.refs_10_), channel_id=1, source_target_pairs={{0,24},{8,16},{16,8},{24,0},{1,25},{9,17},{17,9},{25,1},{2,26},{10... | collective-permute-start | bytes 3145736 | tf_op jit(solution)/shard_map/ppermute | solution.py:591
  358.5 56.8 %collective-permute-start.26 = (bf16[2,256,1024]{2,1,0:T(8,128)(2,1)S(1)}, bf16[2,256,1024]{2,1,0:T(8,128)(2,1)}, u32[]{:S(2)}, u32[]{:S(2)}) collective-permute-start(bf16[2,256,1024]{2,1,0:T(8,128)(2,1)S(1)} %pad_maximum_fusion.5.refs_11_), channel_id=1, source_target_pairs={{0,4},{1,5},{2,6},{3,7},{4,0},{5,1},{6,2},{7,3},{8,12},{9,13},{10,... | collective-permute-start | bytes 3145736 | tf_op jit(solution)/shard_map/ppermute | solution.py:585
  369.5 41.9 %collective-permute-start.27 = (bf16[2,4,32,1024]{3,2,1,0:T(8,128)(2,1)}, bf16[2,4,32,1024]{3,2,1,0:T(8,128)(2,1)S(1)}, u32[]{:S(2)}, u32[]{:S(2)}) collective-permute-start(bf16[2,4,32,1024]{3,2,1,0:T(8,128)(2,1)} %get-tuple-element.112.refs_8_), channel_id=1, source_target_pairs={{0,8},{8,0},{16,24},{24,16},{1,9},{9,1},{17,25},{25,17},{2,10},{10... | collective-permute-start | bytes 1572872 | tf_op jit(solution)/shard_map/ppermute | solution.py:591
  372.6 38.8 %collective-permute-start.28 = (bf16[2,4,32,1024]{3,2,1,0:T(8,128)(2,1)}, bf16[2,4,32,1024]{3,2,1,0:T(8,128)(2,1)}, u32[]{:S(2)}, u32[]{:S(2)}) collective-permute-start(bf16[2,4,32,1024]{3,2,1,0:T(8,128)(2,1)} %get-tuple-element.113.refs_9_), channel_id=1, source_target_pairs={{0,16},{8,24},{16,0},{24,8},{1,17},{9,25},{17,1},{25,9},{2,18},{10... | collective-permute-start | bytes 1572872 | tf_op jit(solution)/shard_map/ppermute | solution.py:591
  372.9 38.5 %collective-permute-start.29 = (bf16[2,4,32,1024]{3,2,1,0:T(8,128)(2,1)}, bf16[2,4,32,1024]{3,2,1,0:T(8,128)(2,1)}, u32[]{:S(2)}, u32[]{:S(2)}) collective-permute-start(bf16[2,4,32,1024]{3,2,1,0:T(8,128)(2,1)} %get-tuple-element.114.refs_10_), channel_id=1, source_target_pairs={{0,24},{8,16},{16,8},{24,0},{1,25},{9,17},{17,9},{25,1},{2,26},{10... | collective-permute-start | bytes 1572872 | tf_op jit(solution)/shard_map/ppermute | solution.py:591
  431.0 33.1 %collective-permute-start.22 = (bf16[1024,1024]{1,0:T(8,128)(2,1)}, bf16[1024,1024]{1,0:T(8,128)(2,1)}, u32[]{:S(2)}, u32[]{:S(2)}) collective-permute-start(bf16[1024,1024]{1,0:T(8,128)(2,1)} %shard_map.263.refs_11_), channel_id=1, source_target_pairs={{0,1},{1,0},{2,3},{3,2},{4,5},{5,4},{6,7},{7,6},{8,9},{9,8},{10,11... | collective-permute-start | bytes 6291464 | tf_op jit(solution)/shard_map/ppermute | solution.py:585
  438.3 45.7 %collective-permute-start.34 = (bf16[1024,1024]{1,0:T(8,128)(2,1)}, bf16[1024,1024]{1,0:T(8,128)(2,1)}, u32[]{:S(2)}, u32[]{:S(2)}) collective-permute-start(bf16[1024,1024]{1,0:T(8,128)(2,1)} %shard_map.272.refs_2_), channel_id=1, source_target_pairs={{0,1},{1,0},{2,3},{3,2},{4,5},{5,4},{6,7},{7,6},{8,9},{9,8},{10,11... | collective-permute-start | bytes 6291464 | tf_op jit(solution)/shard_map/ppermute | solution.py:585
  464.1 30.7 %collective-permute-start.42 = (bf16[2,4,32,1024]{3,2,1,0:T(8,128)(2,1)}, bf16[2,4,32,1024]{3,2,1,0:T(8,128)(2,1)S(1)}, u32[]{:S(2)}, u32[]{:S(2)}) collective-permute-start(bf16[2,4,32,1024]{3,2,1,0:T(8,128)(2,1)} %pad_maximum_fusion.10.refs_1_.refs_4_), channel_id=1, source_target_pairs={{0,4},{1,5},{2,6},{3,7},{4,0},{5,1},{6,2},{7,3},{8,12},{9,13},{10,... | collective-permute-start | bytes 1572872 | tf_op jit(solution)/shard_map/ppermute | solution.py:585
  (61 other events, 641.1 us)

commit v4 on v3

--- a/solution.py
+++ b/solution.py
@@ -1,4 +1,5 @@
 import functools
+import math
 
 import jax
 import jax.numpy as jnp
@@ -175,11 +176,10 @@
     heads = strips.shape[0]
     pairs = heads // 2
 
-    def columns(p, kind):
-        return slice((3 * (p + begin) + kind) * PAIR, (3 * (p + begin) + kind + 1) * PAIR)
+    columns = columns_of
 
     def wide_columns(p):
-        return slice((p + begin) * PAIR, (p + begin + 1) * PAIR)
+        return slice(p * PAIR, (p + 1) * PAIR)
 
     @pl.when(i == 0)
     def _():
@@ -216,11 +216,14 @@
             values = x_ref[here, columns(p, 2)]
             dk_new = dk[here, span]
             dv_new = dv[here, span]
+            both_scores = dot_nt(keys, jnp.concatenate(own_q[2 * p : 2 * p + 2], axis=0))
+            both_grads = dot_nt(values, jnp.concatenate(own_up[2 * p : 2 * p + 2], axis=0))
             for h in (2 * p, 2 * p + 1):
-                scores = dot_nt(keys, own_q[h]) + strip_tile(strips, h, t, block)
+                half = slice((h - 2 * p) * block, (h - 2 * p + 1) * block)
+                scores = both_scores[:, half] + strip_tile(strips, h, t, block)
                 scores = jnp.where(allowed, scores, MASKED_SCORE)
                 probs = jnp.exp(scores - lse_ref[i, 2 * begin + h : 2 * begin + h + 1, :])
-                score_grad = probs * (dot_nt(values, own_up[h]) - deltas[h])
+                score_grad = probs * (both_grads[:, half] - deltas[h])
                 add_to_strip(sums, h, t, score_grad)
                 low_grad = score_grad.astype(jnp.bfloat16)
                 dv_new = dv_new + dot_nn(probs.astype(jnp.bfloat16), own_up[h])
@@ -288,12 +291,19 @@
     length = joined.shape[0]
     span = lines.shape[1]
     heads = 2 * (end - begin)
+    part = begin // (end - begin)
     blocks = length // block
     strip = pltpu.VMEM((heads, min(128, block), span), jnp.float32)
     grid_spec = pltpu.PrefetchScalarGridSpec(
         num_scalar_prefetch=1,
         grid=(blocks,),
-        in_specs=[WHOLE] * 6 + [ANYWHERE] * len(waits),
+        in_specs=[
+            pl.BlockSpec((length, 3 * heads * HD), lambda i, s: (0, part)),
+            pl.BlockSpec((length, heads * HD), lambda i, s: (0, part)),
+            pl.BlockSpec((length, heads * HD), lambda i, s: (0, part)),
+        ]
+        + [WHOLE] * 3
+        + [ANYWHERE] * len(waits),
         out_specs=[WHOLE] * 2,
         scratch_shapes=[
             strip,
@@ -317,10 +327,21 @@
     )(scalars, joined, mixed, upstream, first, lines, lse, *waits)
 
 
-def hidden_kernel(*refs, slots, blocks, chunk):
+def hidden_kernel(*refs, slots, blocks, wide, chunk):
     a2_refs, dy_refs = refs[:slots], refs[slots : 2 * slots]
-    up_ref, down_ref, act_ref, up_grad_ref = refs[2 * slots : 2 * slots + 4]
-    back_refs = refs[2 * slots + 4 :]
+    at = 2 * slots
+    up_parts, down_parts = refs[at : at + wide], refs[at + wide : at + 2 * wide]
+    act_ref, up_grad_ref = refs[at + 2 * wide : at + 2 * wide + 2]
+    back_refs = refs[at + 2 * wide + 2 : -2]
+    up_ref, down_ref = refs[-2:]
+
+    @pl.when(pl.program_id(0) == 0)
+    def _():
+        each = up_ref.shape[0] // wide
+        for s in range(wide):
+            up_ref[s * each : (s + 1) * each, :] = up_parts[s][...].reshape(each, up_ref.shape[1])
+            down_ref[s * each : (s + 1) * each, :] = down_parts[s][...].reshape(each, up_ref.shape[1])
+
     for s in range(slots):
 
         @pl.when(pl.program_id(0) // blocks == s)
@@ -342,10 +363,10 @@
             back_refs[s][...] = total.astype(jnp.bfloat16)
 
 
-def hidden_units(a2, dy, w_up_t, w_down):
+def hidden_units(a2, dy, up_parts, down_parts):
     tokens, width = a2[0].shape
-    slots = len(a2)
-    units = w_up_t.shape[0]
+    slots, wide = len(a2), len(up_parts)
+    units = wide * up_parts[0].shape[0] * up_parts[0].shape[1]
     block = min(256, tokens)
     blocks = tokens // block
     unit_block = pl.BlockSpec((block, units), lambda i: (i, 0))
@@ -354,15 +375,16 @@
         for s in range(slots)
     ]
     return pl.pallas_call(
-        functools.partial(hidden_kernel, slots=slots, blocks=blocks, chunk=min(512, units)),
+        functools.partial(hidden_kernel, slots=slots, blocks=blocks, wide=wide, chunk=min(1024, units)),
         grid=(slots * blocks,),
-        in_specs=by_slot + by_slot + [WHOLE, WHOLE],
+        in_specs=by_slot + by_slot + [WHOLE] * (2 * wide),
         out_specs=[unit_block, unit_block] + by_slot,
         out_shape=[jax.ShapeDtypeStruct((slots * tokens, units), jnp.bfloat16)] * 2
         + [jax.ShapeDtypeStruct((tokens, width), jnp.bfloat16)] * slots,
+        scratch_shapes=[pltpu.VMEM((units, width), jnp.bfloat16)] * 2,
         compiler_params=pltpu.CompilerParams(vmem_limit_bytes=VMEM),
         cost_estimate=LIGHT,
-    )(*a2, *dy, w_up_t, w_down)
+    )(*a2, *dy, *up_parts, *down_parts)
 
 
 def norm_back_kernel(*refs, parts):
@@ -389,7 +411,7 @@
 
 def norm_back(values, add, gain, parts, waits=()):
     tokens, width = values.shape
-    block = min(256, tokens)
+    block = min(512, tokens)
     rows = pl.BlockSpec((block, width), lambda i: (i, 0))
     result, low, sums = pl.pallas_call(
         ignoring(functools.partial(norm_back_kernel, parts=len(parts)), 3 + len(parts), len(waits)),
@@ -424,7 +446,7 @@
 
 def project(slots, weight, scale):
     tokens, width = slots[0].shape
-    rows = min(256, tokens)
+    rows = min(512, tokens)
     blocks = tokens // rows
     units = weight.shape[0]
     return pl.pallas_call(
@@ -442,41 +464,48 @@
     )(*slots, weight, scale)
 
 
-def product_kernel(*refs, parts, added):
-    weight_ref, out_ref = refs[parts], refs[-1]
+def product_kernel(*refs, parts, weights, added):
+    sides = refs[:parts]
+    weight_refs = refs[parts : parts + weights]
+    out_ref = refs[-1]
+    depth = min([ref.shape[1] for ref in sides] + [math.prod(ref.shape[:-1]) for ref in weight_refs])
     total = None
-    at = 0
-    for ref in refs[:parts]:
-        depth = ref.shape[1]
-        part = dot_nn(ref[...], weight_ref[at : at + depth, :])
+    for at in range(0, sum(ref.shape[1] for ref in sides), depth):
+        ref, here = sides[at // sides[0].shape[1]], at % sides[0].shape[1]
+        rows = math.prod(weight_refs[0].shape[:-1])
+        weight_ref, there = weight_refs[at // rows], at % rows
+        if len(weight_ref.shape) == 2:
+            weight = weight_ref[there : there + depth, :]
+        else:
+            weight = weight_ref[...].reshape(rows, weight_ref.shape[-1])
+        part = dot_nn(ref[:, here : here + depth], weight)
         total = part if total is None else total + part
-        at += depth
-    for ref in refs[parts + 1 : parts + 1 + added]:
+    for ref in refs[parts + weights : parts + weights + added]:
         total = total + ref[...].astype(jnp.float32)
     out_ref[...] = total.astype(out_ref.dtype)
 
 
-def product(parts, slot, tokens, weight, addends, dtype, waits=()):
+def product(parts, slot, tokens, weights, addends, dtype, waits=()):
     rows = min(256, tokens)
     blocks = tokens // rows
-    width = weight.shape[1]
+    width = weights[0].shape[-1]
     own = pl.BlockSpec((rows, width), lambda i: (i, 0))
     return pl.pallas_call(
         ignoring(
-            functools.partial(product_kernel, parts=len(parts), added=len(addends)),
-            len(parts) + 1 + len(addends),
+            functools.partial(product_kernel, parts=len(parts), weights=len(weights), added=len(addends)),
+            len(parts) + len(weights) + len(addends),
             len(waits),
         ),
         grid=(blocks,),
         in_specs=[pl.BlockSpec((rows, part.shape[1]), lambda i: (slot * blocks + i, 0)) for part in parts]
-        + [WHOLE]
+        + [WHOLE] * len(weights)
         + [own] * len(addends)
         + [ANYWHERE] * len(waits),
         out_specs=own,
         out_shape=jax.ShapeDtypeStruct((tokens, width), dtype),
         compiler_params=pltpu.CompilerParams(vmem_limit_bytes=VMEM),
         cost_estimate=LIGHT,
-    )(*parts, weight, *addends, *waits)
+    )(*parts, *weights, *addends, *waits)
 
 
 def unit_grads_kernel(me_ref, x_ref, *refs, slots, runs):
@@ -501,7 +530,7 @@
     tokens, units = x.shape
     width = slots[0].shape[1]
     each = units // wide
-    rows = min(256, each)
+    rows = min(512, each)
     runs = each // rows
     if split:
         out_specs = [
@@ -609,11 +638,16 @@
         return [parts[0]] + [self.from_wide(parts[s], s) for s in range(1, self.wide)]
 
     def spread_doubling(self, unit, turn):
-        order, pieces = [0], [unit]
+        order, pieces = [0], [(unit[None], 0)]
         for bit in self.bit_order(turn):
-            away = self.from_wide(jnp.stack(pieces, axis=0), bit)
+            stacked = []
+            for array, _ in pieces:
+                if not any(array is other for other in stacked):
+                    stacked.append(array)
+            stacked = stacked[0] if len(stacked) == 1 else jnp.concatenate(stacked, axis=0)
+            away = self.from_wide(stacked, bit)
             order = order + [s ^ bit for s in order]
-            pieces = pieces + [away[k] for k in range(len(pieces))]
+            pieces = [(stacked, k) for k in range(len(pieces))] + [(away, k) for k in range(len(pieces))]
         return [pieces[order.index(s)] for s in range(self.wide)]
 
     def swap_wide(self, parts):
@@ -680,8 +714,9 @@
         return self
 
 
-def place_rows_kernel(me_ref, *refs, order, rows, wide):
-    sources, out_ref = refs[:-1], refs[-1]
+def place_rows_kernel(me_ref, *refs, order, rows, wide, spots):
+    out_ref = refs[-1]
+    sources = [refs[k].at[at] for k, at in spots]
     places = {}
     for at, (r, t, w) in enumerate(order):
         places[r, t, w] = at
@@ -698,38 +733,24 @@
 
 
 def place_rows(me, sources, order, rows, wide, waits=()):
+    arrays, spots = [], []
+    for array, at in sources:
+        known = [k for k, other in enumerate(arrays) if other is array]
+        if not known:
+            arrays.append(array)
+        spots.append((known[0] if known else len(arrays) - 1, at))
     return pl.pallas_call(
         ignoring(
-            functools.partial(place_rows_kernel, order=order, rows=rows, wide=wide), 1 + len(sources), len(waits)
+            functools.partial(place_rows_kernel, order=order, rows=rows, wide=wide, spots=spots),
+            1 + len(arrays),
+            len(waits),
         ),
-        in_specs=[pl.BlockSpec(memory_space=pltpu.SMEM)] + [WHOLE] * len(sources) + [ANYWHERE] * len(waits),
+        in_specs=[pl.BlockSpec(memory_space=pltpu.SMEM)] + [WHOLE] * len(arrays) + [ANYWHERE] * len(waits),
         out_specs=WHOLE,
-        out_shape=jax.ShapeDtypeStruct((len(order) * rows, sources[0].shape[-1]), sources[0].dtype),
+        out_shape=jax.ShapeDtypeStruct((len(order) * rows, arrays[0].shape[-1]), arrays[0].dtype),
         compiler_params=pltpu.CompilerParams(vmem_limit_bytes=VMEM),
         cost_estimate=LIGHT,
-    )(me, *sources, *waits)
-
-
-def place_units_kernel(me_ref, *refs, ring, wide):
-    sources, out_ref = refs[:wide], refs[wide]
-    unit = out_ref.shape[0] // (ring * wide)
-    for s, ref in enumerate(sources):
-        for r in range(ring):
-            begin = pl.multiple_of(((me_ref[1] ^ s) * ring + (me_ref[0] ^ r)) * unit, unit)
-            out_ref[pl.ds(begin, unit), :] = ref[r]
-
-
-def place_units(me, pieces, ring):
-    wide = len(pieces)
-    unit, width = pieces[0].shape[1:]
-    return pl.pallas_call(
-        functools.partial(place_units_kernel, ring=ring, wide=wide),
-        in_specs=[pl.BlockSpec(memory_space=pltpu.SMEM)] + [WHOLE] * wide,
-        out_specs=WHOLE,
-        out_shape=jax.ShapeDtypeStruct((wide * ring * unit, width), pieces[0].dtype),
-        compiler_params=pltpu.CompilerParams(vmem_limit_bytes=VMEM),
-        cost_estimate=LIGHT,
-    )(me, *pieces)
+    )(me, *arrays, *waits)
 
 
 def on_device(
@@ -847,28 +868,28 @@
     mixed, ffn_hops = after((mixed, ffn_hops))
     ffn_pieces = [net.spread(units, k, ffn_hops[k]) for k, units in enumerate(ffn_units)]
 
-    attended_part = [product([mixed], s, tokens, w_out_full, [], bf16) for s in range(1, group)]
+    attended_part = [product([mixed], s, tokens, [w_out_full], [], bf16) for s in range(1, group)]
     attended_away = [net.from_group(part, s + 1) for s, part in enumerate(attended_part)]
-    hidden_state = product([mixed], 0, tokens, w_out_full, [inputs] + attended_away, f32)
+    hidden_state = product([mixed], 0, tokens, [w_out_full], [inputs] + attended_away, f32)
     normed2, inverse2 = row_norm(hidden_state)
     a2_own = (normed2 * norm2_gain + norm2_shift).astype(bf16)
     a2_own, ffn_pieces = after((a2_own, ffn_pieces))
     a2 = [a2_own] + [net.from_group(a2_own, s) for s in range(1, group)]
 
-    w_up_t, w_down_full = (place_units(me, pieces, ring) for pieces in ffn_pieces)
-    active, up_grad, *normed2_part = hidden_units(a2, dy, w_up_t, w_down_full)
+    w_down = ffn_pieces[1]
+    active, up_grad, *normed2_part = hidden_units(a2, dy, ffn_pieces[0], ffn_pieces[1])
     normed2_away = [net.from_group(normed2_part[s], s) for s in range(1, group)]
     here = jnp.zeros((1,), jnp.int32)
-    down_grads = unit_grads(active, dy, here, wide, False).reshape(wide, -1, width)
+    down_grads = unit_grads(active, dy, me[1:], wide, False).reshape(wide, -1, width)
     down_parts = net.swap_wide(down_grads)
     state_grad, state_low, grad_gain2, grad_shift2 = norm_back(
         hidden_state, out_grad, norm2_gain, [normed2_part[0]] + normed2_away, [down_grads]
     )
     state_away = [net.from_group(state_low, s) for s in range(1, group)]
-    up_grads = unit_grads(up_grad, a2, me[1:], wide, True, [state_low])
+    up_grads = unit_grads(up_grad, a2, here, wide, True, [state_low])
     states = [state_low] + after(state_away, up_grads)
     mixed_grad = project(states, w_out_full, jnp.ones((1, w_out_full.shape[0]), f32))
-    feed_part = [product([active], s, tokens, w_down_full, [], bf16, [mixed_grad]) for s in range(1, group)]
+    feed_part = [product([active], s, tokens, w_down, [], bf16, [mixed_grad]) for s in range(1, group)]
     feed_away = [net.from_group(rows, s + 1) for s, rows in enumerate(feed_part)]
 
     def grads_of(begin, end, waits):
@@ -897,7 +918,7 @@
     down_low = sum_low(down_parts).reshape(ring, -1, width)
     up_low = sum_low(jnp.stack(up_parts)).reshape(ring, -1, width)
     ffn_low = jnp.concatenate([down_low, up_low], axis=1)
-    ffn_ring = RingSum(net, by_xor([ffn_low[z] for z in range(ring)], me_ring)).send()
+    ffn_ring = RingSum(net, [ffn_low[r] for r in range(ring)]).send()
     grads_b, lines_b = grads_of(cut, pairs, list(head_a) + [ffn_ring.gone])
     grads_b, ffn_ring.arrived, parts_a = after((grads_b, ffn_ring.arrived, parts_a))
     ffn_ring.add().send()
@@ -907,17 +928,17 @@
 
     w_late = after(w_joined, head_b, ffn_ring.gone)
 
-    normed1_part = [product(all_grads, s, tokens, w_late, [], bf16) for s in range(1, group)]
+    normed1_part = [product(all_grads, s, tokens, [w_late], [], bf16) for s in range(1, group)]
     normed1_away = [net.from_group(part, s + 1) for s, part in enumerate(normed1_part)]
     w_late, ffn_ring.arrived = after((w_late, ffn_ring.arrived), normed1_part)
-    normed1_own = product(all_grads, 0, tokens, w_late, [], f32)
+    normed1_own = product(all_grads, 0, tokens, [w_late], [], f32)
     parts_b = after(parts_b, normed1_own)
     head_low = jnp.concatenate([sum_low(jnp.stack(parts_a)), sum_low(jnp.stack(parts_b))], axis=0)
     head_ring = RingSum(net, by_xor([head_low[z] for z in range(ring)], me_ring)).send()
     ffn_part = after(ffn_ring.add().parts[0], head_ring.gone)
     ffn_pieces = [net.from_wide(ffn_part, s) for s in range(1, wide)]
     out = product(
-        [active], 0, tokens, w_down_full, [hidden_state] + feed_away, bf16, [head_ring.gone, ffn_part]
+        [active], 0, tokens, w_down, [hidden_state] + feed_away, bf16, [head_ring.gone, ffn_part]
     )
     input_grad, _, grad_gain1, grad_shift1 = norm_back(
         inputs, state_grad, norm1_gain, [normed1_own] + normed1_away, [out] + ffn_pieces

time: 541 us -> 518 us (0.957)
  Pallas kernels: 294 us -> 271 us
  waiting for transfers between devices: 78.1 us -> 99 us
  local copies, waits for them, and re-layouts: 37 us -> 26.6 us
  other arithmetic: 52.4 us -> 45.7 us
    ppermute x22, waiting for transfers between devices: 45.9 us -> 62.1 us  [from_group(): lax.ppermute(value, 'narrow', [(i, i ^ s) for i in range(self.narrow)])]
    pallas_call x2 -> x0, Pallas kernels: 9.03 us -> none  [place_units(): pl.pallas_call(functools.partial(place_units_kernel, ring=ring, wide=wide...]
    another operation x4 -> x0, other arithmetic: 6.29 us -> none  [spread_doubling(): away = self.from_wide(jnp.stack(pieces, axis=0), bit)]
    pallas_call x2, Pallas kernels: 74.7 us -> 69.2 us  [attend_back(): pl.pallas_call(ignoring(functools.partial(attend_back_kernel, block=block...]
  transfers between devices with their start and end apart: 49 -> 49, of which waited for: 16 -> 17; matrix products, arithmetic and copies ran while one was open for 13% -> 11% of each run, Pallas kernels for 47% -> 45%
where the time goes in v4:
time: 518 us; the launch traced here: 511 us
  Pallas kernels  271 us (52%)
  waiting for transfers between devices  99 us (19%)
  starting transfers between devices  65.8 us (13%)
  other arithmetic  45.7 us (9%)
  local copies, waits for them, and re-layouts  26.6 us (5%)
    pallas_call x2, Pallas kernels, attend_back(): pl.pallas_call(ignoring(functools.partial(attend_back_kernel, block=block...  69.2 us
    ppermute x22, waiting for transfers between devices, from_group(): lax.ppermute(value, 'narrow', [(i, i ^ s) for i in range(self.narrow)])  62.1 us
    pallas_call x6, Pallas kernels, product(): pl.pallas_call(ignoring(functools.partial(product_kernel, parts=len(parts...  44.4 us
    pallas_call x1, Pallas kernels, hidden_units(): pl.pallas_call(functools.partial(hidden_kernel, slots=slots, blocks=block...  35.9 us
    ppermute x25, waiting for transfers between devices, from_wide(): return lax.ppermute(value, 'wide', [(i, i ^ s) for i in range(self.wide)])  32.4 us
    pallas_call x1, Pallas kernels, attend(): pl.pallas_call(ignoring(functools.partial(attend_kernel, block=block, per...  31.8 us
    ppermute x22, starting transfers between devices, from_group(): lax.ppermute(value, 'narrow', [(i, i ^ s) for i in range(self.narrow)])  29 us
    pallas_call x2, Pallas kernels, unit_grads(): pl.pallas_call(ignoring(functools.partial(unit_grads_kernel, slots=len(sl...  28.2 us
  transfers between devices with their start and end apart: 49, of which 17 were waited for; matrix products, arithmetic and copies ran while one was open for 11% of the time, Pallas kernels for 45%

profile of v4, /device:TPU:0, one launch (start us, length us, event | category | flops | bytes accessed | tf_op | source)
XLA Modules:
  0.0 511.3 jit_solution(4342476534436249318)
XLA Ops:
  3.5 5.0 collective-permute-start.5
  18.0 16.0 %collective-permute-done.4.refs_2_ = bf16[144,1024]{1,0:T(8,128)(2,1)} collective-permute-done((bf16[144,1024]{1,0:T(8,128)(2,1)}, bf16[144,1024]{1,0:T(8,128)(2,1)}, u32[]{:S(2)}, u32[]{:S(2)}) %collective-permute-start.4) | collective-permute-done | bytes 294944 | tf_op jit(solution)/shard_map/ppermute | solution.py:614
  57.6 27.7 %collective-permute-done.10 = bf16[256,1024]{1,0:T(8,128)(2,1)} collective-permute-done((bf16[256,1024]{1,0:T(8,128)(2,1)}, bf16[256,1024]{1,0:T(8,128)(2,1)}, u32[]{:S(2)}, u32[]{:S(2)}) %collective-permute-start.10) | collective-permute-done | bytes 524320 | tf_op jit(solution)/shard_map/ppermute | solution.py:614
  103.0 11.4 %shard_map.248.refs_1_ = bf16[2048,1536]{1,0:T(8,128)(2,1)} custom-call(bf16[1024,1024]{1,0:T(8,128)(2,1)} %fusion.5.refs_0_, bf16[1024,1024]{1,0:T(8,128)(2,1)} %collective-permute-done.refs_1_, bf16[1536,1024]{1,0:T(8,128)(2,1)} %shard_map.247.refs_2_.refs_0_, f32[1,1536]{1,0:T(1,128)} %compare_select_fusion.refs_3_), custom_call_target="tpu_custom_call" | custom-call | flops 1 | bytes 1 | tf_op jit(solution)/shard_map/pallas_call | solution.py:452
  117.7 31.8 %shard_map.249 = (bf16[2048,512]{1,0:T(8,128)(2,1)}, f32[8,8,256]{2,1,0:T(8,128)}) custom-call(s32[9]{0:T(128)} %pad_add_fusion.refs_0_, bf16[2048,1536]{1,0:T(8,128)(2,1)} %shard_map.248.refs_1_, s32[8,256]{1,0:T(8,128)} %reshape.221.refs_2_.refs_4_, f32[8,1536]{1,0:T(8,128)} %concatenate.36.refs_3_.refs_5_, ...), custom_call_target="tpu_custom_call" | custom-call | flops 1 | bytes 1 | tf_op jit(solution)/shard_map/pallas_call | solution.py:278
  158.7 6.2 %shard_map.253.refs_0_.refs_5_ = f32[1024,1024]{1,0:T(8,128)} custom-call(bf16[2048,512]{1,0:T(8,128)(2,1)} %get-tuple-element.81.refs_0_.refs_2_.mixed_ref, bf16[512,1024]{1,0:T(8,128)(2,1)} %shard_map.251.refs_1_.refs_2_, bf16[1024,1024]{1,0:T(8,128)(2,1)} %refs_0_.1, bf16[1024,1024]{1,0:T(8,128)(2,1)} %collective-permute-done.16.refs_3_), custom_call_target="tpu_custom_call" | custom-call | flops 1 | bytes 1 | tf_op jit(solution)/shard_map/pallas_call | solution.py:493
  172.9 7.2 %collective-permute-done.17.refs_4_ = bf16[4,128,1024]{2,1,0:T(8,128)(2,1)S(1)} collective-permute-done((bf16[4,128,1024]{2,1,0:T(8,128)(2,1)}, bf16[4,128,1024]{2,1,0:T(8,128)(2,1)S(1)}, u32[]{:S(2)}, u32[]{:S(2)}) %collective-permute-start.17) | collective-permute-done | bytes 1048608 | tf_op jit(solution)/shard_map/ppermute | solution.py:620
  187.1 35.9 %shard_map.255 = (bf16[2048,2048]{1,0:T(8,128)(2,1)}, bf16[2048,2048]{1,0:T(8,128)(2,1)}, bf16[1024,1024]{1,0:T(8,128)(2,1)}, bf16[1024,1024]{1,0:T(8,128)(2,1)}) custom-call(bf16[1024,1024]{1,0:T(8,128)(2,1)} %get-tuple-element.86.refs_0_.refs_2_, bf16[1024,1024]{1,0:T(8,128)(2,1)} %copy-done.12, bf16[1024,1024]{1,0:T(8,128)(2,1)} %refs_1_.1, ...), custom_call_target="tpu_custom_call" | custom-call | flops 1 | bytes 1 | tf_op jit(solution)/shard_map/pallas_call | solution.py:377
  223.2 13.4 %shard_map.256 = bf16[2048,1024]{1,0:T(8,128)(2,1)} custom-call(s32[1]{0:T(128)} %bitcast.3.refs_0_.me_ref, bf16[2048,2048]{1,0:T(8,128)(2,1)} %get-tuple-element.95.refs_1_.refs_0_, bf16[1024,1024]{1,0:T(8,128)(2,1)} %refs_1_.1, bf16[1024,1024]{1,0:T(8,128)(2,1)} %collective-permute-done.8.refs_5_.refs_3_), custom_call_target="tpu_custom_call" | custom-call | flops 1 | bytes 1 | tf_op jit(solution)/shard_map/pallas_call | solution.py:552
  243.0 7.8 %shard_map.257 = (f32[1024,1024]{1,0:T(8,128)}, bf16[1024,1024]{1,0:T(8,128)(2,1)}, f32[8,1024]{1,0:T(8,128)}) custom-call(f32[1024,1024]{1,0:T(8,128)} %shard_map.253.refs_0_.refs_5_, bf16[1024,1024]{1,0:T(8,128)(2,1)} %refs_1_.1, f32[1,1024]{1,0:T(1,128)} %bitcast.128, bf16[1024,1024]{1,0:T(8,128)(2,1)} %get-tuple-element.96.refs_3_, ...), custom_call_target="tpu_custom_call" | custom-call | flops 1 | bytes 1 | tf_op jit(solution)/shard_map/pallas_call | solution.py:416
  251.2 14.8 %shard_map.258 = (bf16[512,1024]{1,0:T(8,128)(2,1)}, bf16[512,1024]{1,0:T(8,128)(2,1)}, bf16[512,1024]{1,0:T(8,128)(2,1)}, bf16[512,1024]{1,0:T(8,128)(2,1)}) custom-call(s32[1]{0:T(128)} %constant.105.clone.1.refs_0_, bf16[2048,2048]{1,0:T(8,128)(2,1)} %get-tuple-element.99.refs_1_, bf16[1024,1024]{1,0:T(8,128)(2,1)} %get-tuple-element.86.refs_0_.refs_2_, ...), custom_call_target="tpu_custom_call" | custom-call | flops 1 | bytes 1 | tf_op jit(solution)/shard_map/pallas_call | solution.py:552
  271.4 6.4 %shard_map.260.refs_5_.refs_3_ = bf16[2048,512]{1,0:T(8,128)(2,1)} custom-call(bf16[1024,1024]{1,0:T(8,128)(2,1)} %get-tuple-element.98.refs_4_.refs_0_.refs_2_, bf16[1024,1024]{1,0:T(8,128)(2,1)} %shard_map.259.refs_1_.refs_3_, bf16[512,1024]{1,0:T(8,128)(2,1)} %shard_map.251.refs_1_.refs_2_, f32[1,512]{1,0:T(1,128)} %broadcast_in_dim.52.refs_3_), custom_call_target="tpu_custom_call" | custom-call | flops 1 | bytes 1 | tf_op jit(solution)/shard_map/pallas_call | solution.py:452
  277.8 8.5 %shard_map.261.refs_11_ = bf16[1024,1024]{1,0:T(8,128)(2,1)} custom-call(bf16[2048,2048]{1,0:T(8,128)(2,1)} %get-tuple-element.95.refs_1_.refs_0_, bf16[4,128,1024]{2,1,0:T(8,128)(2,1)} %get-tuple-element.91.refs_8_.refs_1_, bf16[4,128,1024]{2,1,0:T(8,128)(2,1)} %get-tuple-element.92.refs_9_.refs_2_, ...), custom_call_target="tpu_custom_call" | custom-call | flops 1 | bytes 1 | tf_op jit(solution)/shard_map/pallas_call | solution.py:493
  286.4 34.6 %shard_map.262 = (bf16[2048,768]{1,0:T(8,128)(2,1)}, f32[4,1536]{1,0:T(4,128)}) custom-call(s32[9]{0:T(128)} %pad_add_fusion.refs_0_, bf16[2048,1536]{1,0:T(8,128)(2,1)} %shard_map.248.refs_1_, bf16[2048,512]{1,0:T(8,128)(2,1)} %get-tuple-element.81.refs_0_.refs_2_.mixed_ref, bf16[2048,512]{1,0:T(8,128)(2,1)} %shard_map.260.refs_5_.refs_3_, ...), custom_call_target="tpu_custom_call" | custom-call | flops 1 | bytes 1 | tf_op jit(solution)/shard_map/pallas_call | solution.py:316
  321.0 10.1 %shard_map.264 = (bf16[2,4,32,1024]{3,2,1,0:T(8,128)(2,1)}, bf16[2,4,32,1024]{3,2,1,0:T(8,128)(2,1)}, bf16[2,4,32,1024]{3,2,1,0:T(8,128)(2,1)}, bf16[2,4,32,1024]{3,2,1,0:T(8,128)(2,1)}) custom-call(s32[1]{0:T(128)} %bitcast.3.refs_0_.me_ref, bf16[2048,768]{1,0:T(8,128)(2,1)} %get-tuple-element.106.grads_ref.refs_0_, ...), custom_call_target="tpu_custom_call" | custom-call | flops 1 | bytes 1 | tf_op jit(solution)/shard_map/pallas_call | solution.py:599
  338.2 12.3 %collective-permute-start.26 = (bf16[2,256,1024]{2,1,0:T(8,128)(2,1)S(1)}, bf16[2,256,1024]{2,1,0:T(8,128)(2,1)}, u32[]{:S(2)}, u32[]{:S(2)}) collective-permute-start(bf16[2,256,1024]{2,1,0:T(8,128)(2,1)S(1)} %fusion.6.refs_11_), channel_id=1, source_target_pairs={{0,4},{1,5},{2,6},{3,7},{4,0},{5,1},{6,2},{7,3},{8,12},{9,13},{10,... | collective-permute-start | bytes 3145736 | tf_op jit(solution)/shard_map/ppermute | solution.py:614
  354.0 34.6 %shard_map.266 = (bf16[2048,768]{1,0:T(8,128)(2,1)}, f32[4,1536]{1,0:T(4,128)}) custom-call(s32[9]{0:T(128)} %pad_add_fusion.refs_0_, bf16[2048,1536]{1,0:T(8,128)(2,1)} %shard_map.248.refs_1_, bf16[2048,512]{1,0:T(8,128)(2,1)} %get-tuple-element.81.refs_0_.refs_2_.mixed_ref, bf16[2048,512]{1,0:T(8,128)(2,1)} %shard_map.260.refs_5_.refs_3_, ...), custom_call_target="tpu_custom_call" | custom-call | flops 1 | bytes 1 | tf_op jit(solution)/shard_map/pallas_call | solution.py:316
  388.6 7.3 %collective-permute-done.26.refs_1_ = bf16[2,256,1024]{2,1,0:T(8,128)(2,1)} collective-permute-done((bf16[2,256,1024]{2,1,0:T(8,128)(2,1)S(1)}, bf16[2,256,1024]{2,1,0:T(8,128)(2,1)}, u32[]{:S(2)}, u32[]{:S(2)}) %collective-permute-start.26) | collective-permute-done | bytes 1048608 | tf_op jit(solution)/shard_map/ppermute | solution.py:614
  397.3 10.0 %shard_map.268 = (bf16[2,4,32,1024]{3,2,1,0:T(8,128)(2,1)}, bf16[2,4,32,1024]{3,2,1,0:T(8,128)(2,1)}, bf16[2,4,32,1024]{3,2,1,0:T(8,128)(2,1)}, bf16[2,4,32,1024]{3,2,1,0:T(8,128)(2,1)}) custom-call(s32[1]{0:T(128)} %bitcast.3.refs_0_.me_ref, bf16[2048,768]{1,0:T(8,128)(2,1)} %get-tuple-element.125.grads_ref.refs_1_, ...), custom_call_target="tpu_custom_call" | custom-call | flops 1 | bytes 1 | tf_op jit(solution)/shard_map/pallas_call | solution.py:599
  410.9 7.3 %shard_map.270.refs_2_ = bf16[1024,1024]{1,0:T(8,128)(2,1)} custom-call(bf16[2048,768]{1,0:T(8,128)(2,1)} %get-tuple-element.106.grads_ref.refs_0_, bf16[2048,768]{1,0:T(8,128)(2,1)} %get-tuple-element.125.grads_ref.refs_1_, bf16[1536,1024]{1,0:T(8,128)(2,1)} %shard_map.269.refs_2_.refs_0_), custom_call_target="tpu_custom_call" | custom-call | flops 1 | bytes 1 | tf_op jit(solution)/shard_map/pallas_call | solution.py:493
  420.2 7.7 %shard_map.272.refs_4_.refs_3_ = f32[1024,1024]{1,0:T(8,128)} custom-call(bf16[2048,768]{1,0:T(8,128)(2,1)} %get-tuple-element.106.grads_ref.refs_0_, bf16[2048,768]{1,0:T(8,128)(2,1)} %get-tuple-element.125.grads_ref.refs_1_, bf16[1536,1024]{1,0:T(8,128)(2,1)} %get-tuple-element.131.refs_2_), custom_call_target="tpu_custom_call" | custom-call | flops 1 | bytes 1 | tf_op jit(solution)/shard_map/pallas_call | solution.py:493
  443.4 9.9 %shard_map.275.refs_5_ = bf16[1024,1024]{1,0:T(8,128)(2,1)} custom-call(bf16[2048,2048]{1,0:T(8,128)(2,1)} %get-tuple-element.95.refs_1_.refs_0_, bf16[4,128,1024]{2,1,0:T(8,128)(2,1)} %get-tuple-element.91.refs_8_.refs_1_, bf16[4,128,1024]{2,1,0:T(8,128)(2,1)} %get-tuple-element.92.refs_9_.refs_2_, ...), custom_call_target="tpu_custom_call" | custom-call | flops 1 | bytes 1 | tf_op jit(solution)/shard_map/pallas_call | solution.py:493
  453.3 7.7 %collective-permute-done.36.refs_7_.refs_1_ = bf16[256,1024]{1,0:T(8,128)(2,1)S(1)} collective-permute-done((bf16[256,1024]{1,0:T(8,128)(2,1)}, bf16[256,1024]{1,0:T(8,128)(2,1)S(1)}, u32[]{:S(2)}, u32[]{:S(2)}) %collective-permute-start.36) | collective-permute-done | bytes 524320 | tf_op jit(solution)/shard_map/ppermute | solution.py:620
  462.0 8.7 %shard_map.276 = (f32[1024,1024]{1,0:T(8,128)}, bf16[1024,1024]{1,0:T(8,128)(2,1)}, f32[8,1024]{1,0:T(8,128)}) custom-call(bf16[1024,1024]{1,0:T(8,128)(2,1)} %refs_0_.1, f32[1024,1024]{1,0:T(8,128)} %get-tuple-element.137.refs_1_, f32[1,1024]{1,0:T(1,128)} %bitcast.127, f32[1024,1024]{1,0:T(8,128)} %shard_map.272.refs_4_.refs_3_, ...), custom_call_target="tpu_custom_call" | custom-call | flops 1 | bytes 1 | tf_op jit(solution)/shard_map/pallas_call | solution.py:416
  (283 shorter events, 166.9 us)
Async XLA Ops:
  8.6 25.4 %collective-permute-start.4 = (bf16[144,1024]{1,0:T(8,128)(2,1)}, bf16[144,1024]{1,0:T(8,128)(2,1)}, u32[]{:S(2)}, u32[]{:S(2)}) collective-permute-start(bf16[144,1024]{1,0:T(8,128)(2,1)} %pad_maximum_fusion.8), channel_id=1, source_target_pairs={{0,4},{1,5},{2,6},{3,7},{4,0},{5,1},{6,2},{7,3},{8,12},{9,13},{10,... | collective-permute-start | bytes 884744 | tf_op jit(solution)/shard_map/ppermute | solution.py:614
  8.6 28.0 %collective-permute-start.1 = (bf16[144,1024]{1,0:T(8,128)(2,1)}, bf16[144,1024]{1,0:T(8,128)(2,1)}, u32[]{:S(2)}, u32[]{:S(2)}) collective-permute-start(bf16[144,1024]{1,0:T(8,128)(2,1)} %pad_maximum_fusion.8), channel_id=1, source_target_pairs={{0,2},{1,3},{2,0},{3,1},{4,6},{5,7},{6,4},{7,5},{8,10},{9,11},{10,... | collective-permute-start | bytes 884744 | tf_op jit(solution)/shard_map/ppermute | solution.py:614
  9.2 82.3 %collective-permute-start.8 = (bf16[1024,1024]{1,0:T(8,128)(2,1)}, bf16[1024,1024]{1,0:T(8,128)(2,1)}, u32[]{:S(2)}, u32[]{:S(2)}) collective-permute-start(bf16[1024,1024]{1,0:T(8,128)(2,1)} %refs_1_.1), channel_id=1, source_target_pairs={{0,1},{1,0},{2,3},{3,2},{4,5},{5,4},{6,7},{7,6},{8,9},{9,8},{10,11... | collective-permute-start | bytes 6291464 | tf_op jit(solution)/shard_map/ppermute | solution.py:614
  42.4 42.8 %collective-permute-start.10 = (bf16[256,1024]{1,0:T(8,128)(2,1)}, bf16[256,1024]{1,0:T(8,128)(2,1)}, u32[]{:S(2)}, u32[]{:S(2)}) collective-permute-start(bf16[256,1024]{1,0:T(8,128)(2,1)} %shard_map.246), channel_id=1, source_target_pairs={{0,4},{1,5},{2,6},{3,7},{4,0},{5,1},{6,2},{7,3},{8,12},{9,13},{10,... | collective-permute-start | bytes 1572872 | tf_op jit(solution)/shard_map/ppermute | solution.py:614
  48.1 39.4 %collective-permute-start.9 = (bf16[256,1024]{1,0:T(8,128)(2,1)}, bf16[256,1024]{1,0:T(8,128)(2,1)S(1)}, u32[]{:S(2)}, u32[]{:S(2)}) collective-permute-start(bf16[256,1024]{1,0:T(8,128)(2,1)} %shard_map.246), channel_id=1, source_target_pairs={{0,2},{1,3},{2,0},{3,1},{4,6},{5,7},{6,4},{7,5},{8,10},{9,11},{10,... | collective-permute-start | bytes 1572872 | tf_op jit(solution)/shard_map/ppermute | solution.py:614
  51.5 37.8 %collective-permute-start.7 = (bf16[2,2,128,1024]{3,2,1,0:T(8,128)(2,1)S(1)}, bf16[2,2,128,1024]{3,2,1,0:T(8,128)(2,1)S(1)}, u32[]{:S(2)}, u32[]{:S(2)}) collective-permute-start(bf16[2,2,128,1024]{3,2,1,0:T(8,128)(2,1)S(1)} %pad_maximum_fusion.2.refs_3_), channel_id=1, source_target_pairs={{0,8},{8,0},{16,24},{24,16},{1,9},{9,1},{17,25},{25,17},{2,10},{10... | collective-permute-start | bytes 3145736 | tf_op jit(solution)/shard_map/ppermute | solution.py:620
  57.0 32.9 %collective-permute-start.3 = (bf16[2,2,128,1024]{3,2,1,0:T(8,128)(2,1)S(1)}, bf16[2,2,128,1024]{3,2,1,0:T(8,128)(2,1)S(1)}, u32[]{:S(2)}, u32[]{:S(2)}) collective-permute-start(bf16[2,2,128,1024]{3,2,1,0:T(8,128)(2,1)S(1)} %pad_maximum_fusion.1.refs_1_), channel_id=1, source_target_pairs={{0,16},{8,24},{16,0},{24,8},{1,17},{9,25},{17,1},{25,9},{2,18},{10... | collective-permute-start | bytes 3145736 | tf_op jit(solution)/shard_map/ppermute | solution.py:620
  88.6 60.8 %collective-permute-start.13 = (bf16[4,128,1024]{2,1,0:T(8,128)(2,1)}, bf16[4,128,1024]{2,1,0:T(8,128)(2,1)}, u32[]{:S(2)}, u32[]{:S(2)}) collective-permute-start(bf16[4,128,1024]{2,1,0:T(8,128)(2,1)} %pad_maximum_fusion.3.refs_6_.refs_4_.refs_1_), channel_id=1, source_target_pairs={{0,16},{8,24},{16,0},{24,8},{1,17},{9,25},{17,1},{25,9},{2,18},{10... | collective-permute-start | bytes 3145736 | tf_op jit(solution)/shard_map/ppermute | solution.py:620
  89.3 60.1 %collective-permute-start.12 = (bf16[4,128,1024]{2,1,0:T(8,128)(2,1)}, bf16[4,128,1024]{2,1,0:T(8,128)(2,1)}, u32[]{:S(2)}, u32[]{:S(2)}) collective-permute-start(bf16[4,128,1024]{2,1,0:T(8,128)(2,1)} %pad_maximum_fusion.3.refs_6_.refs_4_.refs_1_), channel_id=1, source_target_pairs={{0,8},{8,0},{16,24},{24,16},{1,9},{9,1},{17,25},{25,17},{2,10},{10... | collective-permute-start | bytes 3145736 | tf_op jit(solution)/shard_map/ppermute | solution.py:620
  89.9 59.5 %collective-permute-start.15 = (bf16[4,128,1024]{2,1,0:T(8,128)(2,1)S(1)}, bf16[4,128,1024]{2,1,0:T(8,128)(2,1)}, u32[]{:S(2)}, u32[]{:S(2)}) collective-permute-start(bf16[4,128,1024]{2,1,0:T(8,128)(2,1)S(1)} %pad_maximum_fusion.4.refs_7_.refs_5_), channel_id=1, source_target_pairs={{0,16},{8,24},{16,0},{24,8},{1,17},{9,25},{17,1},{25,9},{2,18},{10... | collective-permute-start | bytes 3145736 | tf_op jit(solution)/shard_map/ppermute | solution.py:620
  91.4 58.0 %collective-permute-start.14 = (bf16[4,128,1024]{2,1,0:T(8,128)(2,1)S(1)}, bf16[4,128,1024]{2,1,0:T(8,128)(2,1)}, u32[]{:S(2)}, u32[]{:S(2)}) collective-permute-start(bf16[4,128,1024]{2,1,0:T(8,128)(2,1)S(1)} %pad_maximum_fusion.4.refs_7_.refs_5_), channel_id=1, source_target_pairs={{0,8},{8,0},{16,24},{24,16},{1,9},{9,1},{17,25},{25,17},{2,10},{10... | collective-permute-start | bytes 3145736 | tf_op jit(solution)/shard_map/ppermute | solution.py:620
  154.2 25.8 %collective-permute-start.17 = (bf16[4,128,1024]{2,1,0:T(8,128)(2,1)}, bf16[4,128,1024]{2,1,0:T(8,128)(2,1)S(1)}, u32[]{:S(2)}, u32[]{:S(2)}) collective-permute-start(bf16[4,128,1024]{2,1,0:T(8,128)(2,1)} %get-tuple-element.82.refs_2_), channel_id=1, source_target_pairs={{0,16},{8,24},{16,0},{24,8},{1,17},{9,25},{17,1},{25,9},{2,18},{10... | collective-permute-start | bytes 3145736 | tf_op jit(solution)/shard_map/ppermute | solution.py:620
  154.2 25.8 %collective-permute-start.18 = (bf16[4,128,1024]{2,1,0:T(8,128)(2,1)}, bf16[4,128,1024]{2,1,0:T(8,128)(2,1)S(1)}, u32[]{:S(2)}, u32[]{:S(2)}) collective-permute-start(bf16[4,128,1024]{2,1,0:T(8,128)(2,1)} %get-tuple-element.85.refs_7_), channel_id=1, source_target_pairs={{0,8},{8,0},{16,24},{24,16},{1,9},{9,1},{17,25},{25,17},{2,10},{10... | collective-permute-start | bytes 3145736 | tf_op jit(solution)/shard_map/ppermute | solution.py:620
  236.6 84.4 %all-to-all-start = ((bf16[4,512,1024]{2,1,0:T(8,128)(2,1)}), bf16[4,512,1024]{2,1,0:T(8,128)(2,1)}, u32[]{:S(2)}, u32[]{:S(2)}) async-start(bf16[4,512,1024]{2,1,0:T(8,128)(2,1)} %bitcast.103), calls=%async_computation | async-start | bytes 8388608 | tf_op jit(solution)/shard_map/all_to_all | solution.py:654
  266.1 68.4 %collective-permute-start.23 = (bf16[512,1024]{1,0:T(8,128)(2,1)}, bf16[512,1024]{1,0:T(8,128)(2,1)}, u32[]{:S(2)}, u32[]{:S(2)}) collective-permute-start(bf16[512,1024]{1,0:T(8,128)(2,1)} %get-tuple-element.101.refs_2_.refs_8_), channel_id=1, source_target_pairs={{0,8},{8,0},{16,24},{24,16},{1,9},{9,1},{17,25},{25,17},{2,10},{10... | collective-permute-start | bytes 3145736 | tf_op jit(solution)/shard_map/ppermute | solution.py:620
  267.8 66.7 %collective-permute-start.24 = (bf16[512,1024]{1,0:T(8,128)(2,1)}, bf16[512,1024]{1,0:T(8,128)(2,1)}, u32[]{:S(2)}, u32[]{:S(2)}) collective-permute-start(bf16[512,1024]{1,0:T(8,128)(2,1)} %get-tuple-element.102.refs_3_.refs_9_), channel_id=1, source_target_pairs={{0,16},{8,24},{16,0},{24,8},{1,17},{9,25},{17,1},{25,9},{2,18},{10... | collective-permute-start | bytes 3145736 | tf_op jit(solution)/shard_map/ppermute | solution.py:620
  269.2 66.4 %collective-permute-start.25 = (bf16[512,1024]{1,0:T(8,128)(2,1)}, bf16[512,1024]{1,0:T(8,128)(2,1)}, u32[]{:S(2)}, u32[]{:S(2)}) collective-permute-start(bf16[512,1024]{1,0:T(8,128)(2,1)} %get-tuple-element.103.refs_4_.refs_10_), channel_id=1, source_target_pairs={{0,24},{8,16},{16,8},{24,0},{1,25},{9,17},{17,9},{25,1},{2,26},{10... | collective-permute-start | bytes 3145736 | tf_op jit(solution)/shard_map/ppermute | solution.py:620
  338.2 57.8 %collective-permute-start.26 = (bf16[2,256,1024]{2,1,0:T(8,128)(2,1)S(1)}, bf16[2,256,1024]{2,1,0:T(8,128)(2,1)}, u32[]{:S(2)}, u32[]{:S(2)}) collective-permute-start(bf16[2,256,1024]{2,1,0:T(8,128)(2,1)S(1)} %fusion.6.refs_11_), channel_id=1, source_target_pairs={{0,4},{1,5},{2,6},{3,7},{4,0},{5,1},{6,2},{7,3},{8,12},{9,13},{10,... | collective-permute-start | bytes 3145736 | tf_op jit(solution)/shard_map/ppermute | solution.py:614
  350.5 38.1 %collective-permute-start.27 = (bf16[2,4,32,1024]{3,2,1,0:T(8,128)(2,1)}, bf16[2,4,32,1024]{3,2,1,0:T(8,128)(2,1)S(1)}, u32[]{:S(2)}, u32[]{:S(2)}) collective-permute-start(bf16[2,4,32,1024]{3,2,1,0:T(8,128)(2,1)} %get-tuple-element.112.refs_8_), channel_id=1, source_target_pairs={{0,8},{8,0},{16,24},{24,16},{1,9},{9,1},{17,25},{25,17},{2,10},{10... | collective-permute-start | bytes 1572872 | tf_op jit(solution)/shard_map/ppermute | solution.py:620
  351.1 37.5 %collective-permute-start.28 = (bf16[2,4,32,1024]{3,2,1,0:T(8,128)(2,1)}, bf16[2,4,32,1024]{3,2,1,0:T(8,128)(2,1)}, u32[]{:S(2)}, u32[]{:S(2)}) collective-permute-start(bf16[2,4,32,1024]{3,2,1,0:T(8,128)(2,1)} %get-tuple-element.113.refs_9_), channel_id=1, source_target_pairs={{0,16},{8,24},{16,0},{24,8},{1,17},{9,25},{17,1},{25,9},{2,18},{10... | collective-permute-start | bytes 1572872 | tf_op jit(solution)/shard_map/ppermute | solution.py:620
  351.6 37.0 %collective-permute-start.29 = (bf16[2,4,32,1024]{3,2,1,0:T(8,128)(2,1)}, bf16[2,4,32,1024]{3,2,1,0:T(8,128)(2,1)}, u32[]{:S(2)}, u32[]{:S(2)}) collective-permute-start(bf16[2,4,32,1024]{3,2,1,0:T(8,128)(2,1)} %get-tuple-element.114.refs_10_), channel_id=1, source_target_pairs={{0,24},{8,16},{16,8},{24,0},{1,25},{9,17},{17,9},{25,1},{2,26},{10... | collective-permute-start | bytes 1572872 | tf_op jit(solution)/shard_map/ppermute | solution.py:620
  410.9 31.2 %collective-permute-start.22 = (bf16[1024,1024]{1,0:T(8,128)(2,1)}, bf16[1024,1024]{1,0:T(8,128)(2,1)}, u32[]{:S(2)}, u32[]{:S(2)}) collective-permute-start(bf16[1024,1024]{1,0:T(8,128)(2,1)} %shard_map.261.refs_11_), channel_id=1, source_target_pairs={{0,1},{1,0},{2,3},{3,2},{4,5},{5,4},{6,7},{7,6},{8,9},{9,8},{10,11... | collective-permute-start | bytes 6291464 | tf_op jit(solution)/shard_map/ppermute | solution.py:614
  418.2 42.9 %collective-permute-start.34 = (bf16[1024,1024]{1,0:T(8,128)(2,1)}, bf16[1024,1024]{1,0:T(8,128)(2,1)}, u32[]{:S(2)}, u32[]{:S(2)}) collective-permute-start(bf16[1024,1024]{1,0:T(8,128)(2,1)} %shard_map.270.refs_2_), channel_id=1, source_target_pairs={{0,1},{1,0},{2,3},{3,2},{4,5},{5,4},{6,7},{7,6},{8,9},{9,8},{10,11... | collective-permute-start | bytes 6291464 | tf_op jit(solution)/shard_map/ppermute | solution.py:614
  442.0 29.6 %collective-permute-start.42 = (bf16[2,4,32,1024]{3,2,1,0:T(8,128)(2,1)}, bf16[2,4,32,1024]{3,2,1,0:T(8,128)(2,1)S(1)}, u32[]{:S(2)}, u32[]{:S(2)}) collective-permute-start(bf16[2,4,32,1024]{3,2,1,0:T(8,128)(2,1)} %pad_maximum_fusion.7.refs_1_.refs_7_), channel_id=1, source_target_pairs={{0,4},{1,5},{2,6},{3,7},{4,0},{5,1},{6,2},{7,3},{8,12},{9,13},{10,... | collective-permute-start | bytes 1572872 | tf_op jit(solution)/shard_map/ppermute | solution.py:614
  (61 other events, 653.3 us)

commit v5 on v4

--- a/solution.py
+++ b/solution.py
@@ -931,7 +931,7 @@
     normed1_part = [product(all_grads, s, tokens, [w_late], [], bf16) for s in range(1, group)]
     normed1_away = [net.from_group(part, s + 1) for s, part in enumerate(normed1_part)]
     w_late, ffn_ring.arrived = after((w_late, ffn_ring.arrived), normed1_part)
-    normed1_own = product(all_grads, 0, tokens, [w_late], [], f32)
+    normed1_own = product(all_grads, 0, tokens, [w_late], [], bf16)
     parts_b = after(parts_b, normed1_own)
     head_low = jnp.concatenate([sum_low(jnp.stack(parts_a)), sum_low(jnp.stack(parts_b))], axis=0)
     head_ring = RingSum(net, by_xor([head_low[z] for z in range(ring)], me_ring)).send()
@@ -956,18 +956,18 @@
     small_own = small
     small = jnp.pad(small, (0, pad)).reshape(-1, 128)
     small = small + sum(net.from_group(small, s) for s in range(1, group))
-    small = small + sum(net.from_wide(small, s) for s in range(1, wide))
+    small_away = [net.from_wide(small, s) for s in range(1, wide)]
     head_ring.arrived = after(head_ring.arrived, small_own)
     head_ring.add().send()
-    small, head_gone = after((small, head_ring.gone))
+    attention_part = head_ring.add().parts[0]
+    attention_part = jnp.broadcast_to(attention_part[None], (wide,) + attention_part.shape)
+    small = small + sum(after(small_away, attention_part))
     small = small + sum(net.from_ring(small, r) for r in range(1, ring))
     small = small.reshape(-1)
     gain1, shift1, gain2, shift2 = (small[k * width : (k + 1) * width] for k in range(4))
     table_sum = small[4 * width : 4 * width + table_all.size].reshape(table_all.shape)
     table_out = lax.dynamic_slice_in_dim(table_sum, me_narrow * heads_here, heads_here, 0).T
 
-    attention_part = head_ring.add().parts[0]
-    attention_part = jnp.broadcast_to(after(attention_part, small_own)[None], (wide,) + attention_part.shape)
     ffn_pieces = after(ffn_pieces, attention_part)
     ffn_all = jnp.stack(by_xor([ffn_part] + ffn_pieces, me_wide), axis=0)
     down_all = ffn_all[:, :unit].reshape(-1, width).astype(f32)

time: 518 us -> 512 us (0.988)
  waiting for transfers between devices: 99 us -> 93.6 us
  transfers between devices with their start and end apart: 49 -> 49, of which waited for: 17 -> 15; matrix products, arithmetic and copies ran while one was open for 11% -> 11% of each run, Pallas kernels for 45% -> 45%
where the time goes in v5:
time: 512 us; the launch traced here: 505 us
  Pallas kernels  267 us (52%)
  waiting for transfers between devices  93.6 us (18%)
  starting transfers between devices  68 us (13%)
  other arithmetic  45.3 us (9%)
  local copies, waits for them, and re-layouts  27.4 us (5%)
    pallas_call x2, Pallas kernels, attend_back(): pl.pallas_call(ignoring(functools.partial(attend_back_kernel, block=block...  67.2 us
    ppermute x22, waiting for transfers between devices, from_group(): lax.ppermute(value, 'narrow', [(i, i ^ s) for i in range(self.narrow)])  64.2 us
    pallas_call x6, Pallas kernels, product(): pl.pallas_call(ignoring(functools.partial(product_kernel, parts=len(parts...  44 us
    pallas_call x1, Pallas kernels, hidden_units(): pl.pallas_call(functools.partial(hidden_kernel, slots=slots, blocks=block...  36 us
    pallas_call x1, Pallas kernels, attend(): pl.pallas_call(ignoring(functools.partial(attend_kernel, block=block, per...  30.8 us
    ppermute x22, starting transfers between devices, from_group(): lax.ppermute(value, 'narrow', [(i, i ^ s) for i in range(self.narrow)])  30.5 us
    ppermute x25, waiting for transfers between devices, from_wide(): return lax.ppermute(value, 'wide', [(i, i ^ s) for i in range(self.wide)])  29.4 us
    ppermute x25, starting transfers between devices, from_wide(): return lax.ppermute(value, 'wide', [(i, i ^ s) for i in range(self.wide)])  28.3 us
  transfers between devices with their start and end apart: 49, of which 15 were waited for; matrix products, arithmetic and copies ran while one was open for 11% of the time, Pallas kernels for 45%

profile of v5, /device:TPU:0, one launch (start us, length us, event | category | flops | bytes accessed | tf_op | source)
XLA Modules:
  0.0 504.6 jit_solution(16750759075514362446)
XLA Ops:
  3.5 5.0 %collective-permute-start.5 = (bf16[144,1024]{1,0:T(8,128)(2,1)}, bf16[144,1024]{1,0:T(8,128)(2,1)}, u32[]{:S(2)}, u32[]{:S(2)}) collective-permute-start(bf16[144,1024]{1,0:T(8,128)(2,1)} %pad_maximum_fusion.8), channel_id=1, source_target_pairs={{0,6},{1,7},{2,4},{3,5},{4,2},{5,3},{6,0},{7,1},{8,14},{9,15},{10,... | collective-permute-start | bytes 884744 | tf_op jit(solution)/shard_map/ppermute | solution.py:614
  18.0 16.0 %collective-permute-done.4.refs_2_ = bf16[144,1024]{1,0:T(8,128)(2,1)} collective-permute-done((bf16[144,1024]{1,0:T(8,128)(2,1)}, bf16[144,1024]{1,0:T(8,128)(2,1)}, u32[]{:S(2)}, u32[]{:S(2)}) %collective-permute-start.4) | collective-permute-done | bytes 294944 | tf_op jit(solution)/shard_map/ppermute | solution.py:614
  57.6 27.7 %collective-permute-done.10 = bf16[256,1024]{1,0:T(8,128)(2,1)} collective-permute-done((bf16[256,1024]{1,0:T(8,128)(2,1)}, bf16[256,1024]{1,0:T(8,128)(2,1)}, u32[]{:S(2)}, u32[]{:S(2)}) %collective-permute-start.10) | collective-permute-done | bytes 524320 | tf_op jit(solution)/shard_map/ppermute | solution.py:614
  103.0 11.4 %shard_map.248.refs_1_ = bf16[2048,1536]{1,0:T(8,128)(2,1)} custom-call(bf16[1024,1024]{1,0:T(8,128)(2,1)} %fusion.5.refs_0_, bf16[1024,1024]{1,0:T(8,128)(2,1)} %collective-permute-done.refs_1_, bf16[1536,1024]{1,0:T(8,128)(2,1)} %shard_map.247.refs_2_.refs_0_, f32[1,1536]{1,0:T(1,128)} %compare_select_fusion.refs_3_), custom_call_target="tpu_custom_call" | custom-call | flops 1 | bytes 1 | tf_op jit(solution)/shard_map/pallas_call | solution.py:452
  117.7 30.8 %shard_map.249 = (bf16[2048,512]{1,0:T(8,128)(2,1)}, f32[8,8,256]{2,1,0:T(8,128)}) custom-call(s32[9]{0:T(128)} %pad_add_fusion.refs_0_, bf16[2048,1536]{1,0:T(8,128)(2,1)} %shard_map.248.refs_1_, s32[8,256]{1,0:T(8,128)} %reshape.221.refs_2_.refs_4_, f32[8,1536]{1,0:T(8,128)} %concatenate.36.refs_3_.refs_5_, ...), custom_call_target="tpu_custom_call" | custom-call | flops 1 | bytes 1 | tf_op jit(solution)/shard_map/pallas_call | solution.py:278
  157.8 6.2 %shard_map.253.refs_0_.refs_5_ = f32[1024,1024]{1,0:T(8,128)} custom-call(bf16[2048,512]{1,0:T(8,128)(2,1)} %get-tuple-element.83.refs_0_.refs_2_.mixed_ref, bf16[512,1024]{1,0:T(8,128)(2,1)} %shard_map.251.refs_1_.refs_2_, bf16[1024,1024]{1,0:T(8,128)(2,1)} %refs_0_.1, bf16[1024,1024]{1,0:T(8,128)(2,1)} %collective-permute-done.16.refs_3_), custom_call_target="tpu_custom_call" | custom-call | flops 1 | bytes 1 | tf_op jit(solution)/shard_map/pallas_call | solution.py:493
  171.9 7.2 %collective-permute-done.17.refs_4_ = bf16[4,128,1024]{2,1,0:T(8,128)(2,1)S(1)} collective-permute-done((bf16[4,128,1024]{2,1,0:T(8,128)(2,1)}, bf16[4,128,1024]{2,1,0:T(8,128)(2,1)S(1)}, u32[]{:S(2)}, u32[]{:S(2)}) %collective-permute-start.17) | collective-permute-done | bytes 1048608 | tf_op jit(solution)/shard_map/ppermute | solution.py:620
  186.3 36.0 %shard_map.255 = (bf16[2048,2048]{1,0:T(8,128)(2,1)}, bf16[2048,2048]{1,0:T(8,128)(2,1)}, bf16[1024,1024]{1,0:T(8,128)(2,1)}, bf16[1024,1024]{1,0:T(8,128)(2,1)}) custom-call(bf16[1024,1024]{1,0:T(8,128)(2,1)} %get-tuple-element.88.refs_0_.refs_2_, bf16[1024,1024]{1,0:T(8,128)(2,1)} %copy-done.12, bf16[1024,1024]{1,0:T(8,128)(2,1)} %refs_1_.1, ...), custom_call_target="tpu_custom_call" | custom-call | flops 1 | bytes 1 | tf_op jit(solution)/shard_map/pallas_call | solution.py:377
  222.5 13.4 %shard_map.256 = bf16[2048,1024]{1,0:T(8,128)(2,1)} custom-call(s32[1]{0:T(128)} %bitcast.3.refs_0_.me_ref, bf16[2048,2048]{1,0:T(8,128)(2,1)} %get-tuple-element.97.refs_1_.refs_0_, bf16[1024,1024]{1,0:T(8,128)(2,1)} %refs_1_.1, bf16[1024,1024]{1,0:T(8,128)(2,1)} %collective-permute-done.8.refs_5_.refs_3_), custom_call_target="tpu_custom_call" | custom-call | flops 1 | bytes 1 | tf_op jit(solution)/shard_map/pallas_call | solution.py:552
  242.2 7.8 %shard_map.257 = (f32[1024,1024]{1,0:T(8,128)}, bf16[1024,1024]{1,0:T(8,128)(2,1)}, f32[8,1024]{1,0:T(8,128)}) custom-call(f32[1024,1024]{1,0:T(8,128)} %shard_map.253.refs_0_.refs_5_, bf16[1024,1024]{1,0:T(8,128)(2,1)} %refs_1_.1, f32[1,1024]{1,0:T(1,128)} %bitcast.127, bf16[1024,1024]{1,0:T(8,128)(2,1)} %get-tuple-element.98.refs_3_, ...), custom_call_target="tpu_custom_call" | custom-call | flops 1 | bytes 1 | tf_op jit(solution)/shard_map/pallas_call | solution.py:416
  250.4 14.8 %shard_map.258 = (bf16[512,1024]{1,0:T(8,128)(2,1)}, bf16[512,1024]{1,0:T(8,128)(2,1)}, bf16[512,1024]{1,0:T(8,128)(2,1)}, bf16[512,1024]{1,0:T(8,128)(2,1)}) custom-call(s32[1]{0:T(128)} %constant.105.clone.1.refs_0_, bf16[2048,2048]{1,0:T(8,128)(2,1)} %get-tuple-element.101.refs_1_, bf16[1024,1024]{1,0:T(8,128)(2,1)} %get-tuple-element.88.refs_0_.refs_2_, ...), custom_call_target="tpu_custom_call" | custom-call | flops 1 | bytes 1 | tf_op jit(solution)/shard_map/pallas_call | solution.py:552
  270.6 6.4 %shard_map.260.refs_5_.refs_3_ = bf16[2048,512]{1,0:T(8,128)(2,1)} custom-call(bf16[1024,1024]{1,0:T(8,128)(2,1)} %get-tuple-element.100.refs_4_.refs_0_.refs_2_, bf16[1024,1024]{1,0:T(8,128)(2,1)} %shard_map.259.refs_1_.refs_3_, bf16[512,1024]{1,0:T(8,128)(2,1)} %shard_map.251.refs_1_.refs_2_, f32[1,512]{1,0:T(1,128)} %broadcast_in_dim.52.refs_3_), custom_call_target="tpu_custom_call" | custom-call | flops 1 | bytes 1 | tf_op jit(solution)/shard_map/pallas_call | solution.py:452
  277.0 8.5 %shard_map.261.refs_11_ = bf16[1024,1024]{1,0:T(8,128)(2,1)} custom-call(bf16[2048,2048]{1,0:T(8,128)(2,1)} %get-tuple-element.97.refs_1_.refs_0_, bf16[4,128,1024]{2,1,0:T(8,128)(2,1)} %get-tuple-element.93.refs_8_.refs_1_, bf16[4,128,1024]{2,1,0:T(8,128)(2,1)} %get-tuple-element.94.refs_9_.refs_2_, ...), custom_call_target="tpu_custom_call" | custom-call | flops 1 | bytes 1 | tf_op jit(solution)/shard_map/pallas_call | solution.py:493
  285.5 33.6 %shard_map.262 = (bf16[2048,768]{1,0:T(8,128)(2,1)}, f32[4,1536]{1,0:T(4,128)}) custom-call(s32[9]{0:T(128)} %pad_add_fusion.refs_0_, bf16[2048,1536]{1,0:T(8,128)(2,1)} %shard_map.248.refs_1_, bf16[2048,512]{1,0:T(8,128)(2,1)} %get-tuple-element.83.refs_0_.refs_2_.mixed_ref, bf16[2048,512]{1,0:T(8,128)(2,1)} %shard_map.260.refs_5_.refs_3_, ...), custom_call_target="tpu_custom_call" | custom-call | flops 1 | bytes 1 | tf_op jit(solution)/shard_map/pallas_call | solution.py:316
  319.0 10.1 %shard_map.264 = (bf16[2,4,32,1024]{3,2,1,0:T(8,128)(2,1)}, bf16[2,4,32,1024]{3,2,1,0:T(8,128)(2,1)}, bf16[2,4,32,1024]{3,2,1,0:T(8,128)(2,1)}, bf16[2,4,32,1024]{3,2,1,0:T(8,128)(2,1)}) custom-call(s32[1]{0:T(128)} %bitcast.3.refs_0_.me_ref, bf16[2048,768]{1,0:T(8,128)(2,1)} %get-tuple-element.108.grads_ref.refs_0_, ...), custom_call_target="tpu_custom_call" | custom-call | flops 1 | bytes 1 | tf_op jit(solution)/shard_map/pallas_call | solution.py:599
  337.4 12.5 %collective-permute-start.26 = (bf16[2,256,1024]{2,1,0:T(8,128)(2,1)S(1)}, bf16[2,256,1024]{2,1,0:T(8,128)(2,1)}, u32[]{:S(2)}, u32[]{:S(2)}) collective-permute-start(bf16[2,256,1024]{2,1,0:T(8,128)(2,1)S(1)} %fusion.6.refs_11_), channel_id=1, source_target_pairs={{0,4},{1,5},{2,6},{3,7},{4,0},{5,1},{6,2},{7,3},{8,12},{9,13},{10,... | collective-permute-start | bytes 3145736 | tf_op jit(solution)/shard_map/ppermute | solution.py:614
  353.4 33.6 %shard_map.266 = (bf16[2048,768]{1,0:T(8,128)(2,1)}, f32[4,1536]{1,0:T(4,128)}) custom-call(s32[9]{0:T(128)} %pad_add_fusion.refs_0_, bf16[2048,1536]{1,0:T(8,128)(2,1)} %shard_map.248.refs_1_, bf16[2048,512]{1,0:T(8,128)(2,1)} %get-tuple-element.83.refs_0_.refs_2_.mixed_ref, bf16[2048,512]{1,0:T(8,128)(2,1)} %shard_map.260.refs_5_.refs_3_, ...), custom_call_target="tpu_custom_call" | custom-call | flops 1 | bytes 1 | tf_op jit(solution)/shard_map/pallas_call | solution.py:316
  387.0 8.3 %collective-permute-done.26.refs_1_ = bf16[2,256,1024]{2,1,0:T(8,128)(2,1)} collective-permute-done((bf16[2,256,1024]{2,1,0:T(8,128)(2,1)S(1)}, bf16[2,256,1024]{2,1,0:T(8,128)(2,1)}, u32[]{:S(2)}, u32[]{:S(2)}) %collective-permute-start.26) | collective-permute-done | bytes 1048608 | tf_op jit(solution)/shard_map/ppermute | solution.py:614
  396.7 10.0 %shard_map.268 = (bf16[2,4,32,1024]{3,2,1,0:T(8,128)(2,1)}, bf16[2,4,32,1024]{3,2,1,0:T(8,128)(2,1)}, bf16[2,4,32,1024]{3,2,1,0:T(8,128)(2,1)}, bf16[2,4,32,1024]{3,2,1,0:T(8,128)(2,1)}) custom-call(s32[1]{0:T(128)} %bitcast.3.refs_0_.me_ref, bf16[2048,768]{1,0:T(8,128)(2,1)} %get-tuple-element.127.grads_ref.refs_1_, ...), custom_call_target="tpu_custom_call" | custom-call | flops 1 | bytes 1 | tf_op jit(solution)/shard_map/pallas_call | solution.py:599
  410.3 7.3 %shard_map.270.refs_2_ = bf16[1024,1024]{1,0:T(8,128)(2,1)} custom-call(bf16[2048,768]{1,0:T(8,128)(2,1)} %get-tuple-element.108.grads_ref.refs_0_, bf16[2048,768]{1,0:T(8,128)(2,1)} %get-tuple-element.127.grads_ref.refs_1_, bf16[1536,1024]{1,0:T(8,128)(2,1)} %shard_map.269.refs_2_.refs_0_), custom_call_target="tpu_custom_call" | custom-call | flops 1 | bytes 1 | tf_op jit(solution)/shard_map/pallas_call | solution.py:493
  419.6 7.3 %shard_map.272.refs_4_.refs_3_ = bf16[1024,1024]{1,0:T(8,128)(2,1)} custom-call(bf16[2048,768]{1,0:T(8,128)(2,1)} %get-tuple-element.108.grads_ref.refs_0_, bf16[2048,768]{1,0:T(8,128)(2,1)} %get-tuple-element.127.grads_ref.refs_1_, bf16[1536,1024]{1,0:T(8,128)(2,1)} %get-tuple-element.133.refs_2_), custom_call_target="tpu_custom_call" | custom-call | flops 1 | bytes 1 | tf_op jit(solution)/shard_map/pallas_call | solution.py:493
  444.0 9.9 %shard_map.275.refs_5_ = bf16[1024,1024]{1,0:T(8,128)(2,1)} custom-call(bf16[2048,2048]{1,0:T(8,128)(2,1)} %get-tuple-element.97.refs_1_.refs_0_, bf16[4,128,1024]{2,1,0:T(8,128)(2,1)} %get-tuple-element.93.refs_8_.refs_1_, bf16[4,128,1024]{2,1,0:T(8,128)(2,1)} %get-tuple-element.94.refs_9_.refs_2_, ...), custom_call_target="tpu_custom_call" | custom-call | flops 1 | bytes 1 | tf_op jit(solution)/shard_map/pallas_call | solution.py:493
  453.9 6.4 %collective-permute-done.36.refs_7_.refs_1_ = bf16[256,1024]{1,0:T(8,128)(2,1)S(1)} collective-permute-done((bf16[256,1024]{1,0:T(8,128)(2,1)}, bf16[256,1024]{1,0:T(8,128)(2,1)S(1)}, u32[]{:S(2)}, u32[]{:S(2)}) %collective-permute-start.36) | collective-permute-done | bytes 524320 | tf_op jit(solution)/shard_map/ppermute | solution.py:620
  461.3 8.4 %shard_map.276 = (f32[1024,1024]{1,0:T(8,128)}, bf16[1024,1024]{1,0:T(8,128)(2,1)}, f32[8,1024]{1,0:T(8,128)}) custom-call(bf16[1024,1024]{1,0:T(8,128)(2,1)} %refs_0_.1, f32[1024,1024]{1,0:T(8,128)} %get-tuple-element.139.refs_1_, f32[1,1024]{1,0:T(1,128)} %bitcast.128, bf16[1024,1024]{1,0:T(8,128)(2,1)} %shard_map.272.refs_4_.refs_3_, ...), custom_call_target="tpu_custom_call" | custom-call | flops 1 | bytes 1 | tf_op jit(solution)/shard_map/pallas_call | solution.py:416
  (284 shorter events, 164.3 us)
Async XLA Ops:
  8.6 25.4 %collective-permute-start.4 = (bf16[144,1024]{1,0:T(8,128)(2,1)}, bf16[144,1024]{1,0:T(8,128)(2,1)}, u32[]{:S(2)}, u32[]{:S(2)}) collective-permute-start(bf16[144,1024]{1,0:T(8,128)(2,1)} %pad_maximum_fusion.8), channel_id=1, source_target_pairs={{0,4},{1,5},{2,6},{3,7},{4,0},{5,1},{6,2},{7,3},{8,12},{9,13},{10,... | collective-permute-start | bytes 884744 | tf_op jit(solution)/shard_map/ppermute | solution.py:614
  8.6 28.0 %collective-permute-start.1 = (bf16[144,1024]{1,0:T(8,128)(2,1)}, bf16[144,1024]{1,0:T(8,128)(2,1)}, u32[]{:S(2)}, u32[]{:S(2)}) collective-permute-start(bf16[144,1024]{1,0:T(8,128)(2,1)} %pad_maximum_fusion.8), channel_id=1, source_target_pairs={{0,2},{1,3},{2,0},{3,1},{4,6},{5,7},{6,4},{7,5},{8,10},{9,11},{10,... | collective-permute-start | bytes 884744 | tf_op jit(solution)/shard_map/ppermute | solution.py:614
  9.2 82.3 %collective-permute-start.8 = (bf16[1024,1024]{1,0:T(8,128)(2,1)}, bf16[1024,1024]{1,0:T(8,128)(2,1)}, u32[]{:S(2)}, u32[]{:S(2)}) collective-permute-start(bf16[1024,1024]{1,0:T(8,128)(2,1)} %refs_1_.1), channel_id=1, source_target_pairs={{0,1},{1,0},{2,3},{3,2},{4,5},{5,4},{6,7},{7,6},{8,9},{9,8},{10,11... | collective-permute-start | bytes 6291464 | tf_op jit(solution)/shard_map/ppermute | solution.py:614
  42.4 42.8 %collective-permute-start.10 = (bf16[256,1024]{1,0:T(8,128)(2,1)}, bf16[256,1024]{1,0:T(8,128)(2,1)}, u32[]{:S(2)}, u32[]{:S(2)}) collective-permute-start(bf16[256,1024]{1,0:T(8,128)(2,1)} %shard_map.246), channel_id=1, source_target_pairs={{0,4},{1,5},{2,6},{3,7},{4,0},{5,1},{6,2},{7,3},{8,12},{9,13},{10,... | collective-permute-start | bytes 1572872 | tf_op jit(solution)/shard_map/ppermute | solution.py:614
  48.1 39.4 %collective-permute-start.9 = (bf16[256,1024]{1,0:T(8,128)(2,1)}, bf16[256,1024]{1,0:T(8,128)(2,1)S(1)}, u32[]{:S(2)}, u32[]{:S(2)}) collective-permute-start(bf16[256,1024]{1,0:T(8,128)(2,1)} %shard_map.246), channel_id=1, source_target_pairs={{0,2},{1,3},{2,0},{3,1},{4,6},{5,7},{6,4},{7,5},{8,10},{9,11},{10,... | collective-permute-start | bytes 1572872 | tf_op jit(solution)/shard_map/ppermute | solution.py:614
  51.5 37.8 %collective-permute-start.7 = (bf16[2,2,128,1024]{3,2,1,0:T(8,128)(2,1)S(1)}, bf16[2,2,128,1024]{3,2,1,0:T(8,128)(2,1)S(1)}, u32[]{:S(2)}, u32[]{:S(2)}) collective-permute-start(bf16[2,2,128,1024]{3,2,1,0:T(8,128)(2,1)S(1)} %pad_maximum_fusion.2.refs_3_), channel_id=1, source_target_pairs={{0,8},{8,0},{16,24},{24,16},{1,9},{9,1},{17,25},{25,17},{2,10},{10... | collective-permute-start | bytes 3145736 | tf_op jit(solution)/shard_map/ppermute | solution.py:620
  57.0 32.9 %collective-permute-start.3 = (bf16[2,2,128,1024]{3,2,1,0:T(8,128)(2,1)S(1)}, bf16[2,2,128,1024]{3,2,1,0:T(8,128)(2,1)S(1)}, u32[]{:S(2)}, u32[]{:S(2)}) collective-permute-start(bf16[2,2,128,1024]{3,2,1,0:T(8,128)(2,1)S(1)} %pad_maximum_fusion.1.refs_1_), channel_id=1, source_target_pairs={{0,16},{8,24},{16,0},{24,8},{1,17},{9,25},{17,1},{25,9},{2,18},{10... | collective-permute-start | bytes 3145736 | tf_op jit(solution)/shard_map/ppermute | solution.py:620
  88.6 59.8 %collective-permute-start.13 = (bf16[4,128,1024]{2,1,0:T(8,128)(2,1)}, bf16[4,128,1024]{2,1,0:T(8,128)(2,1)}, u32[]{:S(2)}, u32[]{:S(2)}) collective-permute-start(bf16[4,128,1024]{2,1,0:T(8,128)(2,1)} %pad_maximum_fusion.3.refs_6_.refs_4_.refs_1_), channel_id=1, source_target_pairs={{0,16},{8,24},{16,0},{24,8},{1,17},{9,25},{17,1},{25,9},{2,18},{10... | collective-permute-start | bytes 3145736 | tf_op jit(solution)/shard_map/ppermute | solution.py:620
  89.3 59.2 %collective-permute-start.12 = (bf16[4,128,1024]{2,1,0:T(8,128)(2,1)}, bf16[4,128,1024]{2,1,0:T(8,128)(2,1)}, u32[]{:S(2)}, u32[]{:S(2)}) collective-permute-start(bf16[4,128,1024]{2,1,0:T(8,128)(2,1)} %pad_maximum_fusion.3.refs_6_.refs_4_.refs_1_), channel_id=1, source_target_pairs={{0,8},{8,0},{16,24},{24,16},{1,9},{9,1},{17,25},{25,17},{2,10},{10... | collective-permute-start | bytes 3145736 | tf_op jit(solution)/shard_map/ppermute | solution.py:620
  89.9 58.6 %collective-permute-start.15 = (bf16[4,128,1024]{2,1,0:T(8,128)(2,1)S(1)}, bf16[4,128,1024]{2,1,0:T(8,128)(2,1)}, u32[]{:S(2)}, u32[]{:S(2)}) collective-permute-start(bf16[4,128,1024]{2,1,0:T(8,128)(2,1)S(1)} %pad_maximum_fusion.4.refs_7_.refs_5_), channel_id=1, source_target_pairs={{0,16},{8,24},{16,0},{24,8},{1,17},{9,25},{17,1},{25,9},{2,18},{10... | collective-permute-start | bytes 3145736 | tf_op jit(solution)/shard_map/ppermute | solution.py:620
  91.4 57.0 %collective-permute-start.14 = (bf16[4,128,1024]{2,1,0:T(8,128)(2,1)S(1)}, bf16[4,128,1024]{2,1,0:T(8,128)(2,1)}, u32[]{:S(2)}, u32[]{:S(2)}) collective-permute-start(bf16[4,128,1024]{2,1,0:T(8,128)(2,1)S(1)} %pad_maximum_fusion.4.refs_7_.refs_5_), channel_id=1, source_target_pairs={{0,8},{8,0},{16,24},{24,16},{1,9},{9,1},{17,25},{25,17},{2,10},{10... | collective-permute-start | bytes 3145736 | tf_op jit(solution)/shard_map/ppermute | solution.py:620
  153.3 25.8 %collective-permute-start.17 = (bf16[4,128,1024]{2,1,0:T(8,128)(2,1)}, bf16[4,128,1024]{2,1,0:T(8,128)(2,1)S(1)}, u32[]{:S(2)}, u32[]{:S(2)}) collective-permute-start(bf16[4,128,1024]{2,1,0:T(8,128)(2,1)} %get-tuple-element.84.refs_2_), channel_id=1, source_target_pairs={{0,16},{8,24},{16,0},{24,8},{1,17},{9,25},{17,1},{25,9},{2,18},{10... | collective-permute-start | bytes 3145736 | tf_op jit(solution)/shard_map/ppermute | solution.py:620
  154.2 25.5 %collective-permute-start.18 = (bf16[4,128,1024]{2,1,0:T(8,128)(2,1)}, bf16[4,128,1024]{2,1,0:T(8,128)(2,1)S(1)}, u32[]{:S(2)}, u32[]{:S(2)}) collective-permute-start(bf16[4,128,1024]{2,1,0:T(8,128)(2,1)} %get-tuple-element.87.refs_7_), channel_id=1, source_target_pairs={{0,8},{8,0},{16,24},{24,16},{1,9},{9,1},{17,25},{25,17},{2,10},{10... | collective-permute-start | bytes 3145736 | tf_op jit(solution)/shard_map/ppermute | solution.py:620
  235.9 83.2 %all-to-all-start = ((bf16[4,512,1024]{2,1,0:T(8,128)(2,1)}), bf16[4,512,1024]{2,1,0:T(8,128)(2,1)}, u32[]{:S(2)}, u32[]{:S(2)}) async-start(bf16[4,512,1024]{2,1,0:T(8,128)(2,1)} %bitcast.103), calls=%async_computation | async-start | bytes 8388608 | tf_op jit(solution)/shard_map/all_to_all | solution.py:654
  265.2 67.3 %collective-permute-start.23 = (bf16[512,1024]{1,0:T(8,128)(2,1)}, bf16[512,1024]{1,0:T(8,128)(2,1)}, u32[]{:S(2)}, u32[]{:S(2)}) collective-permute-start(bf16[512,1024]{1,0:T(8,128)(2,1)} %get-tuple-element.103.refs_2_.refs_8_), channel_id=1, source_target_pairs={{0,8},{8,0},{16,24},{24,16},{1,9},{9,1},{17,25},{25,17},{2,10},{10... | collective-permute-start | bytes 3145736 | tf_op jit(solution)/shard_map/ppermute | solution.py:620
  266.9 65.6 %collective-permute-start.24 = (bf16[512,1024]{1,0:T(8,128)(2,1)}, bf16[512,1024]{1,0:T(8,128)(2,1)}, u32[]{:S(2)}, u32[]{:S(2)}) collective-permute-start(bf16[512,1024]{1,0:T(8,128)(2,1)} %get-tuple-element.104.refs_3_.refs_9_), channel_id=1, source_target_pairs={{0,16},{8,24},{16,0},{24,8},{1,17},{9,25},{17,1},{25,9},{2,18},{10... | collective-permute-start | bytes 3145736 | tf_op jit(solution)/shard_map/ppermute | solution.py:620
  268.4 66.6 %collective-permute-start.25 = (bf16[512,1024]{1,0:T(8,128)(2,1)}, bf16[512,1024]{1,0:T(8,128)(2,1)}, u32[]{:S(2)}, u32[]{:S(2)}) collective-permute-start(bf16[512,1024]{1,0:T(8,128)(2,1)} %get-tuple-element.105.refs_4_.refs_10_), channel_id=1, source_target_pairs={{0,24},{8,16},{16,8},{24,0},{1,25},{9,17},{17,9},{25,1},{2,26},{10... | collective-permute-start | bytes 3145736 | tf_op jit(solution)/shard_map/ppermute | solution.py:620
  337.4 58.0 %collective-permute-start.26 = (bf16[2,256,1024]{2,1,0:T(8,128)(2,1)S(1)}, bf16[2,256,1024]{2,1,0:T(8,128)(2,1)}, u32[]{:S(2)}, u32[]{:S(2)}) collective-permute-start(bf16[2,256,1024]{2,1,0:T(8,128)(2,1)S(1)} %fusion.6.refs_11_), channel_id=1, source_target_pairs={{0,4},{1,5},{2,6},{3,7},{4,0},{5,1},{6,2},{7,3},{8,12},{9,13},{10,... | collective-permute-start | bytes 3145736 | tf_op jit(solution)/shard_map/ppermute | solution.py:614
  349.9 37.1 %collective-permute-start.27 = (bf16[2,4,32,1024]{3,2,1,0:T(8,128)(2,1)}, bf16[2,4,32,1024]{3,2,1,0:T(8,128)(2,1)S(1)}, u32[]{:S(2)}, u32[]{:S(2)}) collective-permute-start(bf16[2,4,32,1024]{3,2,1,0:T(8,128)(2,1)} %get-tuple-element.114.refs_8_), channel_id=1, source_target_pairs={{0,8},{8,0},{16,24},{24,16},{1,9},{9,1},{17,25},{25,17},{2,10},{10... | collective-permute-start | bytes 1572872 | tf_op jit(solution)/shard_map/ppermute | solution.py:620
  350.5 36.5 %collective-permute-start.28 = (bf16[2,4,32,1024]{3,2,1,0:T(8,128)(2,1)}, bf16[2,4,32,1024]{3,2,1,0:T(8,128)(2,1)}, u32[]{:S(2)}, u32[]{:S(2)}) collective-permute-start(bf16[2,4,32,1024]{3,2,1,0:T(8,128)(2,1)} %get-tuple-element.115.refs_9_), channel_id=1, source_target_pairs={{0,16},{8,24},{16,0},{24,8},{1,17},{9,25},{17,1},{25,9},{2,18},{10... | collective-permute-start | bytes 1572872 | tf_op jit(solution)/shard_map/ppermute | solution.py:620
  351.0 36.0 %collective-permute-start.29 = (bf16[2,4,32,1024]{3,2,1,0:T(8,128)(2,1)}, bf16[2,4,32,1024]{3,2,1,0:T(8,128)(2,1)}, u32[]{:S(2)}, u32[]{:S(2)}) collective-permute-start(bf16[2,4,32,1024]{3,2,1,0:T(8,128)(2,1)} %get-tuple-element.116.refs_10_), channel_id=1, source_target_pairs={{0,24},{8,16},{16,8},{24,0},{1,25},{9,17},{17,9},{25,1},{2,26},{10... | collective-permute-start | bytes 1572872 | tf_op jit(solution)/shard_map/ppermute | solution.py:620
  410.3 31.1 %collective-permute-start.22 = (bf16[1024,1024]{1,0:T(8,128)(2,1)}, bf16[1024,1024]{1,0:T(8,128)(2,1)}, u32[]{:S(2)}, u32[]{:S(2)}) collective-permute-start(bf16[1024,1024]{1,0:T(8,128)(2,1)} %shard_map.261.refs_11_), channel_id=1, source_target_pairs={{0,1},{1,0},{2,3},{3,2},{4,5},{5,4},{6,7},{7,6},{8,9},{9,8},{10,11... | collective-permute-start | bytes 6291464 | tf_op jit(solution)/shard_map/ppermute | solution.py:614
  417.6 42.7 %collective-permute-start.34 = (bf16[1024,1024]{1,0:T(8,128)(2,1)}, bf16[1024,1024]{1,0:T(8,128)(2,1)}, u32[]{:S(2)}, u32[]{:S(2)}) collective-permute-start(bf16[1024,1024]{1,0:T(8,128)(2,1)} %shard_map.270.refs_2_), channel_id=1, source_target_pairs={{0,1},{1,0},{2,3},{3,2},{4,5},{5,4},{6,7},{7,6},{8,9},{9,8},{10,11... | collective-permute-start | bytes 6291464 | tf_op jit(solution)/shard_map/ppermute | solution.py:614
  441.3 29.3 %collective-permute-start.42 = (bf16[2,4,32,1024]{3,2,1,0:T(8,128)(2,1)}, bf16[2,4,32,1024]{3,2,1,0:T(8,128)(2,1)S(1)}, u32[]{:S(2)}, u32[]{:S(2)}) collective-permute-start(bf16[2,4,32,1024]{3,2,1,0:T(8,128)(2,1)} %pad_maximum_fusion.7.refs_1_.refs_7_), channel_id=1, source_target_pairs={{0,4},{1,5},{2,6},{3,7},{4,0},{5,1},{6,2},{7,3},{8,12},{9,13},{10,... | collective-permute-start | bytes 1572872 | tf_op jit(solution)/shard_map/ppermute | solution.py:614
  (62 other events, 625.5 us)

commit v6 on v5

--- a/solution.py
+++ b/solution.py
@@ -15,6 +15,7 @@
 MASKED_SCORE = -1e30
 ROOT = (2.0 / 3.141592653589793) ** 0.5
 VMEM = 60 * 1024 * 1024
+ATTEND_VMEM = 44 * 1024 * 1024
 LIGHT = pl.CostEstimate(flops=1, bytes_accessed=1, transcendentals=0)
 NT = (((1,), (1,)), ((), ()))
 TN = (((0,), (0,)), ((), ()))
@@ -282,7 +283,7 @@
             jax.ShapeDtypeStruct((length, heads * HD), jnp.bfloat16),
             jax.ShapeDtypeStruct((blocks, heads, block), jnp.float32),
         ],
-        compiler_params=pltpu.CompilerParams(vmem_limit_bytes=VMEM),
+        compiler_params=pltpu.CompilerParams(vmem_limit_bytes=ATTEND_VMEM),
         cost_estimate=LIGHT,
     )(scalars, joined, first, lines, *waits)
 

time: 512 us -> 511 us (level)
    unnamed x79 -> x87, local copies, waits for them, and re-layouts: 9.21 us -> 11.3 us
where the time goes in v6:
time: 511 us; the launch traced here: 504 us
  Pallas kernels  266 us (52%)
  waiting for transfers between devices  93.3 us (18%)
  starting transfers between devices  67.6 us (13%)
  other arithmetic  45.8 us (9%)
  local copies, waits for them, and re-layouts  28.3 us (6%)
    pallas_call x2, Pallas kernels, attend_back(): pl.pallas_call(ignoring(functools.partial(attend_back_kernel, block=block...  67.2 us
    ppermute x22, waiting for transfers between devices, from_group(): lax.ppermute(value, 'narrow', [(i, i ^ s) for i in range(self.narrow)])  64.6 us
    pallas_call x6, Pallas kernels, product(): pl.pallas_call(ignoring(functools.partial(product_kernel, parts=len(parts...  44 us
    pallas_call x1, Pallas kernels, hidden_units(): pl.pallas_call(functools.partial(hidden_kernel, slots=slots, blocks=block...  36 us
    ppermute x22, starting transfers between devices, from_group(): lax.ppermute(value, 'narrow', [(i, i ^ s) for i in range(self.narrow)])  30.6 us
    pallas_call x1, Pallas kernels, attend(): pl.pallas_call(ignoring(functools.partial(attend_kernel, block=block, per...  29.2 us
    ppermute x25, waiting for transfers between devices, from_wide(): return lax.ppermute(value, 'wide', [(i, i ^ s) for i in range(self.wide)])  28.7 us
    pallas_call x2, Pallas kernels, unit_grads(): pl.pallas_call(ignoring(functools.partial(unit_grads_kernel, slots=len(sl...  28.1 us
  transfers between devices with their start and end apart: 49, of which 15 were waited for; matrix products, arithmetic and copies ran while one was open for 11% of the time, Pallas kernels for 45%

profile of v6, /device:TPU:0, one launch (start us, length us, event | category | flops | bytes accessed | tf_op | source)
XLA Modules:
  0.0 503.8 jit_solution(12419254311347145999)
XLA Ops:
  18.0 16.0 %collective-permute-done.4.refs_2_ = bf16[144,1024]{1,0:T(8,128)(2,1)} collective-permute-done((bf16[144,1024]{1,0:T(8,128)(2,1)}, bf16[144,1024]{1,0:T(8,128)(2,1)}, u32[]{:S(2)}, u32[]{:S(2)}) %collective-permute-start.4) | collective-permute-done | bytes 294944 | tf_op jit(solution)/shard_map/ppermute | solution.py:615
  57.6 27.7 %collective-permute-done.10 = bf16[256,1024]{1,0:T(8,128)(2,1)} collective-permute-done((bf16[256,1024]{1,0:T(8,128)(2,1)}, bf16[256,1024]{1,0:T(8,128)(2,1)}, u32[]{:S(2)}, u32[]{:S(2)}) %collective-permute-start.10) | collective-permute-done | bytes 524320 | tf_op jit(solution)/shard_map/ppermute | solution.py:615
  102.2 11.4 %shard_map.248.refs_1_ = bf16[2048,1536]{1,0:T(8,128)(2,1)} custom-call(bf16[1024,1024]{1,0:T(8,128)(2,1)} %fusion.5.refs_0_, bf16[1024,1024]{1,0:T(8,128)(2,1)} %collective-permute-done.refs_1_, bf16[1536,1024]{1,0:T(8,128)(2,1)} %shard_map.247.refs_2_.refs_0_, f32[1,1536]{1,0:T(1,128)} %compare_select_fusion.refs_3_), custom_call_target="tpu_custom_call" | custom-call | flops 1 | bytes 1 | tf_op jit(solution)/shard_map/pallas_call | solution.py:453
  116.8 29.2 %shard_map.249 = (bf16[2048,512]{1,0:T(8,128)(2,1)S(1)}, f32[8,8,256]{2,1,0:T(8,128)S(1)}) custom-call(s32[9]{0:T(128)S(1)} %pad_add_fusion.refs_0_, bf16[2048,1536]{1,0:T(8,128)(2,1)} %shard_map.248.refs_1_, s32[8,256]{1,0:T(8,128)S(1)} %reshape.221.refs_2_.refs_4_, f32[8,1536]{1,0:T(8,128)S(1)} %concatenate.36.refs_3_.refs_5_, ...), custom_call_target="tpu_custom_call" | custom-call | flops 1 | bytes 1 | tf_op jit(solution)/shard_map/pallas_call | solution.py:279
  157.3 6.2 %shard_map.253.refs_0_.refs_5_ = f32[1024,1024]{1,0:T(8,128)} custom-call(bf16[2048,512]{1,0:T(8,128)(2,1)} %get-tuple-element.83.refs_0_.refs_2_.mixed_ref, bf16[512,1024]{1,0:T(8,128)(2,1)} %shard_map.251.refs_1_.refs_2_, bf16[1024,1024]{1,0:T(8,128)(2,1)} %refs_0_.1, bf16[1024,1024]{1,0:T(8,128)(2,1)} %collective-permute-done.16.refs_3_), custom_call_target="tpu_custom_call" | custom-call | flops 1 | bytes 1 | tf_op jit(solution)/shard_map/pallas_call | solution.py:494
  171.4 7.2 %collective-permute-done.17.refs_4_ = bf16[4,128,1024]{2,1,0:T(8,128)(2,1)S(1)} collective-permute-done((bf16[4,128,1024]{2,1,0:T(8,128)(2,1)}, bf16[4,128,1024]{2,1,0:T(8,128)(2,1)S(1)}, u32[]{:S(2)}, u32[]{:S(2)}) %collective-permute-start.17) | collective-permute-done | bytes 1048608 | tf_op jit(solution)/shard_map/ppermute | solution.py:621
  185.6 36.0 %shard_map.255 = (bf16[2048,2048]{1,0:T(8,128)(2,1)}, bf16[2048,2048]{1,0:T(8,128)(2,1)}, bf16[1024,1024]{1,0:T(8,128)(2,1)}, bf16[1024,1024]{1,0:T(8,128)(2,1)}) custom-call(bf16[1024,1024]{1,0:T(8,128)(2,1)} %get-tuple-element.88.refs_0_.refs_2_, bf16[1024,1024]{1,0:T(8,128)(2,1)} %copy-done.16, bf16[1024,1024]{1,0:T(8,128)(2,1)} %refs_1_.1, ...), custom_call_target="tpu_custom_call" | custom-call | flops 1 | bytes 1 | tf_op jit(solution)/shard_map/pallas_call | solution.py:378
  221.8 13.4 %shard_map.256 = bf16[2048,1024]{1,0:T(8,128)(2,1)} custom-call(s32[1]{0:T(128)} %bitcast.3.refs_0_.me_ref, bf16[2048,2048]{1,0:T(8,128)(2,1)} %get-tuple-element.97.refs_1_.refs_0_, bf16[1024,1024]{1,0:T(8,128)(2,1)} %refs_1_.1, bf16[1024,1024]{1,0:T(8,128)(2,1)} %collective-permute-done.8.refs_5_.refs_3_), custom_call_target="tpu_custom_call" | custom-call | flops 1 | bytes 1 | tf_op jit(solution)/shard_map/pallas_call | solution.py:553
  235.1 5.0 %all-to-all-start = ((bf16[4,512,1024]{2,1,0:T(8,128)(2,1)}), bf16[4,512,1024]{2,1,0:T(8,128)(2,1)}, u32[]{:S(2)}, u32[]{:S(2)}) async-start(bf16[4,512,1024]{2,1,0:T(8,128)(2,1)} %bitcast.103), calls=%async_computation | async-start | bytes 8388608 | tf_op jit(solution)/shard_map/all_to_all | solution.py:655
  241.5 7.8 %shard_map.257 = (f32[1024,1024]{1,0:T(8,128)}, bf16[1024,1024]{1,0:T(8,128)(2,1)}, f32[8,1024]{1,0:T(8,128)}) custom-call(f32[1024,1024]{1,0:T(8,128)} %shard_map.253.refs_0_.refs_5_, bf16[1024,1024]{1,0:T(8,128)(2,1)} %refs_1_.1, f32[1,1024]{1,0:T(1,128)} %bitcast.127, bf16[1024,1024]{1,0:T(8,128)(2,1)} %get-tuple-element.98.refs_3_, ...), custom_call_target="tpu_custom_call" | custom-call | flops 1 | bytes 1 | tf_op jit(solution)/shard_map/pallas_call | solution.py:417
  249.7 14.8 %shard_map.258 = (bf16[512,1024]{1,0:T(8,128)(2,1)}, bf16[512,1024]{1,0:T(8,128)(2,1)}, bf16[512,1024]{1,0:T(8,128)(2,1)}, bf16[512,1024]{1,0:T(8,128)(2,1)}) custom-call(s32[1]{0:T(128)} %constant.105.clone.1.refs_0_, bf16[2048,2048]{1,0:T(8,128)(2,1)} %get-tuple-element.101.refs_1_, bf16[1024,1024]{1,0:T(8,128)(2,1)} %get-tuple-element.88.refs_0_.refs_2_, ...), custom_call_target="tpu_custom_call" | custom-call | flops 1 | bytes 1 | tf_op jit(solution)/shard_map/pallas_call | solution.py:553
  269.9 6.4 %shard_map.260.refs_5_.refs_3_ = bf16[2048,512]{1,0:T(8,128)(2,1)} custom-call(bf16[1024,1024]{1,0:T(8,128)(2,1)} %get-tuple-element.100.refs_4_.refs_0_.refs_2_, bf16[1024,1024]{1,0:T(8,128)(2,1)} %shard_map.259.refs_1_.refs_3_, bf16[512,1024]{1,0:T(8,128)(2,1)} %shard_map.251.refs_1_.refs_2_, f32[1,512]{1,0:T(1,128)} %broadcast_in_dim.52.refs_3_), custom_call_target="tpu_custom_call" | custom-call | flops 1 | bytes 1 | tf_op jit(solution)/shard_map/pallas_call | solution.py:453
  276.3 8.5 %shard_map.261.refs_11_ = bf16[1024,1024]{1,0:T(8,128)(2,1)} custom-call(bf16[2048,2048]{1,0:T(8,128)(2,1)} %get-tuple-element.97.refs_1_.refs_0_, bf16[4,128,1024]{2,1,0:T(8,128)(2,1)} %get-tuple-element.93.refs_8_.refs_1_, bf16[4,128,1024]{2,1,0:T(8,128)(2,1)} %get-tuple-element.94.refs_9_.refs_2_, ...), custom_call_target="tpu_custom_call" | custom-call | flops 1 | bytes 1 | tf_op jit(solution)/shard_map/pallas_call | solution.py:494
  284.8 33.6 %shard_map.262 = (bf16[2048,768]{1,0:T(8,128)(2,1)}, f32[4,1536]{1,0:T(4,128)}) custom-call(s32[9]{0:T(128)} %copy-done.6, bf16[2048,1536]{1,0:T(8,128)(2,1)} %shard_map.248.refs_1_, bf16[2048,512]{1,0:T(8,128)(2,1)} %get-tuple-element.83.refs_0_.refs_2_.mixed_ref, bf16[2048,512]{1,0:T(8,128)(2,1)} %shard_map.260.refs_5_.refs_3_, s32[8,256]{1,0:T(8,128)} %copy-done.5, ...), custom_call_target="tpu_custom_call" | custom-call | flops 1 | bytes 1 | tf_op jit(solution)/shard_map/pallas_call | solution.py:317
  318.4 10.1 %shard_map.264 = (bf16[2,4,32,1024]{3,2,1,0:T(8,128)(2,1)}, bf16[2,4,32,1024]{3,2,1,0:T(8,128)(2,1)}, bf16[2,4,32,1024]{3,2,1,0:T(8,128)(2,1)}, bf16[2,4,32,1024]{3,2,1,0:T(8,128)(2,1)}) custom-call(s32[1]{0:T(128)} %bitcast.3.refs_0_.me_ref, bf16[2048,768]{1,0:T(8,128)(2,1)} %get-tuple-element.108.grads_ref.refs_0_, ...), custom_call_target="tpu_custom_call" | custom-call | flops 1 | bytes 1 | tf_op jit(solution)/shard_map/pallas_call | solution.py:600
  336.7 12.2 %collective-permute-start.26 = (bf16[2,256,1024]{2,1,0:T(8,128)(2,1)S(1)}, bf16[2,256,1024]{2,1,0:T(8,128)(2,1)}, u32[]{:S(2)}, u32[]{:S(2)}) collective-permute-start(bf16[2,256,1024]{2,1,0:T(8,128)(2,1)S(1)} %fusion.6.refs_11_), channel_id=1, source_target_pairs={{0,4},{1,5},{2,6},{3,7},{4,0},{5,1},{6,2},{7,3},{8,12},{9,13},{10,... | collective-permute-start | bytes 3145736 | tf_op jit(solution)/shard_map/ppermute | solution.py:615
  352.3 33.6 %shard_map.266 = (bf16[2048,768]{1,0:T(8,128)(2,1)}, f32[4,1536]{1,0:T(4,128)}) custom-call(s32[9]{0:T(128)} %copy-done.6, bf16[2048,1536]{1,0:T(8,128)(2,1)} %shard_map.248.refs_1_, bf16[2048,512]{1,0:T(8,128)(2,1)} %get-tuple-element.83.refs_0_.refs_2_.mixed_ref, bf16[2048,512]{1,0:T(8,128)(2,1)} %shard_map.260.refs_5_.refs_3_, s32[8,256]{1,0:T(8,128)} %copy-done.5, ...), custom_call_target="tpu_custom_call" | custom-call | flops 1 | bytes 1 | tf_op jit(solution)/shard_map/pallas_call | solution.py:317
  386.0 8.3 %collective-permute-done.26.refs_1_ = bf16[2,256,1024]{2,1,0:T(8,128)(2,1)} collective-permute-done((bf16[2,256,1024]{2,1,0:T(8,128)(2,1)S(1)}, bf16[2,256,1024]{2,1,0:T(8,128)(2,1)}, u32[]{:S(2)}, u32[]{:S(2)}) %collective-permute-start.26) | collective-permute-done | bytes 1048608 | tf_op jit(solution)/shard_map/ppermute | solution.py:615
  395.6 10.0 %shard_map.268 = (bf16[2,4,32,1024]{3,2,1,0:T(8,128)(2,1)}, bf16[2,4,32,1024]{3,2,1,0:T(8,128)(2,1)}, bf16[2,4,32,1024]{3,2,1,0:T(8,128)(2,1)}, bf16[2,4,32,1024]{3,2,1,0:T(8,128)(2,1)}) custom-call(s32[1]{0:T(128)} %bitcast.3.refs_0_.me_ref, bf16[2048,768]{1,0:T(8,128)(2,1)} %get-tuple-element.127.grads_ref.refs_1_, ...), custom_call_target="tpu_custom_call" | custom-call | flops 1 | bytes 1 | tf_op jit(solution)/shard_map/pallas_call | solution.py:600
  409.2 7.3 %shard_map.270.refs_2_ = bf16[1024,1024]{1,0:T(8,128)(2,1)} custom-call(bf16[2048,768]{1,0:T(8,128)(2,1)} %get-tuple-element.108.grads_ref.refs_0_, bf16[2048,768]{1,0:T(8,128)(2,1)} %get-tuple-element.127.grads_ref.refs_1_, bf16[1536,1024]{1,0:T(8,128)(2,1)} %shard_map.269.refs_2_.refs_0_), custom_call_target="tpu_custom_call" | custom-call | flops 1 | bytes 1 | tf_op jit(solution)/shard_map/pallas_call | solution.py:494
  418.5 7.3 %shard_map.272.refs_4_.refs_3_ = bf16[1024,1024]{1,0:T(8,128)(2,1)} custom-call(bf16[2048,768]{1,0:T(8,128)(2,1)} %get-tuple-element.108.grads_ref.refs_0_, bf16[2048,768]{1,0:T(8,128)(2,1)} %get-tuple-element.127.grads_ref.refs_1_, bf16[1536,1024]{1,0:T(8,128)(2,1)} %get-tuple-element.133.refs_2_), custom_call_target="tpu_custom_call" | custom-call | flops 1 | bytes 1 | tf_op jit(solution)/shard_map/pallas_call | solution.py:494
  443.5 9.9 %shard_map.275.refs_5_ = bf16[1024,1024]{1,0:T(8,128)(2,1)} custom-call(bf16[2048,2048]{1,0:T(8,128)(2,1)} %get-tuple-element.97.refs_1_.refs_0_, bf16[4,128,1024]{2,1,0:T(8,128)(2,1)} %get-tuple-element.93.refs_8_.refs_1_, bf16[4,128,1024]{2,1,0:T(8,128)(2,1)} %get-tuple-element.94.refs_9_.refs_2_, ...), custom_call_target="tpu_custom_call" | custom-call | flops 1 | bytes 1 | tf_op jit(solution)/shard_map/pallas_call | solution.py:494
  453.4 6.1 %collective-permute-done.36.refs_7_.refs_1_ = bf16[256,1024]{1,0:T(8,128)(2,1)S(1)} collective-permute-done((bf16[256,1024]{1,0:T(8,128)(2,1)}, bf16[256,1024]{1,0:T(8,128)(2,1)S(1)}, u32[]{:S(2)}, u32[]{:S(2)}) %collective-permute-start.36) | collective-permute-done | bytes 524320 | tf_op jit(solution)/shard_map/ppermute | solution.py:621
  460.5 8.4 %shard_map.276 = (f32[1024,1024]{1,0:T(8,128)}, bf16[1024,1024]{1,0:T(8,128)(2,1)}, f32[8,1024]{1,0:T(8,128)}) custom-call(bf16[1024,1024]{1,0:T(8,128)(2,1)} %refs_0_.1, f32[1024,1024]{1,0:T(8,128)} %get-tuple-element.139.refs_1_, f32[1,1024]{1,0:T(1,128)} %bitcast.128, bf16[1024,1024]{1,0:T(8,128)(2,1)} %shard_map.272.refs_4_.refs_3_, ...), custom_call_target="tpu_custom_call" | custom-call | flops 1 | bytes 1 | tf_op jit(solution)/shard_map/pallas_call | solution.py:417
  (292 shorter events, 165.5 us)
Async XLA Ops:
  8.6 25.4 %collective-permute-start.4 = (bf16[144,1024]{1,0:T(8,128)(2,1)}, bf16[144,1024]{1,0:T(8,128)(2,1)}, u32[]{:S(2)}, u32[]{:S(2)}) collective-permute-start(bf16[144,1024]{1,0:T(8,128)(2,1)} %pad_maximum_fusion.8), channel_id=1, source_target_pairs={{0,4},{1,5},{2,6},{3,7},{4,0},{5,1},{6,2},{7,3},{8,12},{9,13},{10,... | collective-permute-start | bytes 884744 | tf_op jit(solution)/shard_map/ppermute | solution.py:615
  8.6 28.0 %collective-permute-start.1 = (bf16[144,1024]{1,0:T(8,128)(2,1)}, bf16[144,1024]{1,0:T(8,128)(2,1)}, u32[]{:S(2)}, u32[]{:S(2)}) collective-permute-start(bf16[144,1024]{1,0:T(8,128)(2,1)} %pad_maximum_fusion.8), channel_id=1, source_target_pairs={{0,2},{1,3},{2,0},{3,1},{4,6},{5,7},{6,4},{7,5},{8,10},{9,11},{10,... | collective-permute-start | bytes 884744 | tf_op jit(solution)/shard_map/ppermute | solution.py:615
  9.2 83.2 %collective-permute-start.8 = (bf16[1024,1024]{1,0:T(8,128)(2,1)}, bf16[1024,1024]{1,0:T(8,128)(2,1)}, u32[]{:S(2)}, u32[]{:S(2)}) collective-permute-start(bf16[1024,1024]{1,0:T(8,128)(2,1)} %refs_1_.1), channel_id=1, source_target_pairs={{0,1},{1,0},{2,3},{3,2},{4,5},{5,4},{6,7},{7,6},{8,9},{9,8},{10,11... | collective-permute-start | bytes 6291464 | tf_op jit(solution)/shard_map/ppermute | solution.py:615
  42.4 42.8 %collective-permute-start.10 = (bf16[256,1024]{1,0:T(8,128)(2,1)}, bf16[256,1024]{1,0:T(8,128)(2,1)}, u32[]{:S(2)}, u32[]{:S(2)}) collective-permute-start(bf16[256,1024]{1,0:T(8,128)(2,1)} %shard_map.246), channel_id=1, source_target_pairs={{0,4},{1,5},{2,6},{3,7},{4,0},{5,1},{6,2},{7,3},{8,12},{9,13},{10,... | collective-permute-start | bytes 1572872 | tf_op jit(solution)/shard_map/ppermute | solution.py:615
  48.1 39.4 %collective-permute-start.9 = (bf16[256,1024]{1,0:T(8,128)(2,1)}, bf16[256,1024]{1,0:T(8,128)(2,1)S(1)}, u32[]{:S(2)}, u32[]{:S(2)}) collective-permute-start(bf16[256,1024]{1,0:T(8,128)(2,1)} %shard_map.246), channel_id=1, source_target_pairs={{0,2},{1,3},{2,0},{3,1},{4,6},{5,7},{6,4},{7,5},{8,10},{9,11},{10,... | collective-permute-start | bytes 1572872 | tf_op jit(solution)/shard_map/ppermute | solution.py:615
  51.5 38.8 %collective-permute-start.7 = (bf16[2,2,128,1024]{3,2,1,0:T(8,128)(2,1)S(1)}, bf16[2,2,128,1024]{3,2,1,0:T(8,128)(2,1)S(1)}, u32[]{:S(2)}, u32[]{:S(2)}) collective-permute-start(bf16[2,2,128,1024]{3,2,1,0:T(8,128)(2,1)S(1)} %pad_maximum_fusion.2.refs_3_), channel_id=1, source_target_pairs={{0,8},{8,0},{16,24},{24,16},{1,9},{9,1},{17,25},{25,17},{2,10},{10... | collective-permute-start | bytes 3145736 | tf_op jit(solution)/shard_map/ppermute | solution.py:621
  57.0 33.8 %collective-permute-start.3 = (bf16[2,2,128,1024]{3,2,1,0:T(8,128)(2,1)S(1)}, bf16[2,2,128,1024]{3,2,1,0:T(8,128)(2,1)S(1)}, u32[]{:S(2)}, u32[]{:S(2)}) collective-permute-start(bf16[2,2,128,1024]{3,2,1,0:T(8,128)(2,1)S(1)} %pad_maximum_fusion.1.refs_1_), channel_id=1, source_target_pairs={{0,16},{8,24},{16,0},{24,8},{1,17},{9,25},{17,1},{25,9},{2,18},{10... | collective-permute-start | bytes 3145736 | tf_op jit(solution)/shard_map/ppermute | solution.py:621
  88.6 59.4 %collective-permute-start.13 = (bf16[4,128,1024]{2,1,0:T(8,128)(2,1)}, bf16[4,128,1024]{2,1,0:T(8,128)(2,1)}, u32[]{:S(2)}, u32[]{:S(2)}) collective-permute-start(bf16[4,128,1024]{2,1,0:T(8,128)(2,1)} %pad_maximum_fusion.3.refs_6_.refs_4_.refs_1_), channel_id=1, source_target_pairs={{0,16},{8,24},{16,0},{24,8},{1,17},{9,25},{17,1},{25,9},{2,18},{10... | collective-permute-start | bytes 3145736 | tf_op jit(solution)/shard_map/ppermute | solution.py:621
  90.3 57.8 %collective-permute-start.12 = (bf16[4,128,1024]{2,1,0:T(8,128)(2,1)}, bf16[4,128,1024]{2,1,0:T(8,128)(2,1)}, u32[]{:S(2)}, u32[]{:S(2)}) collective-permute-start(bf16[4,128,1024]{2,1,0:T(8,128)(2,1)} %pad_maximum_fusion.3.refs_6_.refs_4_.refs_1_), channel_id=1, source_target_pairs={{0,8},{8,0},{16,24},{24,16},{1,9},{9,1},{17,25},{25,17},{2,10},{10... | collective-permute-start | bytes 3145736 | tf_op jit(solution)/shard_map/ppermute | solution.py:621
  90.8 57.2 %collective-permute-start.15 = (bf16[4,128,1024]{2,1,0:T(8,128)(2,1)}, bf16[4,128,1024]{2,1,0:T(8,128)(2,1)}, u32[]{:S(2)}, u32[]{:S(2)}) collective-permute-start(bf16[4,128,1024]{2,1,0:T(8,128)(2,1)} %pad_maximum_fusion.4.refs_7_.refs_5_), channel_id=1, source_target_pairs={{0,16},{8,24},{16,0},{24,8},{1,17},{9,25},{17,1},{25,9},{2,18},{10... | collective-permute-start | bytes 3145736 | tf_op jit(solution)/shard_map/ppermute | solution.py:621
  92.3 55.7 %collective-permute-start.14 = (bf16[4,128,1024]{2,1,0:T(8,128)(2,1)}, bf16[4,128,1024]{2,1,0:T(8,128)(2,1)}, u32[]{:S(2)}, u32[]{:S(2)}) collective-permute-start(bf16[4,128,1024]{2,1,0:T(8,128)(2,1)} %pad_maximum_fusion.4.refs_7_.refs_5_), channel_id=1, source_target_pairs={{0,8},{8,0},{16,24},{24,16},{1,9},{9,1},{17,25},{25,17},{2,10},{10... | collective-permute-start | bytes 3145736 | tf_op jit(solution)/shard_map/ppermute | solution.py:621
  152.8 25.8 %collective-permute-start.17 = (bf16[4,128,1024]{2,1,0:T(8,128)(2,1)}, bf16[4,128,1024]{2,1,0:T(8,128)(2,1)S(1)}, u32[]{:S(2)}, u32[]{:S(2)}) collective-permute-start(bf16[4,128,1024]{2,1,0:T(8,128)(2,1)} %get-tuple-element.84.refs_2_), channel_id=1, source_target_pairs={{0,16},{8,24},{16,0},{24,8},{1,17},{9,25},{17,1},{25,9},{2,18},{10... | collective-permute-start | bytes 3145736 | tf_op jit(solution)/shard_map/ppermute | solution.py:621
  153.3 25.5 %collective-permute-start.18 = (bf16[4,128,1024]{2,1,0:T(8,128)(2,1)}, bf16[4,128,1024]{2,1,0:T(8,128)(2,1)S(1)}, u32[]{:S(2)}, u32[]{:S(2)}) collective-permute-start(bf16[4,128,1024]{2,1,0:T(8,128)(2,1)} %get-tuple-element.87.refs_7_), channel_id=1, source_target_pairs={{0,8},{8,0},{16,24},{24,16},{1,9},{9,1},{17,25},{25,17},{2,10},{10... | collective-permute-start | bytes 3145736 | tf_op jit(solution)/shard_map/ppermute | solution.py:621
  235.1 83.3 %all-to-all-start = ((bf16[4,512,1024]{2,1,0:T(8,128)(2,1)}), bf16[4,512,1024]{2,1,0:T(8,128)(2,1)}, u32[]{:S(2)}, u32[]{:S(2)}) async-start(bf16[4,512,1024]{2,1,0:T(8,128)(2,1)} %bitcast.103), calls=%async_computation | async-start | bytes 8388608 | tf_op jit(solution)/shard_map/all_to_all | solution.py:655
  264.5 67.4 %collective-permute-start.23 = (bf16[512,1024]{1,0:T(8,128)(2,1)}, bf16[512,1024]{1,0:T(8,128)(2,1)}, u32[]{:S(2)}, u32[]{:S(2)}) collective-permute-start(bf16[512,1024]{1,0:T(8,128)(2,1)} %get-tuple-element.103.refs_2_.refs_8_), channel_id=1, source_target_pairs={{0,8},{8,0},{16,24},{24,16},{1,9},{9,1},{17,25},{25,17},{2,10},{10... | collective-permute-start | bytes 3145736 | tf_op jit(solution)/shard_map/ppermute | solution.py:621
  266.2 65.7 %collective-permute-start.24 = (bf16[512,1024]{1,0:T(8,128)(2,1)}, bf16[512,1024]{1,0:T(8,128)(2,1)}, u32[]{:S(2)}, u32[]{:S(2)}) collective-permute-start(bf16[512,1024]{1,0:T(8,128)(2,1)} %get-tuple-element.104.refs_3_.refs_9_), channel_id=1, source_target_pairs={{0,16},{8,24},{16,0},{24,8},{1,17},{9,25},{17,1},{25,9},{2,18},{10... | collective-permute-start | bytes 3145736 | tf_op jit(solution)/shard_map/ppermute | solution.py:621
  267.7 66.5 %collective-permute-start.25 = (bf16[512,1024]{1,0:T(8,128)(2,1)}, bf16[512,1024]{1,0:T(8,128)(2,1)}, u32[]{:S(2)}, u32[]{:S(2)}) collective-permute-start(bf16[512,1024]{1,0:T(8,128)(2,1)} %get-tuple-element.105.refs_4_.refs_10_), channel_id=1, source_target_pairs={{0,24},{8,16},{16,8},{24,0},{1,25},{9,17},{17,9},{25,1},{2,26},{10... | collective-permute-start | bytes 3145736 | tf_op jit(solution)/shard_map/ppermute | solution.py:621
  336.7 57.6 %collective-permute-start.26 = (bf16[2,256,1024]{2,1,0:T(8,128)(2,1)S(1)}, bf16[2,256,1024]{2,1,0:T(8,128)(2,1)}, u32[]{:S(2)}, u32[]{:S(2)}) collective-permute-start(bf16[2,256,1024]{2,1,0:T(8,128)(2,1)S(1)} %fusion.6.refs_11_), channel_id=1, source_target_pairs={{0,4},{1,5},{2,6},{3,7},{4,0},{5,1},{6,2},{7,3},{8,12},{9,13},{10,... | collective-permute-start | bytes 3145736 | tf_op jit(solution)/shard_map/ppermute | solution.py:615
  348.9 37.1 %collective-permute-start.27 = (bf16[2,4,32,1024]{3,2,1,0:T(8,128)(2,1)}, bf16[2,4,32,1024]{3,2,1,0:T(8,128)(2,1)S(1)}, u32[]{:S(2)}, u32[]{:S(2)}) collective-permute-start(bf16[2,4,32,1024]{3,2,1,0:T(8,128)(2,1)} %get-tuple-element.114.refs_8_), channel_id=1, source_target_pairs={{0,8},{8,0},{16,24},{24,16},{1,9},{9,1},{17,25},{25,17},{2,10},{10... | collective-permute-start | bytes 1572872 | tf_op jit(solution)/shard_map/ppermute | solution.py:621
  349.4 36.5 %collective-permute-start.28 = (bf16[2,4,32,1024]{3,2,1,0:T(8,128)(2,1)}, bf16[2,4,32,1024]{3,2,1,0:T(8,128)(2,1)}, u32[]{:S(2)}, u32[]{:S(2)}) collective-permute-start(bf16[2,4,32,1024]{3,2,1,0:T(8,128)(2,1)} %get-tuple-element.115.refs_9_), channel_id=1, source_target_pairs={{0,16},{8,24},{16,0},{24,8},{1,17},{9,25},{17,1},{25,9},{2,18},{10... | collective-permute-start | bytes 1572872 | tf_op jit(solution)/shard_map/ppermute | solution.py:621
  350.8 35.2 %collective-permute-start.29 = (bf16[2,4,32,1024]{3,2,1,0:T(8,128)(2,1)}, bf16[2,4,32,1024]{3,2,1,0:T(8,128)(2,1)}, u32[]{:S(2)}, u32[]{:S(2)}) collective-permute-start(bf16[2,4,32,1024]{3,2,1,0:T(8,128)(2,1)} %get-tuple-element.116.refs_10_), channel_id=1, source_target_pairs={{0,24},{8,16},{16,8},{24,0},{1,25},{9,17},{17,9},{25,1},{2,26},{10... | collective-permute-start | bytes 1572872 | tf_op jit(solution)/shard_map/ppermute | solution.py:621
  409.2 31.0 %collective-permute-start.22 = (bf16[1024,1024]{1,0:T(8,128)(2,1)}, bf16[1024,1024]{1,0:T(8,128)(2,1)}, u32[]{:S(2)}, u32[]{:S(2)}) collective-permute-start(bf16[1024,1024]{1,0:T(8,128)(2,1)} %shard_map.261.refs_11_), channel_id=1, source_target_pairs={{0,1},{1,0},{2,3},{3,2},{4,5},{5,4},{6,7},{7,6},{8,9},{9,8},{10,11... | collective-permute-start | bytes 6291464 | tf_op jit(solution)/shard_map/ppermute | solution.py:615
  416.6 43.0 %collective-permute-start.34 = (bf16[1024,1024]{1,0:T(8,128)(2,1)}, bf16[1024,1024]{1,0:T(8,128)(2,1)}, u32[]{:S(2)}, u32[]{:S(2)}) collective-permute-start(bf16[1024,1024]{1,0:T(8,128)(2,1)} %shard_map.270.refs_2_), channel_id=1, source_target_pairs={{0,1},{1,0},{2,3},{3,2},{4,5},{5,4},{6,7},{7,6},{8,9},{9,8},{10,11... | collective-permute-start | bytes 6291464 | tf_op jit(solution)/shard_map/ppermute | solution.py:615
  440.3 29.6 %collective-permute-start.42 = (bf16[2,4,32,1024]{3,2,1,0:T(8,128)(2,1)}, bf16[2,4,32,1024]{3,2,1,0:T(8,128)(2,1)S(1)}, u32[]{:S(2)}, u32[]{:S(2)}) collective-permute-start(bf16[2,4,32,1024]{3,2,1,0:T(8,128)(2,1)} %pad_maximum_fusion.7.refs_1_.refs_7_), channel_id=1, source_target_pairs={{0,4},{1,5},{2,6},{3,7},{4,0},{5,1},{6,2},{7,3},{8,12},{9,13},{10,... | collective-permute-start | bytes 1572872 | tf_op jit(solution)/shard_map/ppermute | solution.py:615
  (66 other events, 680.5 us)
